TPU v7x, 512 devices: a whole 4x8x8 slice. The times are simulated.
512 devices in a mesh: dp: 8 (over y), ctx: 16 (over z_hi, x, core), head: 4 (over z_lo).
Axes of the slice: x: 4, y: 8, z: 8 (z_hi: 2, z_lo: 4; z = z_hi * 4 + z_lo), core: 2. Of those that a mesh axis runs over, the one named last changes fastest.
Arguments:
- queries: bfloat16 [65536, 3072], P(('dp', 'ctx'), 'head'), parts along dimension 0, may hold values from -6 to 6
- keys: bfloat16 [65536, 3072], P(('dp', 'ctx'), 'head'), parts along dimension 0, may hold values from -8 to 8
- values: bfloat16 [65536, 3072], P(('dp', 'ctx'), 'head'), parts along dimension 0, may hold values from -8 to 8
- pool_segments: int32 [128, 512], P(('dp', 'ctx')), parts along dimension 0, may hold values from 0 to 7, never falling along the last dimension, each value on 1 to 96 neighbouring positions
- window_map: int32 [128], P(('dp', 'ctx')), parts along dimension 0, may hold values from 0 to 15, each once
- ref_owner: int32 [8], P('dp'), parts along dimension 0, may hold values from 0 to 15
- ref_keys: bfloat16 [128, 512, 3072], P(('dp', 'ctx'), 'head'), parts along dimension 0, may hold values from -6 to 6
- ref_values: bfloat16 [128, 512, 3072], P(('dp', 'ctx'), 'head'), parts along dimension 0, may hold values from -6 to 6
- slopes: float32 [24], P('head'), may hold values from 0.02 to 2
Outputs:
- attended: bfloat16 [65536, 3072], P(('dp', 'ctx'), 'head'), parts along dimension 0
There are 8 independent parts, one for each index of `dp`. A program takes and returns all parts, laid end to end along the dimension named above; an argument that names none is the same for every part. Nothing has to cross between parts.
All inputs are finite; a program needn't handle non-finite values.
Results may differ from a plain program's by a relative error of at most 0.0021.
Values may be sent and summed in bfloat16 or wider, within the bound.
No kernel may reach another device: no remote copies, remote signals or barrier semaphores. Data moves between devices by JAX's collectives and lax.ppermute only.
A program may use at most 64 MiB of HBM per device.

v0:
```python
from functools import reduce
import math

import jax
import jax.numpy as jnp
from jax import lax
from jax.sharding import PartitionSpec as P

HD = 128
RATIO = 64


def spread(block, axis, source):
    block = jnp.where(lax.axis_index(axis) == source, block, jnp.zeros_like(block))
    return lax.psum(block, axis)


def group_terms(query_block, key_block, value_block, bias_term):
    score_scale = 1.0 / math.sqrt(HD)
    scores = (
        jnp.einsum("qhd,khd->hqk", query_block, key_block, preferred_element_type=jnp.float32)
        * score_scale
    )
    if bias_term is not None:
        scores = scores + bias_term[:, None, :]
    row_max = jnp.max(scores, axis=2)
    exp_terms = jnp.exp(scores - row_max[:, :, None])
    row_total = jnp.sum(exp_terms, axis=2)
    weights = exp_terms.astype(jnp.bfloat16)
    numerator = jnp.einsum("hqk,khd->qhd", weights, value_block, preferred_element_type=jnp.float32)
    return (row_max.T, row_total.T, numerator)


def combine_groups(group_list):
    ceiling = reduce(jnp.maximum, [triple[0] for triple in group_list])
    numerator = reduce(
        jnp.add, [jnp.exp(triple[0] - ceiling)[:, :, None] * triple[2] for triple in group_list]
    )
    denominator = reduce(
        jnp.add, [jnp.exp(triple[0] - ceiling) * triple[1] for triple in group_list]
    )
    return numerator / denominator[:, :, None]


def on_device(
    queries, keys, values, pool_segments, window_map, ref_owner, ref_keys, ref_values, slopes
):
    tok_rows = queries.shape[0]
    heads_here = queries.shape[1] // HD
    pool_count = tok_rows // RATIO
    member = (pool_segments[0][None, :] == jnp.arange(pool_count, dtype=jnp.int32)[:, None]).astype(
        jnp.bfloat16
    )
    counts = jnp.sum(member, axis=1, dtype=jnp.float32)
    pooled_keys = (
        jnp.dot(member, keys, preferred_element_type=jnp.float32) / counts[:, None]
    ).astype(jnp.bfloat16)
    pooled_values = (
        jnp.dot(member, values, preferred_element_type=jnp.float32) / counts[:, None]
    ).astype(jnp.bfloat16)
    window_tag = window_map.astype(jnp.bfloat16)
    all_keys, all_values, all_tags = (
        lax.all_gather(pooled_keys, "ctx", axis=0, tiled=True),
        lax.all_gather(pooled_values, "ctx", axis=0, tiled=True),
        lax.all_gather(window_tag, "ctx", axis=0, tiled=True),
    )
    ref_k, ref_v = (
        spread(ref_keys[0], "ctx", ref_owner[0]),
        spread(ref_values[0], "ctx", ref_owner[0]),
    )
    ref_k, ref_v = (
        lax.all_to_all(ref_k, "head", split_axis=1, concat_axis=0, tiled=True),
        lax.all_to_all(ref_v, "head", split_axis=1, concat_axis=0, tiled=True),
    )
    query_block = queries.reshape(tok_rows, heads_here, HD)
    key_block = keys.reshape(tok_rows, heads_here, HD)
    value_block = values.reshape(tok_rows, heads_here, HD)
    key_window = jnp.repeat(all_tags.astype(jnp.float32), pool_count)
    distance = jnp.abs(window_map[0].astype(jnp.float32) - key_window)
    bias_term = -slopes[:, None] * distance[None, :]
    group_list = [
        group_terms(query_block, key_block, value_block, None),
        group_terms(
            query_block,
            all_keys.reshape(-1, heads_here, HD),
            all_values.reshape(-1, heads_here, HD),
            bias_term,
        ),
        group_terms(
            query_block, ref_k.reshape(-1, heads_here, HD), ref_v.reshape(-1, heads_here, HD), None
        ),
    ]
    merged = combine_groups(group_list)
    return merged.reshape(tok_rows, heads_here * HD).astype(jnp.bfloat16)


def solution(mesh):
    return jax.shard_map(
        on_device,
        mesh=mesh,
        in_specs=(
            P(("dp", "ctx"), "head"),
            P(("dp", "ctx"), "head"),
            P(("dp", "ctx"), "head"),
            P(("dp", "ctx"), None),
            P(("dp", "ctx")),
            P("dp"),
            P(("dp", "ctx"), "head", None),
            P(("dp", "ctx"), "head", None),
            P("head"),
        ),
        out_specs=P(("dp", "ctx"), "head"),
        check_vma=False,
    )
```

profile of v0, /device:TPU:1, one launch (start us, length us, event | category | flops | bytes accessed | tf_op | source)
XLA Modules:
  0.0 324.7 jit_solution(16259391540248916373)
XLA Ops:
  7.4 1.2 copy.74
  8.5 1.1 copy.65
  10.4 1.3 dynamic-slice
  11.8 0.7 dynamic-update-slice
  12.5 49.1 %all-reduce = bf16[16]{0:T(256)(128)(2,1)S(1)} all-reduce(bf16[16]{0:T(256)(128)(2,1)S(1)} %dynamic-update-slice), channel_id=1, replica_groups=mesh['dp'=8,'ctx'=16,'head'=4] {'ctx'}, use_global_device_ids=true, to_apply=%add | all-reduce | flops 16 | bytes 64
  61.8 1.3 copy.59
  63.2 141.0 %all-reduce.4.cloned.1.call-done = (bf16[128,4,768]{0,2,1:T(8,128)(2,1)}, bf16[128,4,768]{0,2,1:T(8,128)(2,1)}) async-done(((bf16[128,4,768]{0,2,1:T(8,128)(2,1)}, bf16[128,4,768]{0,2,1:T(8,128)(2,1)}), (bf16[128,4,768]{0,2,1:T(8,128)(2,1)}, bf16[128,4,768]{0,2,1:T(8,128)(2,1)})) %all-reduce.4.cloned.1.call-update) | async-done | bytes 1572880 | tf_op jit(solution)/shard_map/psum | solution.py:15
  204.2 4.2 %all-to-all-start.1 = ((bf16[128,4,768]{0,2,1:T(8,128)(2,1)}), bf16[128,4,768]{0,2,1:T(8,128)(2,1)}, u32[]{:S(2)}, u32[]{:S(2)}) async-start(bf16[128,4,768]{0,2,1:T(8,128)(2,1)} %get-tuple-element.5), calls=%async_computation.1 | async-start | bytes 1572864 | tf_op jit(solution)/shard_map/all_to_all | solution.py:73
  208.4 0.2 fusion.20
  208.6 36.4 %all_gather.9 = bf16[128,768]{1,0:T(8,128)(2,1)S(1)} all-gather(bf16[8,768]{1,0:T(8,128)(2,1)S(1)} %fusion.20), channel_id=1, replica_groups=mesh['dp'=8,'ctx'=16,'head'=4] {'ctx'}, dimensions={0}, use_global_device_ids=true | all-gather | bytes 208896 | tf_op jit(solution)/shard_map/all_gather | solution.py:63
  245.0 0.2 copy.62
  245.1 0.3 copy.58
  245.5 1.0 bitcast_reduce_fusion.1
  246.5 4.9 %multiply_reduce_fusion = (f32[6,512]{1,0:T(8,128)S(1)}, f32[6,512,512]{1,2,0:T(8,128)}) fusion(bf16[512,6,128]{0,2,1:T(8,128)(2,1)S(1)} %bitcast.127, bf16[512,6,128]{0,2,1:T(8,128)(2,1)} %bitcast.132), kind=kOutput, calls=%fused_computation.4 | convolution fusion | flops 405795840 | bytes 7876608 | tf_op jit(solution)/shard_map/qhd,khd->hqk/dot_general | solution.py:21
  251.4 4.5 %all-to-all-start = ((bf16[128,4,768]{0,2,1:T(8,128)(2,1)}), bf16[128,4,768]{0,2,1:T(8,128)(2,1)}, u32[]{:S(2)}, u32[]{:S(2)}) async-start(bf16[128,4,768]{0,2,1:T(8,128)(2,1)} %get-tuple-element.6), calls=%async_computation | async-start | bytes 1572864 | tf_op jit(solution)/shard_map/all_to_all | solution.py:72
  255.9 0.2 fusion.21
  256.1 1.4 copy.70
  257.5 35.2 %all_gather.11 = bf16[128,768]{1,0:T(8,128)(2,1)S(1)} all-gather(bf16[8,768]{1,0:T(8,128)(2,1)S(1)} %fusion.21), channel_id=1, replica_groups=mesh['dp'=8,'ctx'=16,'head'=4] {'ctx'}, dimensions={0}, use_global_device_ids=true | all-gather | bytes 208896 | tf_op jit(solution)/shard_map/all_gather | solution.py:64
  292.8 0.2 copy.72
  292.9 1.0 fusion.18
  293.9 4.0 %fusion.1 = f32[6,512]{1,0:T(8,128)S(1)} fusion(f32[6,512,512]{1,2,0:T(8,128)} %get-tuple-element.14, f32[6,512]{1,0:T(8,128)S(1)} %get-tuple-element.13), kind=kLoop, calls=%fused_computation.5 | loop fusion | flops 4715520 | bytes 6316032 | tf_op jit(solution)/shard_map/reduce_sum | solution.py:28
  297.9 0.6 copy-done
  298.5 2.5 fusion.7
  300.9 2.6 copy.75
  303.6 1.6 reshape.86
  305.2 2.6 copy.66
  307.9 2.4 reshape.83
  310.2 2.2 bitcast_reduce_fusion
  312.5 1.6 fusion.3
  314.1 1.9 fusion.5
  316.1 0.6 fusion.15
  316.7 1.2 copy.76
  (28 shorter events, 0.6 us)
Async XLA Ops:
  6.5 197.6 %all-reduce.4.cloned.1.call-start = ((), (), s32[]{:S(2)}) async-start(), calls=%async_computation.2 | async-start | bytes 3145728 | tf_op jit(solution)/shard_map/psum | solution.py:15
  7.3 54.3 %copy-start.7 = (f32[6]{0:T(128)S(1)}, f32[6]{0:T(128)}, u32[]{:S(2)}) copy-start(f32[6]{0:T(128)} %param.17) | copy-start | bytes 76
  7.3 54.4 %copy-start.1 = (bf16[512,768]{1,0:T(8,128)(2,1)S(1)}, bf16[512,768]{1,0:T(8,128)(2,1)}, u32[]{:S(2)}) copy-start(bf16[512,768]{1,0:T(8,128)(2,1)} %param.10) | copy-start | bytes 2359300
  7.3 55.7 %copy-start.6 = (s32[1,512]{1,0:T(1,128)S(1)}, s32[1,512]{1,0:T(1,128)}, u32[]{:S(2)}) copy-start(s32[1,512]{1,0:T(1,128)} %param.12) | copy-start | bytes 6148
  9.7 235.5 %copy-start.4 = (bf16[512,768]{1,0:T(8,128)(2,1)S(1)}, bf16[512,768]{1,0:T(8,128)(2,1)}, u32[]{:S(2)}) copy-start(bf16[512,768]{1,0:T(8,128)(2,1)} %param.9) | copy-start | bytes 2359300
  204.2 47.2 %all-to-all-start.1 = ((bf16[128,4,768]{0,2,1:T(8,128)(2,1)}), bf16[128,4,768]{0,2,1:T(8,128)(2,1)}, u32[]{:S(2)}, u32[]{:S(2)}) async-start(bf16[128,4,768]{0,2,1:T(8,128)(2,1)} %get-tuple-element.5), calls=%async_computation.1 | async-start | bytes 1572864 | tf_op jit(solution)/shard_map/all_to_all | solution.py:73
  246.5 9.4 %copy-start.2 = (bf16[512,768]{1,0:T(8,128)(2,1)S(1)}, bf16[512,768]{1,0:T(8,128)(2,1)}, u32[]{:S(2)}) copy-start(bf16[512,768]{1,0:T(8,128)(2,1)} %param.11) | copy-start | bytes 2359300
  251.4 53.8 %all-to-all-start = ((bf16[128,4,768]{0,2,1:T(8,128)(2,1)}), bf16[128,4,768]{0,2,1:T(8,128)(2,1)}, u32[]{:S(2)}, u32[]{:S(2)}) async-start(bf16[128,4,768]{0,2,1:T(8,128)(2,1)} %get-tuple-element.6), calls=%async_computation | async-start | bytes 1572864 | tf_op jit(solution)/shard_map/all_to_all | solution.py:72
  293.9 4.6 %copy-start = (f32[6,512,512]{1,2,0:T(8,128)S(1)}, f32[6,512,512]{1,2,0:T(8,128)}, u32[]{:S(2)}) copy-start(f32[6,512,512]{1,2,0:T(8,128)} %get-tuple-element.14) | copy-start | bytes 18874372
  314.1 2.0 copy-start.5
  314.1 2.0 copy-start.3
Sparse Core Ops, SparseCore 0:
  10.3 193.8 all-reduce.3
where the time goes:
time: 325 us
  waiting for transfers between devices  141 us (43%)
  blocking collectives  121 us (37%)
  local copies, waits for them, and re-layouts  18.9 us (6%)
  between operations  15 us (5%)
  matrix products  13.6 us (4%)
  starting transfers between devices  8.65 us (3%)
  other arithmetic  6.88 us (2%)
    psum x1, waiting for transfers between devices, spread(): return lax.psum(block, axis)  141 us
    unnamed x1, blocking collectives  49.1 us
    all_gather x1, blocking collectives, on_device(): lax.all_gather(pooled_keys, 'ctx', axis=0, tiled=True)  36.4 us
    all_gather x1, blocking collectives, on_device(): lax.all_gather(pooled_values, 'ctx', axis=0, tiled=True)  35.2 us
    dot_general x3, matrix products, group_terms(): jnp.einsum('qhd,khd->hqk', query_block, key_block, preferred_element_type...  8.16 us
    reduce_sum x3, other arithmetic, group_terms(): row_total = jnp.sum(exp_terms, axis=2)  6.54 us
  transfers between devices with their start and end apart: 3, of which 1 were waited for; matrix products, arithmetic and copies ran while one was open for 7% of the time, Pallas kernels for 0%

commit v1 on v0

v1 whole, which is shorter than its diff:
```python
import math

import jax
import jax.numpy as jnp
from jax import lax
from jax.experimental import pallas as pl
from jax.experimental.pallas import tpu as pltpu
from jax.sharding import Mesh, PartitionSpec as P

HD = 128
POOLS = 8
LOG2E = math.log2(math.e)
UNIT = LOG2E / math.sqrt(HD)
ROWS = 128
SWAP = [(0, 1), (1, 0)]


def dot_nt(a, b):
    return lax.dot_general(a, b, (((1,), (1,)), ((), ())), preferred_element_type=jnp.float32)


def dot_nn(a, b):
    return jnp.dot(a, b, preferred_element_type=jnp.float32)


def pool_kernel(tag_ref, seg_ref, key_ref, value_ref, out_ref):
    seg = seg_ref[...]
    member = seg == lax.broadcasted_iota(jnp.int32, (POOLS, seg.shape[1]), 0)
    count = jnp.sum(member.astype(jnp.float32), axis=1, keepdims=True)
    member = member.astype(jnp.float32).astype(jnp.bfloat16)
    width = key_ref.shape[1]
    out_ref[:, :width] = (dot_nn(member, key_ref[...]) / count).astype(jnp.bfloat16)
    out_ref[:, width : 2 * width] = (dot_nn(member, value_ref[...]) / count).astype(jnp.bfloat16)
    tag = jnp.full((POOLS, HD), tag_ref[0], jnp.int32)
    out_ref[:, 2 * width :] = tag.astype(jnp.float32).astype(jnp.bfloat16)


def soft(scores):
    row_max = jnp.max(scores, axis=1, keepdims=True)
    exp_terms = jnp.exp2(scores - row_max)
    return row_max, jnp.sum(exp_terms, axis=1, keepdims=True), exp_terms.astype(jnp.bfloat16)


def near_kernel(tag_ref, slope_ref, q_ref, k_ref, v_ref, pk_ref, pv_ref, pt_ref, acc_ref, stat_ref):
    head = pl.program_id(0)
    tags = pt_ref[...].astype(jnp.float32).T[0:1, :]
    bias = jnp.abs(tags - tag_ref[0].astype(jnp.float32)) * (slope_ref[head] * LOG2E)
    lane = lax.broadcasted_iota(jnp.int32, (ROWS, HD), 1)

    @pl.when(head == 0)
    def _():
        stat_ref[...] = jnp.zeros_like(stat_ref)

    for start in range(0, q_ref.shape[0], ROWS):
        rows = pl.ds(start, ROWS)
        q = q_ref[rows, :]
        max_w, total_w, weight_w = soft(dot_nt(q, k_ref[...]) * UNIT)
        num_w = dot_nn(weight_w, v_ref[...])
        max_p, total_p, weight_p = soft(dot_nt(q, pk_ref[...]) * UNIT - bias)
        num_p = dot_nn(weight_p, pv_ref[...])
        top = jnp.maximum(max_w, max_p)
        share_w, share_p = jnp.exp2(max_w - top), jnp.exp2(max_p - top)
        acc_ref[rows, :] = share_w * num_w + share_p * num_p
        total = share_w * total_w + share_p * total_p
        stat = jnp.where(lane == 2 * head, top, stat_ref[rows, :])
        stat_ref[rows, :] = jnp.where(lane == 2 * head + 1, total, stat)


def ref_kernel(core_ref, q_ref, own_ref, got_ref, acc_ref, stat_ref, out_ref):
    head = pl.program_id(0)
    first = core_ref[0] == 0
    keys = jnp.where(first, own_ref[...], got_ref[...])
    values = jnp.where(first, got_ref[...], own_ref[...])
    lane = lax.broadcasted_iota(jnp.int32, (ROWS, HD), 1)
    for start in range(0, q_ref.shape[0], ROWS):
        rows = pl.ds(start, ROWS)
        max_r, total_r, weight_r = soft(dot_nt(q_ref[rows, :], keys) * UNIT)
        num_r = dot_nn(weight_r, values)
        stat = stat_ref[rows, :]
        max_n = jnp.sum(jnp.where(lane == 2 * head, stat, 0.0), axis=1, keepdims=True)
        total_n = jnp.sum(jnp.where(lane == 2 * head + 1, stat, 0.0), axis=1, keepdims=True)
        top = jnp.maximum(max_n, max_r)
        share_n, share_r = jnp.exp2(max_n - top), jnp.exp2(max_r - top)
        total = share_n * total_n + share_r * total_r
        num = share_n * acc_ref[rows, :] + share_r * num_r
        out_ref[rows, :] = (num / total).astype(jnp.bfloat16)


SMEM = pl.BlockSpec(memory_space=pltpu.SMEM)
VMEM = pl.BlockSpec(memory_space=pltpu.VMEM)


def on_device(
    queries, keys, values, pool_segments, window_map, ref_owner, ref_keys, ref_values, slopes
):
    rows, width = queries.shape
    heads = width // HD
    n_zh, n_x, n_head = lax.axis_size("zh"), lax.axis_size("x"), lax.axis_size("head")
    ref_rows = ref_keys.shape[1]
    part = ref_rows // n_x
    core = lax.axis_index("c")
    owner = ref_owner[0]
    owner_c = owner % 2
    owner_x = (owner // 2) % n_x
    owner_z = owner // (2 * n_x)

    slot_k, slot_v = ref_keys[0], ref_values[0]
    got_k = lax.ppermute(slot_k, "c", [(1, 0)])
    got_v = lax.ppermute(slot_v, "c", [(0, 1)])
    mine = jnp.where(
        core == 0,
        jnp.where(owner_c == 0, slot_k, got_k),
        jnp.where(owner_c == 1, slot_v, got_v),
    )
    spread = lax.all_to_all(mine.reshape(n_x, part, -1), "x", 0, 0, tiled=True)
    piece = lax.dynamic_index_in_dim(spread, owner_x, 0, keepdims=False)
    piece = piece.reshape(part, n_head, width).transpose(1, 0, 2)
    piece = jnp.broadcast_to(piece[None], (n_zh, n_head, part, width))
    turned = lax.all_to_all(
        piece.reshape(n_zh * n_head, part, width), ("zh", "head"), 0, 0, tiled=True
    )
    turned = turned.reshape(n_zh, n_head * part, width)
    block = lax.dynamic_index_in_dim(turned, owner_z, 0, keepdims=False)
    block = jnp.broadcast_to(block[None], (n_x, n_head * part, width))
    own = lax.all_to_all(block, "x", 0, 0, tiled=True).reshape(-1, width)
    got = lax.ppermute(own, "c", SWAP)

    pooled = pl.pallas_call(
        pool_kernel,
        out_shape=jax.ShapeDtypeStruct((POOLS, 2 * width + HD), jnp.bfloat16),
        in_specs=[SMEM, VMEM, VMEM, VMEM],
        out_specs=VMEM,
        name="pool",
    )(window_map, pool_segments, keys, values)

    def double(block, axis, pairs):
        return jnp.concatenate([block, lax.ppermute(block, axis, pairs)], axis=0)

    pooled = double(pooled, "zh", SWAP)
    pooled = double(pooled, "x", [(i, i ^ 1) for i in range(n_x)])
    pooled = double(pooled, "x", [(i, i ^ 2) for i in range(n_x)])
    pooled = double(pooled, "c", SWAP)
    count = pooled.shape[0]

    by_head = pl.BlockSpec((rows, HD), lambda h: (0, h))
    acc, stat = pl.pallas_call(
        near_kernel,
        grid=(heads,),
        out_shape=(
            jax.ShapeDtypeStruct((rows, width), jnp.float32),
            jax.ShapeDtypeStruct((rows, HD), jnp.float32),
        ),
        in_specs=[
            SMEM,
            SMEM,
            by_head,
            by_head,
            by_head,
            pl.BlockSpec((count, HD), lambda h: (0, h)),
            pl.BlockSpec((count, HD), lambda h: (0, heads + h)),
            pl.BlockSpec((count, HD), lambda h: (0, 2 * heads)),
        ],
        out_specs=(by_head, pl.BlockSpec((rows, HD), lambda h: (0, 0))),
        compiler_params=pltpu.CompilerParams(vmem_limit_bytes=32 * 1024 * 1024),
        name="near",
    )(window_map, slopes, queries, keys, values, pooled, pooled, pooled)

    ref_block = pl.BlockSpec((own.shape[0], HD), lambda h: (0, h))
    return pl.pallas_call(
        ref_kernel,
        grid=(heads,),
        out_shape=jax.ShapeDtypeStruct((rows, width), jnp.bfloat16),
        in_specs=[
            SMEM,
            by_head,
            ref_block,
            ref_block,
            by_head,
            pl.BlockSpec((rows, HD), lambda h: (0, 0)),
        ],
        out_specs=by_head,
        compiler_params=pltpu.CompilerParams(vmem_limit_bytes=32 * 1024 * 1024),
        name="far",
    )(core.astype(jnp.int32)[None], queries, own, got, acc, stat)


def solution(mesh):
    shape = mesh.shape
    ctx = shape["ctx"]
    fine = Mesh(
        mesh.devices.reshape(shape["dp"], 2, ctx // 4, 2, shape["head"]),
        ("dp", "zh", "x", "c", "head"),
    )
    token = ("dp", "zh", "x", "c")
    return jax.shard_map(
        on_device,
        mesh=fine,
        in_specs=(
            P(token, "head"),
            P(token, "head"),
            P(token, "head"),
            P(token, None),
            P(token),
            P("dp"),
            P(token, "head", None),
            P(token, "head", None),
            P("head"),
        ),
        out_specs=P(token, "head"),
        check_vma=False,
    )
```

time: 325 us -> 101 us (0.31)
  blocking collectives: 121 us -> 0 us
  waiting for transfers between devices: 141 us -> 20.3 us
  starting transfers between devices: 8.65 us -> 48 us
  Pallas kernels: 0 us -> 25.3 us
  local copies, waits for them, and re-layouts: 18.9 us -> 2.74 us
  matrix products: 13.6 us -> 0 us
  between operations: 15 us -> 1.61 us
  other arithmetic: 6.88 us -> 2.43 us
    psum x1 -> x0, waiting for transfers between devices: 141 us -> none  [spread(): return lax.psum(block, axis)]
    all_gather x2 -> x0, blocking collectives: 71.6 us -> none  [the longest x1 36.4 us: on_device(): lax.all_gather(pooled_keys, 'ctx', axis=0, tiled=True)]
    unnamed x1 -> x0, blocking collectives: 49.1 us -> none
    ppermute x0 -> x7, starting transfers between devices: none -> 35.6 us  [the longest x4 18.3 us: double(): return jnp.concatenate([block, lax.ppermute(block, axis, pairs)], axis=0)]
    pallas_call x0 -> x3, Pallas kernels: none -> 25.3 us  [the longest x1 14.4 us: on_device(): pl.pallas_call(near_kernel, grid=(heads,), out_shape=(jax.ShapeDtypeStruc...]
    dot_general x8 -> x0, matrix products: 13.6 us -> none  [the longest x3 8.16 us: group_terms(): jnp.einsum('qhd,khd->hqk', query_block, key_block, preferred_element_type...]
    all_to_all x2 -> x3, waiting for transfers between devices: 0.01 us -> 13.2 us  [the longest x1 12 us: on_device(): spread = lax.all_to_all(mine.reshape(n_x, part, -1), 'x', 0, 0, tiled=True)]
    ppermute x0 -> x7, waiting for transfers between devices: none -> 7.14 us  [the longest x4 5.76 us: double(): return jnp.concatenate([block, lax.ppermute(block, axis, pairs)], axis=0)]
  transfers between devices with their start and end apart: 3 -> 10, of which waited for: 1 -> 5; matrix products, arithmetic and copies ran while one was open for 7% -> 2% of each run, Pallas kernels for 0% -> 17%
where the time goes in v1:
time: 101 us; the launch traced here: 100 us
  starting transfers between devices  48 us (48%)
  Pallas kernels  25.3 us (25%)
  waiting for transfers between devices  20.3 us (20%)
  local copies, waits for them, and re-layouts  2.74 us (3%)
  other arithmetic  2.43 us (2%)
  between operations  1.61 us (2%)
    ppermute x4, starting transfers between devices, double(): return jnp.concatenate([block, lax.ppermute(block, axis, pairs)], axis=0)  18.3 us
    pallas_call x1, Pallas kernels, on_device(): pl.pallas_call(near_kernel, grid=(heads,), out_shape=(jax.ShapeDtypeStruc...  14.4 us
    all_to_all x1, waiting for transfers between devices, on_device(): spread = lax.all_to_all(mine.reshape(n_x, part, -1), 'x', 0, 0, tiled=True)  12 us
    ppermute x1, starting transfers between devices, on_device(): got_k = lax.ppermute(slot_k, 'c', [(1, 0)])  8.88 us
    pallas_call x1, Pallas kernels, on_device(): pl.pallas_call(ref_kernel, grid=(heads,), out_shape=jax.ShapeDtypeStruct(...  8.57 us
    ppermute x1, starting transfers between devices, on_device(): got = lax.ppermute(own, 'c', SWAP)  7.08 us
    ppermute x4, waiting for transfers between devices, double(): return jnp.concatenate([block, lax.ppermute(block, axis, pairs)], axis=0)  5.76 us
    all_to_all x1, starting transfers between devices, on_device(): lax.all_to_all(piece.reshape(n_zh * n_head, part, width), ('zh', 'head'),...  5.33 us
  transfers between devices with their start and end apart: 10, of which 5 were waited for; matrix products, arithmetic and copies ran while one was open for 2% of the time, Pallas kernels for 17%

profile of v1, /device:TPU:1, one launch (start us, length us, event | category | flops | bytes accessed | tf_op | source)
XLA Modules:
  0.0 100.4 jit_solution(7714289442964008190)
XLA Ops:
  0.0 1.3 %collective-permute-start.1 = (bf16[128,3072]{1,0:T(8,128)(2,1)}, bf16[128,3072]{1,0:T(8,128)(2,1)S(1)}, u32[]{:S(2)}, u32[]{:S(2)}) collective-permute-start(bf16[128,3072]{1,0:T(8,128)(2,1)} %bitcast.21), channel_id=1, source_target_pairs={{0,4},{1,5},{2,6},{3,7},{8,12},{9,13},{10,14},{11,15},{16,20},{17,... | collective-permute-start | bytes 2359304 | tf_op jit(solution)/shard_map/ppermute | solution.py:109
  1.3 8.9 %collective-permute-start = (bf16[128,3072]{1,0:T(8,128)(2,1)}, bf16[128,3072]{1,0:T(8,128)(2,1)S(1)}, u32[]{:S(2)}, u32[]{:S(2)}) collective-permute-start(bf16[128,3072]{1,0:T(8,128)(2,1)} %bitcast.22), channel_id=1, source_target_pairs={{4,0},{5,1},{6,2},{7,3},{12,8},{13,9},{14,10},{15,11},{20,16},{21,... | collective-permute-start | bytes 2359304 | tf_op jit(solution)/shard_map/ppermute | solution.py:108
  10.8 0.0 collective-permute-done.1
  10.9 1.4 %collective-permute-done = bf16[128,3072]{1,0:T(8,128)(2,1)S(1)} collective-permute-done((bf16[128,3072]{1,0:T(8,128)(2,1)}, bf16[128,3072]{1,0:T(8,128)(2,1)S(1)}, u32[]{:S(2)}, u32[]{:S(2)}) %collective-permute-start) | collective-permute-done | bytes 786464 | tf_op jit(solution)/shard_map/ppermute | solution.py:108
  12.2 2.4 %select_select_fusion = bf16[128,3072]{1,0:T(8,128)(2,1)} fusion(bf16[128,3072]{1,0:T(8,128)(2,1)S(1)} %collective-permute-done.1, bf16[128,3072]{1,0:T(8,128)(2,1)S(1)} %collective-permute-done, pred[]{:T(512)S(6)} %eq.14, pred[]{:T(512)S(6)} %eq.13, pred[]{:T(512)S(6)} %eq.12, bf16[1,128,3072]{2,1,0:T(8,128)(2,1)} %param.16, bf16[1,128,3072]{2,1,0:T(8,128)(2,1)} %param.15), kind=kLoop, calls=%fused_computation | loop fusion | flops 1179648 | bytes 3932163 | tf_op jit(solution)/shard_map/jit(_where)/select_n | solution.py:110
  14.6 3.5 %all-to-all-start = ((bf16[4,32,3072]{2,1,0:T(8,128)(2,1)}), bf16[4,32,3072]{2,1,0:T(8,128)(2,1)S(1)}, u32[]{:S(2)}, u32[]{:S(2)}) async-start(bf16[4,32,3072]{2,1,0:T(8,128)(2,1)} %bitcast.4), calls=%async_computation | async-start | bytes 1572864 | tf_op jit(solution)/shard_map/all_to_all | solution.py:115
  18.2 12.0 %all-to-all-done = bf16[4,32,3072]{2,1,0:T(8,128)(2,1)S(1)} async-done(((bf16[4,32,3072]{2,1,0:T(8,128)(2,1)}), bf16[4,32,3072]{2,1,0:T(8,128)(2,1)S(1)}, u32[]{:S(2)}, u32[]{:S(2)}) %all-to-all-start) | async-done | bytes 786464 | tf_op jit(solution)/shard_map/all_to_all | solution.py:115
  30.1 0.1 reshape.18
  30.3 0.8 broadcast_in_dim.18
  31.1 5.3 %all-to-all-start.1 = ((bf16[8,32,768]{2,1,0:T(8,128)(2,1)}), bf16[8,32,768]{2,1,0:T(8,128)(2,1)S(1)}, u32[]{:S(2)}, u32[]{:S(2)}) async-start(bf16[8,32,768]{2,1,0:T(8,128)(2,1)} %bitcast.6), calls=%async_computation.1 | async-start | bytes 786432 | tf_op jit(solution)/shard_map/all_to_all | solution.py:119
  37.1 2.3 %pool.1 = bf16[8,1664]{1,0:T(8,128)(2,1)} custom-call(s32[1]{0:T(128)S(6)} %copy.15.tag_ref, s32[1,512]{1,0:T(1,128)} %seg_ref.1, bf16[512,768]{1,0:T(8,128)(2,1)} %k_ref.1, bf16[512,768]{1,0:T(8,128)(2,1)} %v_ref.1), custom_call_target="tpu_custom_call" | custom-call | tf_op jit(solution)/shard_map/pool/pallas_call | solution.py:128
  39.4 7.4 %collective-permute-start.3 = (bf16[8,1664]{1,0:T(8,128)(2,1)}, bf16[8,1664]{1,0:T(8,128)(2,1)S(1)}, u32[]{:S(2)}, u32[]{:S(2)}) collective-permute-start(bf16[8,1664]{1,0:T(8,128)(2,1)} %pool.1), channel_id=1, source_target_pairs={{0,32},{32,0},{1,33},{33,1},{2,34},{34,2},{3,35},{35,3},{4,36},{36... | collective-permute-start | bytes 79880 | tf_op jit(solution)/shard_map/ppermute | solution.py:137
  46.8 0.8 constant_dynamic-update-slice_fusion.4
  47.6 1.2 %all-to-all-done.1 = bf16[8,32,768]{2,1,0:T(8,128)(2,1)S(1)} async-done(((bf16[8,32,768]{2,1,0:T(8,128)(2,1)}), bf16[8,32,768]{2,1,0:T(8,128)(2,1)S(1)}, u32[]{:S(2)}, u32[]{:S(2)}) %all-to-all-start.1) | async-done | bytes 393248 | tf_op jit(solution)/shard_map/all_to_all | solution.py:119
  48.8 0.9 broadcast_in_dim.20
  49.7 3.6 %all-to-all-start.2 = ((bf16[4,128,768]{2,1,0:T(8,128)(2,1)}), bf16[4,128,768]{2,1,0:T(8,128)(2,1)S(1)}, u32[]{:S(2)}, u32[]{:S(2)}) async-start(bf16[4,128,768]{2,1,0:T(8,128)(2,1)} %broadcast_in_dim.20), calls=%async_computation.2 | async-start | bytes 1572864 | tf_op jit(solution)/shard_map/all_to_all | solution.py:125
  53.4 0.0 collective-permute-done.3
  53.4 0.0 copy-done.4
  53.4 3.3 %collective-permute-start.4 = (bf16[16,1664]{1,0:T(8,128)(2,1)S(1)}, bf16[16,1664]{1,0:T(8,128)(2,1)S(1)}, u32[]{:S(2)}, u32[]{:S(2)}) collective-permute-start(bf16[16,1664]{1,0:T(8,128)(2,1)S(1)} %pad_maximum_fusion.2), channel_id=1, source_target_pairs={{0,8},{8,0},{16,24},{24,16},{1,9},{9,1},{17,25},{25,17},{2,10},{10... | collective-permute-start | bytes 159752 | tf_op jit(solution)/shard_map/ppermute | solution.py:137
  56.8 4.7 %collective-permute-done.4 = bf16[16,1664]{1,0:T(8,128)(2,1)S(1)} collective-permute-done((bf16[16,1664]{1,0:T(8,128)(2,1)S(1)}, bf16[16,1664]{1,0:T(8,128)(2,1)S(1)}, u32[]{:S(2)}, u32[]{:S(2)}) %collective-permute-start.4) | collective-permute-done | bytes 53280 | tf_op jit(solution)/shard_map/ppermute | solution.py:137
  61.5 4.3 %collective-permute-start.5 = (bf16[32,1664]{1,0:T(8,128)(2,1)S(1)}, bf16[32,1664]{1,0:T(8,128)(2,1)S(1)}, u32[]{:S(2)}, u32[]{:S(2)}) collective-permute-start(bf16[32,1664]{1,0:T(8,128)(2,1)S(1)} %pad_maximum_fusion.1), channel_id=1, source_target_pairs={{0,16},{8,24},{16,0},{24,8},{1,17},{9,25},{17,1},{25,9},{2,18},{10... | collective-permute-start | bytes 319496 | tf_op jit(solution)/shard_map/ppermute | solution.py:137
  65.8 0.0 all-to-all-done.2
  65.8 0.0 copy-start.2
  65.8 7.1 %collective-permute-start.2 = (bf16[512,768]{1,0:T(8,128)(2,1)S(1)}, bf16[512,768]{1,0:T(8,128)(2,1)S(1)}, u32[]{:S(2)}, u32[]{:S(2)}) collective-permute-start(bf16[512,768]{1,0:T(8,128)(2,1)S(1)} %bitcast.17), channel_id=1, source_target_pairs={{0,4},{4,0},{1,5},{5,1},{2,6},{6,2},{3,7},{7,3},{8,12},{12,8},{9,1... | collective-permute-start | bytes 2359304 | tf_op jit(solution)/shard_map/ppermute | solution.py:126
  72.9 0.0 collective-permute-done.5
  73.0 3.3 %collective-permute-start.6 = (bf16[64,1664]{1,0:T(8,128)(2,1)S(1)}, bf16[64,1664]{1,0:T(8,128)(2,1)S(1)}, u32[]{:S(2)}, u32[]{:S(2)}) collective-permute-start(bf16[64,1664]{1,0:T(8,128)(2,1)S(1)} %pad_maximum_fusion), channel_id=1, source_target_pairs={{0,4},{4,0},{1,5},{5,1},{2,6},{6,2},{3,7},{7,3},{8,12},{12,8},{9,1... | collective-permute-start | bytes 638984 | tf_op jit(solution)/shard_map/ppermute | solution.py:137
  76.3 1.0 %collective-permute-done.6 = bf16[64,1664]{1,0:T(8,128)(2,1)S(1)} collective-permute-done((bf16[64,1664]{1,0:T(8,128)(2,1)S(1)}, bf16[64,1664]{1,0:T(8,128)(2,1)S(1)}, u32[]{:S(2)}, u32[]{:S(2)}) %collective-permute-start.6) | collective-permute-done | bytes 213024 | tf_op jit(solution)/shard_map/ppermute | solution.py:137
  77.4 0.0 copy-done
  77.4 0.0 copy-done.1
  77.4 14.4 %near.1 = (f32[512,768]{1,0:T(8,128)S(1)}, f32[512,128]{1,0:T(8,128)S(1)}) custom-call(s32[1]{0:T(128)S(6)} %copy.15.tag_ref, f32[6]{0:T(128)S(1)} %copy-done.3, bf16[512,768]{1,0:T(8,128)(2,1)S(1)} %copy-done, bf16[512,768]{1,0:T(8,128)(2,1)S(1)} %copy-done.1, bf16[512,768]{1,0:T(8,128)(2,1)S(1)} %copy-done.2, ...), custom_call_target="tpu_custom_call" | custom-call | tf_op jit(solution)/shard_map/near/pallas_call | solution.py:146
  91.8 0.0 collective-permute-done.2.got_ref
  91.8 8.6 %far.1 = bf16[512,768]{1,0:T(8,128)(2,1)} custom-call(s32[1]{0:T(128)} %bitcast.core_ref, bf16[512,768]{1,0:T(8,128)(2,1)S(1)} %copy-done, bf16[512,768]{1,0:T(8,128)(2,1)S(1)} %bitcast.18, bf16[512,768]{1,0:T(8,128)(2,1)S(1)} %collective-permute-done.2.got_ref, f32[512,768]{1,0:T(8,128)S(1)} %get-tuple-element.7.acc_ref, ...), custom_call_target="tpu_custom_call" | custom-call | tf_op jit(solution)/shard_map/far/pallas_call | solution.py:169
  (16 shorter events, 0.2 us)
Async XLA Ops:
  0.0 10.8 %collective-permute-start.1 = (bf16[128,3072]{1,0:T(8,128)(2,1)}, bf16[128,3072]{1,0:T(8,128)(2,1)S(1)}, u32[]{:S(2)}, u32[]{:S(2)}) collective-permute-start(bf16[128,3072]{1,0:T(8,128)(2,1)} %bitcast.21), channel_id=1, source_target_pairs={{0,4},{1,5},{2,6},{3,7},{8,12},{9,13},{10,14},{11,15},{16,20},{17,... | collective-permute-start | bytes 2359304 | tf_op jit(solution)/shard_map/ppermute | solution.py:109
  1.3 10.9 %collective-permute-start = (bf16[128,3072]{1,0:T(8,128)(2,1)}, bf16[128,3072]{1,0:T(8,128)(2,1)S(1)}, u32[]{:S(2)}, u32[]{:S(2)}) collective-permute-start(bf16[128,3072]{1,0:T(8,128)(2,1)} %bitcast.22), channel_id=1, source_target_pairs={{4,0},{5,1},{6,2},{7,3},{12,8},{13,9},{14,10},{15,11},{20,16},{21,... | collective-permute-start | bytes 2359304 | tf_op jit(solution)/shard_map/ppermute | solution.py:108
  14.6 15.5 %all-to-all-start = ((bf16[4,32,3072]{2,1,0:T(8,128)(2,1)}), bf16[4,32,3072]{2,1,0:T(8,128)(2,1)S(1)}, u32[]{:S(2)}, u32[]{:S(2)}) async-start(bf16[4,32,3072]{2,1,0:T(8,128)(2,1)} %bitcast.4), calls=%async_computation | async-start | bytes 1572864 | tf_op jit(solution)/shard_map/all_to_all | solution.py:115
  31.1 17.7 %all-to-all-start.1 = ((bf16[8,32,768]{2,1,0:T(8,128)(2,1)}), bf16[8,32,768]{2,1,0:T(8,128)(2,1)S(1)}, u32[]{:S(2)}, u32[]{:S(2)}) async-start(bf16[8,32,768]{2,1,0:T(8,128)(2,1)} %bitcast.6), calls=%async_computation.1 | async-start | bytes 786432 | tf_op jit(solution)/shard_map/all_to_all | solution.py:119
  39.4 14.0 %copy-start.4 = (bf16[8,1664]{1,0:T(8,128)(2,1)S(1)}, bf16[8,1664]{1,0:T(8,128)(2,1)}, u32[]{:S(2)}) copy-start(bf16[8,1664]{1,0:T(8,128)(2,1)} %pool.1) | copy-start | bytes 79876
  39.4 14.0 %collective-permute-start.3 = (bf16[8,1664]{1,0:T(8,128)(2,1)}, bf16[8,1664]{1,0:T(8,128)(2,1)S(1)}, u32[]{:S(2)}, u32[]{:S(2)}) collective-permute-start(bf16[8,1664]{1,0:T(8,128)(2,1)} %pool.1), channel_id=1, source_target_pairs={{0,32},{32,0},{1,33},{33,1},{2,34},{34,2},{3,35},{35,3},{4,36},{36... | collective-permute-start | bytes 79880 | tf_op jit(solution)/shard_map/ppermute | solution.py:137
  49.7 27.6 %copy-start = (bf16[512,768]{1,0:T(8,128)(2,1)S(1)}, bf16[512,768]{1,0:T(8,128)(2,1)}, u32[]{:S(2)}) copy-start(bf16[512,768]{1,0:T(8,128)(2,1)} %q_ref.3) | copy-start | bytes 2359300
  49.7 27.6 %copy-start.1 = (bf16[512,768]{1,0:T(8,128)(2,1)S(1)}, bf16[512,768]{1,0:T(8,128)(2,1)}, u32[]{:S(2)}) copy-start(bf16[512,768]{1,0:T(8,128)(2,1)} %k_ref.1) | copy-start | bytes 2359300
  49.7 27.6 %copy-start.3 = (f32[6]{0:T(128)S(1)}, f32[6]{0:T(128)}, u32[]{:S(2)}) copy-start(f32[6]{0:T(128)} %slope_ref.1) | copy-start | bytes 76
  49.7 16.0 %all-to-all-start.2 = ((bf16[4,128,768]{2,1,0:T(8,128)(2,1)}), bf16[4,128,768]{2,1,0:T(8,128)(2,1)S(1)}, u32[]{:S(2)}, u32[]{:S(2)}) async-start(bf16[4,128,768]{2,1,0:T(8,128)(2,1)} %broadcast_in_dim.20), calls=%async_computation.2 | async-start | bytes 1572864 | tf_op jit(solution)/shard_map/all_to_all | solution.py:125
  53.4 8.0 %collective-permute-start.4 = (bf16[16,1664]{1,0:T(8,128)(2,1)S(1)}, bf16[16,1664]{1,0:T(8,128)(2,1)S(1)}, u32[]{:S(2)}, u32[]{:S(2)}) collective-permute-start(bf16[16,1664]{1,0:T(8,128)(2,1)S(1)} %pad_maximum_fusion.2), channel_id=1, source_target_pairs={{0,8},{8,0},{16,24},{24,16},{1,9},{9,1},{17,25},{25,17},{2,10},{10... | collective-permute-start | bytes 159752 | tf_op jit(solution)/shard_map/ppermute | solution.py:137
  61.5 11.4 %collective-permute-start.5 = (bf16[32,1664]{1,0:T(8,128)(2,1)S(1)}, bf16[32,1664]{1,0:T(8,128)(2,1)S(1)}, u32[]{:S(2)}, u32[]{:S(2)}) collective-permute-start(bf16[32,1664]{1,0:T(8,128)(2,1)S(1)} %pad_maximum_fusion.1), channel_id=1, source_target_pairs={{0,16},{8,24},{16,0},{24,8},{1,17},{9,25},{17,1},{25,9},{2,18},{10... | collective-permute-start | bytes 319496 | tf_op jit(solution)/shard_map/ppermute | solution.py:137
  65.8 11.6 %copy-start.2 = (bf16[512,768]{1,0:T(8,128)(2,1)S(1)}, bf16[512,768]{1,0:T(8,128)(2,1)}, u32[]{:S(2)}) copy-start(bf16[512,768]{1,0:T(8,128)(2,1)} %v_ref.1) | copy-start | bytes 2359300
  65.8 26.0 %collective-permute-start.2 = (bf16[512,768]{1,0:T(8,128)(2,1)S(1)}, bf16[512,768]{1,0:T(8,128)(2,1)S(1)}, u32[]{:S(2)}, u32[]{:S(2)}) collective-permute-start(bf16[512,768]{1,0:T(8,128)(2,1)S(1)} %bitcast.17), channel_id=1, source_target_pairs={{0,4},{4,0},{1,5},{5,1},{2,6},{6,2},{3,7},{7,3},{8,12},{12,8},{9,1... | collective-permute-start | bytes 2359304 | tf_op jit(solution)/shard_map/ppermute | solution.py:126
  73.0 4.4 %collective-permute-start.6 = (bf16[64,1664]{1,0:T(8,128)(2,1)S(1)}, bf16[64,1664]{1,0:T(8,128)(2,1)S(1)}, u32[]{:S(2)}, u32[]{:S(2)}) collective-permute-start(bf16[64,1664]{1,0:T(8,128)(2,1)S(1)} %pad_maximum_fusion), channel_id=1, source_target_pairs={{0,4},{4,0},{1,5},{5,1},{2,6},{6,2},{3,7},{7,3},{8,12},{12,8},{9,1... | collective-permute-start | bytes 638984 | tf_op jit(solution)/shard_map/ppermute | solution.py:137

commit v2 on v1

v2 whole, which is shorter than its diff:
```python
import math

import jax
import jax.numpy as jnp
from jax import lax
from jax.experimental import pallas as pl
from jax.experimental.pallas import tpu as pltpu
from jax.sharding import Mesh, PartitionSpec as P

HD = 128
POOLS = 8
LOG2E = math.log2(math.e)
UNIT = LOG2E / math.sqrt(HD)
STRIP = 128
SWAP = [(0, 1), (1, 0)]


def dot_nt(a, b):
    return lax.dot_general(a, b, (((1,), (1,)), ((), ())), preferred_element_type=jnp.float32)


def dot_nn(a, b):
    return jnp.dot(a, b, preferred_element_type=jnp.float32)


def pool_kernel(tag_ref, seg_ref, key_ref, value_ref, out_ref):
    seg = seg_ref[...]
    member = seg == lax.broadcasted_iota(jnp.int32, (POOLS, seg.shape[1]), 0)
    count = jnp.sum(member.astype(jnp.float32), axis=1, keepdims=True)
    member = member.astype(jnp.float32).astype(jnp.bfloat16)
    width = key_ref.shape[1]
    out_ref[:, :width] = (dot_nn(member, key_ref[...]) / count).astype(jnp.bfloat16)
    out_ref[:, width : 2 * width] = (dot_nn(member, value_ref[...]) / count).astype(jnp.bfloat16)
    tag = jnp.full((POOLS, HD), tag_ref[0], jnp.int32)
    out_ref[:, 2 * width :] = tag.astype(jnp.float32).astype(jnp.bfloat16)


def soft(scores):
    top = jnp.max(scores, axis=0, keepdims=True)
    exp_terms = jnp.exp2(scores - top)
    return top, jnp.sum(exp_terms, axis=0, keepdims=True), exp_terms.astype(jnp.bfloat16)


def window_kernel(q_ref, k_ref, v_ref, acc_ref, stat_ref):
    for head in range(q_ref.shape[1] // HD):
        cols = pl.ds(head * HD, HD)
        values = v_ref[:, cols].T
        for start in range(0, q_ref.shape[0], STRIP):
            rows = pl.ds(start, STRIP)
            top, total, weights = soft(dot_nt(k_ref[:, cols], q_ref[rows, cols]) * UNIT)
            acc_ref[cols, rows] = dot_nn(values, weights)
            stat_ref[2 * head : 2 * head + 1, rows] = top
            stat_ref[2 * head + 1 : 2 * head + 2, rows] = total


def pooled_kernel(tag_ref, slope_ref, q_ref, p_ref, acc_ref, stat_ref):
    count, width = q_ref.shape
    tags = p_ref[:, 2 * width :].astype(jnp.float32)
    dist = jnp.abs(tags - tag_ref[0].astype(jnp.float32)) * LOG2E
    dist = jnp.concatenate([dist] * (count // HD), axis=1)
    for head in range(width // HD):
        cols = pl.ds(head * HD, HD)
        scores = dot_nt(p_ref[:, cols], q_ref[:, cols]) * UNIT - dist * slope_ref[head]
        top, total, weights = soft(scores)
        acc_ref[cols, :] = dot_nn(p_ref[:, pl.ds(width + head * HD, HD)].T, weights)
        stat_ref[2 * head : 2 * head + 1, :] = top
        stat_ref[2 * head + 1 : 2 * head + 2, :] = total


def ref_kernel(
    core_ref, q_ref, own_ref, got_ref, acc_w_ref, stat_w_ref, acc_p_ref, stat_p_ref, out_ref
):
    first = core_ref[0] == 0
    for head in range(q_ref.shape[1] // HD):
        cols = pl.ds(head * HD, HD)
        top_at, total_at = slice(2 * head, 2 * head + 1), slice(2 * head + 1, 2 * head + 2)
        keys = jnp.where(first, own_ref[:, cols], got_ref[:, cols])
        values = jnp.where(first, got_ref[:, cols], own_ref[:, cols]).T
        for start in range(0, q_ref.shape[0], STRIP):
            rows = pl.ds(start, STRIP)
            top, total, weights = soft(dot_nt(keys, q_ref[rows, cols]) * UNIT)
            num = dot_nn(values, weights)
            top_w, top_p = stat_w_ref[top_at, rows], stat_p_ref[top_at, rows]
            ceiling = jnp.maximum(jnp.maximum(top_w, top_p), top)
            share_w, share_p = jnp.exp2(top_w - ceiling), jnp.exp2(top_p - ceiling)
            share = jnp.exp2(top - ceiling)
            scale = 1.0 / (
                share_w * stat_w_ref[total_at, rows]
                + share_p * stat_p_ref[total_at, rows]
                + share * total
            )
            merged = (
                (share_w * scale) * acc_w_ref[cols, rows]
                + (share_p * scale) * acc_p_ref[cols, rows]
                + (share * scale) * num
            )
            out_ref[rows, cols] = merged.astype(jnp.bfloat16).T


SMEM = pl.BlockSpec(memory_space=pltpu.SMEM)
VMEM = pl.BlockSpec(memory_space=pltpu.VMEM)


def on_device(
    queries, keys, values, pool_segments, window_map, ref_owner, ref_keys, ref_values, slopes
):
    rows, width = queries.shape
    heads = width // HD
    n_zh, n_x, n_head = lax.axis_size("zh"), lax.axis_size("x"), lax.axis_size("head")
    ref_rows = ref_keys.shape[1]
    part = ref_rows // n_x
    core = lax.axis_index("c")
    owner = ref_owner[0]
    owner_c = owner % 2
    owner_x = (owner // 2) % n_x
    owner_z = owner // (2 * n_x)

    tie = lax.optimization_barrier
    near = pltpu.CompilerParams(vmem_limit_bytes=16 * 1024 * 1024)
    state = (
        jax.ShapeDtypeStruct((width, rows), jnp.float32),
        jax.ShapeDtypeStruct((16, rows), jnp.float32),
    )

    slot_k, slot_v = ref_keys[0], ref_values[0]
    got_k = lax.ppermute(slot_k, "c", [(1, 0)])
    got_v = lax.ppermute(slot_v, "c", [(0, 1)])
    kept = tie(jnp.where(core == 0, slot_k, slot_v))
    pooled = pl.pallas_call(
        pool_kernel,
        out_shape=jax.ShapeDtypeStruct((POOLS, 2 * width + HD), jnp.bfloat16),
        in_specs=[SMEM, VMEM, VMEM, VMEM],
        out_specs=VMEM,
        name="pool",
    )(window_map, pool_segments, keys, values)
    mine = jnp.where(owner_c == core, kept, jnp.where(core == 0, got_k, got_v))
    mine, pooled = tie((mine, pooled))

    spread = lax.all_to_all(mine.reshape(n_x, part, -1), "x", 0, 0, tiled=True)
    other = lax.ppermute(pooled, "zh", SWAP)
    piece = lax.dynamic_index_in_dim(spread, owner_x, 0, keepdims=False)
    piece = piece.reshape(part, n_head, width).transpose(1, 0, 2)
    piece = jnp.broadcast_to(piece[None], (n_zh, n_head, part, width))
    piece, pooled, other = tie((piece, pooled, other))

    turned = lax.all_to_all(
        piece.reshape(n_zh * n_head, part, width), ("zh", "head"), 0, 0, tiled=True
    )
    pooled = jnp.concatenate([pooled, other], axis=0)
    other = lax.ppermute(pooled, "c", SWAP)
    pooled = jnp.concatenate([pooled, other], axis=0)
    other = lax.ppermute(pooled, "x", [(i, i ^ 1) for i in range(n_x)])
    pooled = jnp.concatenate([pooled, other], axis=0)
    turned = turned.reshape(n_zh, n_head * part, width)
    block = lax.dynamic_index_in_dim(turned, owner_z, 0, keepdims=False)
    block = jnp.broadcast_to(block[None], (n_x, n_head * part, width))
    block, pooled, queries_w = tie((block, pooled, queries))

    own = lax.all_to_all(block, "x", 0, 0, tiled=True).reshape(-1, width)
    other = lax.ppermute(pooled, "x", [(i, i ^ 2) for i in range(n_x)])
    acc_w, stat_w = pl.pallas_call(
        window_kernel,
        out_shape=state,
        in_specs=[VMEM] * 3,
        out_specs=(VMEM, VMEM),
        compiler_params=near,
        cost_estimate=pl.CostEstimate(
            flops=4 * rows * rows * width,
            bytes_accessed=10 * rows * width,
            transcendentals=rows * rows * heads,
        ),
        name="window",
    )(queries_w, keys, values)
    pooled = jnp.concatenate([pooled, other], axis=0)
    own, pooled, acc_w, stat_w = tie((own, pooled, acc_w, stat_w))

    got = lax.ppermute(own, "c", SWAP)
    acc_p, stat_p = pl.pallas_call(
        pooled_kernel,
        out_shape=state,
        in_specs=[SMEM, SMEM, VMEM, VMEM],
        out_specs=(VMEM, VMEM),
        compiler_params=near,
        cost_estimate=pl.CostEstimate(
            flops=4 * rows * pooled.shape[0] * width,
            bytes_accessed=6 * rows * width,
            transcendentals=rows * pooled.shape[0] * heads,
        ),
        name="pooled",
    )(window_map, slopes, queries, pooled)
    return pl.pallas_call(
        ref_kernel,
        out_shape=jax.ShapeDtypeStruct((rows, width), jnp.bfloat16),
        in_specs=[SMEM] + [VMEM] * 7,
        out_specs=VMEM,
        compiler_params=near,
        name="far",
    )(core.astype(jnp.int32)[None], queries, own, got, acc_w, stat_w, acc_p, stat_p)


def solution(mesh):
    shape = mesh.shape
    ctx = shape["ctx"]
    fine = Mesh(
        mesh.devices.reshape(shape["dp"], 2, ctx // 4, 2, shape["head"]),
        ("dp", "zh", "x", "c", "head"),
    )
    token = ("dp", "zh", "x", "c")
    return jax.shard_map(
        on_device,
        mesh=fine,
        in_specs=(
            P(token, "head"),
            P(token, "head"),
            P(token, "head"),
            P(token, None),
            P(token),
            P("dp"),
            P(token, "head", None),
            P(token, "head", None),
            P("head"),
        ),
        out_specs=P(token, "head"),
        check_vma=False,
    )
```

time: 101 us -> 86.7 us (0.86)
  Pallas kernels: 25.3 us -> 11 us
  starting transfers between devices: 48 us -> 42.5 us
  waiting for transfers between devices: 20.3 us -> 23.9 us
  local copies, waits for them, and re-layouts: 2.74 us -> 4.48 us
    pallas_call x2 -> x3, Pallas kernels: 23 us -> 8.72 us  [the longest x1 3.91 us: on_device(): pl.pallas_call(ref_kernel, out_shape=jax.ShapeDtypeStruct((rows, width),...]
    ppermute x4, waiting for transfers between devices: 5.76 us -> 12.3 us  [the longest x1 7.6 us: on_device(): other = lax.ppermute(pooled, 'x', [(i, i ^ 2) for i in range(n_x)])]
    all_to_all x1, waiting for transfers between devices: 12 us -> 6.18 us  [on_device(): spread = lax.all_to_all(mine.reshape(n_x, part, -1), 'x', 0, 0, tiled=True)]
    all_to_all x1, waiting for transfers between devices: 1.2 us -> 5.38 us  [on_device(): lax.all_to_all(piece.reshape(n_zh * n_head, part, width), ('zh', 'head'),...]
    ppermute x1, starting transfers between devices: 7.08 us -> 3.31 us  [on_device(): got = lax.ppermute(own, 'c', SWAP)]
    ppermute x4, starting transfers between devices: 18.3 us -> 16 us  [the longest x1 6.16 us: on_device(): other = lax.ppermute(pooled, 'zh', SWAP)]
    unnamed x14, local copies, waits for them, and re-layouts: 0.83 us -> 2.59 us
    ppermute x1, waiting for transfers between devices: 1.37 us -> 0.01 us  [on_device(): got_k = lax.ppermute(slot_k, 'c', [(1, 0)])]
  transfers between devices with their start and end apart: 10 -> 10, of which waited for: 5 -> 5; matrix products, arithmetic and copies ran while one was open for 2% -> 2% of each run, Pallas kernels for 17% -> 8%
where the time goes in v2:
time: 86.7 us; the launch traced here: 86.1 us
  starting transfers between devices  42.5 us (49%)
  waiting for transfers between devices  23.9 us (28%)
  Pallas kernels  11 us (13%)
  local copies, waits for them, and re-layouts  4.48 us (5%)
  other arithmetic  2.51 us (3%)
  between operations  1.62 us (2%)
    ppermute x1, starting transfers between devices, on_device(): got_k = lax.ppermute(slot_k, 'c', [(1, 0)])  8.88 us
    ppermute x1, waiting for transfers between devices, on_device(): other = lax.ppermute(pooled, 'x', [(i, i ^ 2) for i in range(n_x)])  7.6 us
    all_to_all x1, waiting for transfers between devices, on_device(): spread = lax.all_to_all(mine.reshape(n_x, part, -1), 'x', 0, 0, tiled=True)  6.18 us
    ppermute x1, starting transfers between devices, on_device(): other = lax.ppermute(pooled, 'zh', SWAP)  6.16 us
    all_to_all x1, starting transfers between devices, on_device(): lax.all_to_all(piece.reshape(n_zh * n_head, part, width), ('zh', 'head'),...  5.98 us
    all_to_all x1, waiting for transfers between devices, on_device(): lax.all_to_all(piece.reshape(n_zh * n_head, part, width), ('zh', 'head'),...  5.38 us
    ppermute x1, starting transfers between devices, on_device(): other = lax.ppermute(pooled, 'x', [(i, i ^ 2) for i in range(n_x)])  4.95 us
    pallas_call x1, Pallas kernels, on_device(): pl.pallas_call(ref_kernel, out_shape=jax.ShapeDtypeStruct((rows, width),...  3.91 us
  transfers between devices with their start and end apart: 10, of which 5 were waited for; matrix products, arithmetic and copies ran while one was open for 2% of the time, Pallas kernels for 8%

profile of v2, /device:TPU:1, one launch (start us, length us, event | category | flops | bytes accessed | tf_op | source)
XLA Modules:
  0.0 86.1 jit_solution(14147213923701431939)
XLA Ops:
  0.0 1.3 %collective-permute-start.1 = (bf16[128,3072]{1,0:T(8,128)(2,1)}, bf16[128,3072]{1,0:T(8,128)(2,1)S(1)}, u32[]{:S(2)}, u32[]{:S(2)}) collective-permute-start(bf16[128,3072]{1,0:T(8,128)(2,1)} %bitcast.20), channel_id=1, source_target_pairs={{0,4},{1,5},{2,6},{3,7},{8,12},{9,13},{10,14},{11,15},{16,20},{17,... | collective-permute-start | bytes 2359304 | tf_op jit(solution)/shard_map/ppermute | solution.py:127
  1.3 8.9 %collective-permute-start = (bf16[128,3072]{1,0:T(8,128)(2,1)}, bf16[128,3072]{1,0:T(8,128)(2,1)S(1)}, u32[]{:S(2)}, u32[]{:S(2)}) collective-permute-start(bf16[128,3072]{1,0:T(8,128)(2,1)} %bitcast.21), channel_id=1, source_target_pairs={{4,0},{5,1},{6,2},{7,3},{12,8},{13,9},{14,10},{15,11},{20,16},{21,... | collective-permute-start | bytes 2359304 | tf_op jit(solution)/shard_map/ppermute | solution.py:126
  11.5 1.5 %broadcast_select_fusion = bf16[128,3072]{1,0:T(8,128)(2,1)S(1)} fusion(pred[]{:T(512)S(6)} %eq.11, bf16[1,128,3072]{2,1,0:T(8,128)(2,1)} %param.16, bf16[1,128,3072]{2,1,0:T(8,128)(2,1)} %param.15), kind=kLoop, calls=%fused_computation.1 | loop fusion | flops 393216 | bytes 2359297 | tf_op jit(solution)/shard_map/jit(_where)/select_n | solution.py:128
  12.9 2.3 %pool.1 = bf16[8,1664]{1,0:T(8,128)(2,1)} custom-call(s32[1]{0:T(128)S(6)} %copy.11.tag_ref, s32[1,512]{1,0:T(1,128)} %seg_ref.1, bf16[512,768]{1,0:T(8,128)(2,1)} %k_ref.1, bf16[512,768]{1,0:T(8,128)(2,1)} %v_ref.1), custom_call_target="tpu_custom_call" | custom-call | tf_op jit(solution)/shard_map/pool/pallas_call | solution.py:129
  15.3 1.0 %select_select_fusion = bf16[128,3072]{1,0:T(8,128)(2,1)} fusion(bf16[128,3072]{1,0:T(8,128)(2,1)S(1)} %broadcast_select_fusion, bf16[128,3072]{1,0:T(8,128)(2,1)S(1)} %collective-permute-done, bf16[128,3072]{1,0:T(8,128)(2,1)S(1)} %collective-permute-done.1, pred[]{:T(512)S(6)} %eq.11, pred[]{:T(512)S(6)} %eq.10), kind=kLoop, calls=%fused_computation | loop fusion | flops 786432 | bytes 3145730 | tf_op jit(solution)/shard_map/jit(_where)/select_n | solution.py:136
  16.3 3.6 %all-to-all-start = ((bf16[4,32,3072]{2,1,0:T(8,128)(2,1)}), bf16[4,32,3072]{2,1,0:T(8,128)(2,1)S(1)}, u32[]{:S(2)}, u32[]{:S(2)}) async-start(bf16[4,32,3072]{2,1,0:T(8,128)(2,1)} %bitcast.4), calls=%async_computation | async-start | bytes 1572864 | tf_op jit(solution)/shard_map/all_to_all | solution.py:139
  19.9 6.2 %collective-permute-start.2 = (bf16[8,1664]{1,0:T(8,128)(2,1)S(1)}, bf16[8,1664]{1,0:T(8,128)(2,1)S(1)}, u32[]{:S(2)}, u32[]{:S(2)}) collective-permute-start(bf16[8,1664]{1,0:T(8,128)(2,1)S(1)} %copy-done.6), channel_id=1, source_target_pairs={{0,32},{32,0},{1,33},{33,1},{2,34},{34,2},{3,35},{35,3},{4,36},{36... | collective-permute-start | bytes 79880 | tf_op jit(solution)/shard_map/ppermute | solution.py:140
  26.1 6.2 %all-to-all-done = bf16[4,32,3072]{2,1,0:T(8,128)(2,1)S(1)} async-done(((bf16[4,32,3072]{2,1,0:T(8,128)(2,1)}), bf16[4,32,3072]{2,1,0:T(8,128)(2,1)S(1)}, u32[]{:S(2)}, u32[]{:S(2)}) %all-to-all-start) | async-done | bytes 786464 | tf_op jit(solution)/shard_map/all_to_all | solution.py:139
  32.3 0.1 reshape.18
  32.5 0.0 collective-permute-done.2
  32.5 0.8 broadcast_in_dim.18
  33.3 6.0 %all-to-all-start.1 = ((bf16[8,32,768]{2,1,0:T(8,128)(2,1)}), bf16[8,32,768]{2,1,0:T(8,128)(2,1)S(1)}, u32[]{:S(2)}, u32[]{:S(2)}) async-start(bf16[8,32,768]{2,1,0:T(8,128)(2,1)} %bitcast.6), calls=%async_computation.1 | async-start | bytes 786432 | tf_op jit(solution)/shard_map/all_to_all | solution.py:146
  39.3 2.7 %collective-permute-start.3 = (bf16[16,1664]{1,0:T(8,128)(2,1)S(1)}, bf16[16,1664]{1,0:T(8,128)(2,1)S(1)}, u32[]{:S(2)}, u32[]{:S(2)}) collective-permute-start(bf16[16,1664]{1,0:T(8,128)(2,1)S(1)} %pad_maximum_fusion.3), channel_id=1, source_target_pairs={{0,4},{4,0},{1,5},{5,1},{2,6},{6,2},{3,7},{7,3},{8,12},{12,8},{9,1... | collective-permute-start | bytes 159752 | tf_op jit(solution)/shard_map/ppermute | solution.py:150
  41.9 0.9 %collective-permute-done.3 = bf16[16,1664]{1,0:T(8,128)(2,1)S(1)} collective-permute-done((bf16[16,1664]{1,0:T(8,128)(2,1)S(1)}, bf16[16,1664]{1,0:T(8,128)(2,1)S(1)}, u32[]{:S(2)}, u32[]{:S(2)}) %collective-permute-start.3) | collective-permute-done | bytes 53280 | tf_op jit(solution)/shard_map/ppermute | solution.py:150
  42.8 2.2 %collective-permute-start.4 = (bf16[32,1664]{1,0:T(8,128)(2,1)S(1)}, bf16[32,1664]{1,0:T(8,128)(2,1)S(1)}, u32[]{:S(2)}, u32[]{:S(2)}) collective-permute-start(bf16[32,1664]{1,0:T(8,128)(2,1)S(1)} %pad_maximum_fusion.2), channel_id=1, source_target_pairs={{0,8},{8,0},{16,24},{24,16},{1,9},{9,1},{17,25},{25,17},{2,10},{10... | collective-permute-start | bytes 319496 | tf_op jit(solution)/shard_map/ppermute | solution.py:152
  45.0 3.9 %collective-permute-done.4 = bf16[32,1664]{1,0:T(8,128)(2,1)S(1)} collective-permute-done((bf16[32,1664]{1,0:T(8,128)(2,1)S(1)}, bf16[32,1664]{1,0:T(8,128)(2,1)S(1)}, u32[]{:S(2)}, u32[]{:S(2)}) %collective-permute-start.4) | collective-permute-done | bytes 106528 | tf_op jit(solution)/shard_map/ppermute | solution.py:152
  48.9 0.0 copy-start
  48.9 0.0 copy-start.3
  49.0 0.0 copy-start.4
  49.0 5.4 %all-to-all-done.1 = bf16[8,32,768]{2,1,0:T(8,128)(2,1)S(1)} async-done(((bf16[8,32,768]{2,1,0:T(8,128)(2,1)}), bf16[8,32,768]{2,1,0:T(8,128)(2,1)S(1)}, u32[]{:S(2)}, u32[]{:S(2)}) %all-to-all-start.1) | async-done | bytes 393248 | tf_op jit(solution)/shard_map/all_to_all | solution.py:146
  54.4 0.9 %broadcast_in_dim.20 = bf16[4,128,768]{2,1,0:T(8,128)(2,1)} broadcast(bf16[128,768]{1,0:T(8,128)(2,1)S(1)} %dynamic-slice_bitcast_fusion), dimensions={1,2} | broadcast | bytes 983040 | tf_op jit(solution)/shard_map/broadcast_in_dim | solution.py:156
  55.3 3.5 %all-to-all-start.2 = ((bf16[4,128,768]{2,1,0:T(8,128)(2,1)}), bf16[4,128,768]{2,1,0:T(8,128)(2,1)S(1)}, u32[]{:S(2)}, u32[]{:S(2)}) async-start(bf16[4,128,768]{2,1,0:T(8,128)(2,1)} %broadcast_in_dim.20), calls=%async_computation.2 | async-start | bytes 1572864 | tf_op jit(solution)/shard_map/all_to_all | solution.py:159
  58.8 0.0 copy-start.5
  58.8 5.0 %collective-permute-start.5 = (bf16[64,1664]{1,0:T(8,128)(2,1)S(1)}, bf16[64,1664]{1,0:T(8,128)(2,1)S(1)}, u32[]{:S(2)}, u32[]{:S(2)}) collective-permute-start(bf16[64,1664]{1,0:T(8,128)(2,1)S(1)} %pad_maximum_fusion.1), channel_id=1, source_target_pairs={{0,16},{8,24},{16,0},{24,8},{1,17},{9,25},{17,1},{25,9},{2,18},{10... | collective-permute-start | bytes 638984 | tf_op jit(solution)/shard_map/ppermute | solution.py:160
  63.8 2.6 %window.1 = (f32[768,512]{1,0:T(8,128)S(1)}, f32[16,512]{1,0:T(8,128)S(1)}) custom-call(bf16[512,768]{1,0:T(8,128)(2,1)S(1)} %copy-done, bf16[512,768]{1,0:T(8,128)(2,1)S(1)} %copy-done.3, bf16[512,768]{1,0:T(8,128)(2,1)S(1)} %copy-done.4), custom_call_target="tpu_custom_call" | custom-call | flops 805306368 | bytes 3932160 | tf_op jit(solution)/shard_map/window/pallas_call | solution.py:161
  66.4 1.2 %copy-done.1 = f32[768,512]{1,0:T(8,128)} copy-done((f32[768,512]{1,0:T(8,128)}, f32[768,512]{1,0:T(8,128)S(1)}, u32[]{:S(2)}) %copy-start.1) | copy-done | bytes 1572888
  67.6 7.6 %collective-permute-done.5 = bf16[64,1664]{1,0:T(8,128)(2,1)S(1)} collective-permute-done((bf16[64,1664]{1,0:T(8,128)(2,1)S(1)}, bf16[64,1664]{1,0:T(8,128)(2,1)S(1)}, u32[]{:S(2)}, u32[]{:S(2)}) %collective-permute-start.5) | collective-permute-done | bytes 213024 | tf_op jit(solution)/shard_map/ppermute | solution.py:160
  75.2 0.0 all-to-all-done.2
  75.2 3.3 %collective-permute-start.6 = (bf16[512,768]{1,0:T(8,128)(2,1)S(1)}, bf16[512,768]{1,0:T(8,128)(2,1)S(1)}, u32[]{:S(2)}, u32[]{:S(2)}) collective-permute-start(bf16[512,768]{1,0:T(8,128)(2,1)S(1)} %bitcast.17), channel_id=1, source_target_pairs={{0,4},{4,0},{1,5},{5,1},{2,6},{6,2},{3,7},{7,3},{8,12},{12,8},{9,1... | collective-permute-start | bytes 2359304 | tf_op jit(solution)/shard_map/ppermute | solution.py:177
  78.5 2.2 %pooled.1 = (f32[768,512]{1,0:T(8,128)S(1)}, f32[16,512]{1,0:T(8,128)S(1)}) custom-call(s32[1]{0:T(128)S(6)} %copy.11.tag_ref, f32[6]{0:T(128)S(1)} %copy-done.5, bf16[512,768]{1,0:T(8,128)(2,1)S(1)} %copy-done, bf16[128,1664]{1,0:T(8,128)(2,1)S(1)} %pad_maximum_fusion.p_ref), custom_call_target="tpu_custom_call" | custom-call | flops 201326592 | bytes 2359296 | tf_op jit(solution)/shard_map/pooled/pallas_call | solution.py:178
  80.8 1.4 %copy-done.2 = f32[768,512]{1,0:T(8,128)S(1)} copy-done((f32[768,512]{1,0:T(8,128)S(1)}, f32[768,512]{1,0:T(8,128)}, u32[]{:S(2)}) %copy-start.2) | copy-done | bytes 1572888
  82.2 3.9 %far.1 = bf16[512,768]{1,0:T(8,128)(2,1)} custom-call(s32[1]{0:T(128)} %bitcast.core_ref, bf16[512,768]{1,0:T(8,128)(2,1)S(1)} %copy-done, bf16[512,768]{1,0:T(8,128)(2,1)S(1)} %bitcast.18, bf16[512,768]{1,0:T(8,128)(2,1)S(1)} %collective-permute-done.6.got_ref, f32[768,512]{1,0:T(8,128)S(1)} %copy-done.2, f32[16,512]{1,0:T(8,128)S(1)} %get-tuple-element.33.stat_w_ref, ...), custom_call_target="tpu_custom_call" | custom-call | tf_op jit(solution)/shard_map/far/pallas_call | solution.py:191
  (18 shorter events, 0.1 us)
Async XLA Ops:
  0.0 15.3 %collective-permute-start.1 = (bf16[128,3072]{1,0:T(8,128)(2,1)}, bf16[128,3072]{1,0:T(8,128)(2,1)S(1)}, u32[]{:S(2)}, u32[]{:S(2)}) collective-permute-start(bf16[128,3072]{1,0:T(8,128)(2,1)} %bitcast.20), channel_id=1, source_target_pairs={{0,4},{1,5},{2,6},{3,7},{8,12},{9,13},{10,14},{11,15},{16,20},{17,... | collective-permute-start | bytes 2359304 | tf_op jit(solution)/shard_map/ppermute | solution.py:127
  1.3 14.0 %collective-permute-start = (bf16[128,3072]{1,0:T(8,128)(2,1)}, bf16[128,3072]{1,0:T(8,128)(2,1)S(1)}, u32[]{:S(2)}, u32[]{:S(2)}) collective-permute-start(bf16[128,3072]{1,0:T(8,128)(2,1)} %bitcast.21), channel_id=1, source_target_pairs={{4,0},{5,1},{6,2},{7,3},{12,8},{13,9},{14,10},{15,11},{20,16},{21,... | collective-permute-start | bytes 2359304 | tf_op jit(solution)/shard_map/ppermute | solution.py:126
  16.3 3.7 %copy-start.6 = (bf16[8,1664]{1,0:T(8,128)(2,1)S(1)}, bf16[8,1664]{1,0:T(8,128)(2,1)}, u32[]{:S(2)}) copy-start(bf16[8,1664]{1,0:T(8,128)(2,1)} %pool.1) | copy-start | bytes 79876
  16.3 16.0 %all-to-all-start = ((bf16[4,32,3072]{2,1,0:T(8,128)(2,1)}), bf16[4,32,3072]{2,1,0:T(8,128)(2,1)S(1)}, u32[]{:S(2)}, u32[]{:S(2)}) async-start(bf16[4,32,3072]{2,1,0:T(8,128)(2,1)} %bitcast.4), calls=%async_computation | async-start | bytes 1572864 | tf_op jit(solution)/shard_map/all_to_all | solution.py:139
  19.9 12.5 %collective-permute-start.2 = (bf16[8,1664]{1,0:T(8,128)(2,1)S(1)}, bf16[8,1664]{1,0:T(8,128)(2,1)S(1)}, u32[]{:S(2)}, u32[]{:S(2)}) collective-permute-start(bf16[8,1664]{1,0:T(8,128)(2,1)S(1)} %copy-done.6), channel_id=1, source_target_pairs={{0,32},{32,0},{1,33},{33,1},{2,34},{34,2},{3,35},{35,3},{4,36},{36... | collective-permute-start | bytes 79880 | tf_op jit(solution)/shard_map/ppermute | solution.py:140
  33.3 21.1 %all-to-all-start.1 = ((bf16[8,32,768]{2,1,0:T(8,128)(2,1)}), bf16[8,32,768]{2,1,0:T(8,128)(2,1)S(1)}, u32[]{:S(2)}, u32[]{:S(2)}) async-start(bf16[8,32,768]{2,1,0:T(8,128)(2,1)} %bitcast.6), calls=%async_computation.1 | async-start | bytes 786432 | tf_op jit(solution)/shard_map/all_to_all | solution.py:146
  39.3 3.5 %collective-permute-start.3 = (bf16[16,1664]{1,0:T(8,128)(2,1)S(1)}, bf16[16,1664]{1,0:T(8,128)(2,1)S(1)}, u32[]{:S(2)}, u32[]{:S(2)}) collective-permute-start(bf16[16,1664]{1,0:T(8,128)(2,1)S(1)} %pad_maximum_fusion.3), channel_id=1, source_target_pairs={{0,4},{4,0},{1,5},{5,1},{2,6},{6,2},{3,7},{7,3},{8,12},{12,8},{9,1... | collective-permute-start | bytes 159752 | tf_op jit(solution)/shard_map/ppermute | solution.py:150
  42.8 6.1 %collective-permute-start.4 = (bf16[32,1664]{1,0:T(8,128)(2,1)S(1)}, bf16[32,1664]{1,0:T(8,128)(2,1)S(1)}, u32[]{:S(2)}, u32[]{:S(2)}) collective-permute-start(bf16[32,1664]{1,0:T(8,128)(2,1)S(1)} %pad_maximum_fusion.2), channel_id=1, source_target_pairs={{0,8},{8,0},{16,24},{24,16},{1,9},{9,1},{17,25},{25,17},{2,10},{10... | collective-permute-start | bytes 319496 | tf_op jit(solution)/shard_map/ppermute | solution.py:152
  48.9 14.8 %copy-start = (bf16[512,768]{1,0:T(8,128)(2,1)S(1)}, bf16[512,768]{1,0:T(8,128)(2,1)}, u32[]{:S(2)}) copy-start(bf16[512,768]{1,0:T(8,128)(2,1)} %q_ref.4) | copy-start | bytes 2359300
  48.9 14.8 %copy-start.3 = (bf16[512,768]{1,0:T(8,128)(2,1)S(1)}, bf16[512,768]{1,0:T(8,128)(2,1)}, u32[]{:S(2)}) copy-start(bf16[512,768]{1,0:T(8,128)(2,1)} %k_ref.1) | copy-start | bytes 2359300
  49.0 14.8 %copy-start.4 = (bf16[512,768]{1,0:T(8,128)(2,1)S(1)}, bf16[512,768]{1,0:T(8,128)(2,1)}, u32[]{:S(2)}) copy-start(bf16[512,768]{1,0:T(8,128)(2,1)} %v_ref.1) | copy-start | bytes 2359300
  55.3 19.9 %all-to-all-start.2 = ((bf16[4,128,768]{2,1,0:T(8,128)(2,1)}), bf16[4,128,768]{2,1,0:T(8,128)(2,1)S(1)}, u32[]{:S(2)}, u32[]{:S(2)}) async-start(bf16[4,128,768]{2,1,0:T(8,128)(2,1)} %broadcast_in_dim.20), calls=%async_computation.2 | async-start | bytes 1572864 | tf_op jit(solution)/shard_map/all_to_all | solution.py:159
  58.8 19.7 %copy-start.5 = (f32[6]{0:T(128)S(1)}, f32[6]{0:T(128)}, u32[]{:S(2)}) copy-start(f32[6]{0:T(128)} %slope_ref.1) | copy-start | bytes 76
  58.8 16.4 %collective-permute-start.5 = (bf16[64,1664]{1,0:T(8,128)(2,1)S(1)}, bf16[64,1664]{1,0:T(8,128)(2,1)S(1)}, u32[]{:S(2)}, u32[]{:S(2)}) collective-permute-start(bf16[64,1664]{1,0:T(8,128)(2,1)S(1)} %pad_maximum_fusion.1), channel_id=1, source_target_pairs={{0,16},{8,24},{16,0},{24,8},{1,17},{9,25},{17,1},{25,9},{2,18},{10... | collective-permute-start | bytes 638984 | tf_op jit(solution)/shard_map/ppermute | solution.py:160
  66.4 1.2 %copy-start.1 = (f32[768,512]{1,0:T(8,128)}, f32[768,512]{1,0:T(8,128)S(1)}, u32[]{:S(2)}) copy-start(f32[768,512]{1,0:T(8,128)S(1)} %get-tuple-element.32.acc_w_ref) | copy-start | bytes 4718596
  75.2 5.6 %collective-permute-start.6 = (bf16[512,768]{1,0:T(8,128)(2,1)S(1)}, bf16[512,768]{1,0:T(8,128)(2,1)S(1)}, u32[]{:S(2)}, u32[]{:S(2)}) collective-permute-start(bf16[512,768]{1,0:T(8,128)(2,1)S(1)} %bitcast.17), channel_id=1, source_target_pairs={{0,4},{4,0},{1,5},{5,1},{2,6},{6,2},{3,7},{7,3},{8,12},{12,8},{9,1... | collective-permute-start | bytes 2359304 | tf_op jit(solution)/shard_map/ppermute | solution.py:177
  80.8 1.4 %copy-start.2 = (f32[768,512]{1,0:T(8,128)S(1)}, f32[768,512]{1,0:T(8,128)}, u32[]{:S(2)}) copy-start(f32[768,512]{1,0:T(8,128)} %copy-done.1) | copy-start | bytes 4718596

commit v3 on v2

--- a/solution.py
+++ b/solution.py
@@ -23,16 +23,33 @@
     return jnp.dot(a, b, preferred_element_type=jnp.float32)
 
 
-def pool_kernel(tag_ref, seg_ref, key_ref, value_ref, out_ref):
+def pool_kernel(tag_ref, seg_ref, key_ref, value_ref, out_ref, key_buf, value_buf, sems):
+    rows, width = key_ref.shape
+    pieces = sems.shape[1]
+    step = rows // pieces
+    copies = [
+        [
+            pltpu.make_async_copy(
+                src.at[pl.ds(i * step, step)], buf.at[pl.ds(i * step, step)], sems.at[j, i]
+            )
+            for i in range(pieces)
+        ]
+        for j, (src, buf) in enumerate(((key_ref, key_buf), (value_ref, value_buf)))
+    ]
+    for line in copies:
+        for copy in line:
+            copy.start()
     seg = seg_ref[...]
-    member = seg == lax.broadcasted_iota(jnp.int32, (POOLS, seg.shape[1]), 0)
+    member = seg == lax.broadcasted_iota(jnp.int32, (POOLS, rows), 0)
     count = jnp.sum(member.astype(jnp.float32), axis=1, keepdims=True)
     member = member.astype(jnp.float32).astype(jnp.bfloat16)
-    width = key_ref.shape[1]
-    out_ref[:, :width] = (dot_nn(member, key_ref[...]) / count).astype(jnp.bfloat16)
-    out_ref[:, width : 2 * width] = (dot_nn(member, value_ref[...]) / count).astype(jnp.bfloat16)
     tag = jnp.full((POOLS, HD), tag_ref[0], jnp.int32)
     out_ref[:, 2 * width :] = tag.astype(jnp.float32).astype(jnp.bfloat16)
+    for j, buf in enumerate((key_buf, value_buf)):
+        for copy in copies[j]:
+            copy.wait()
+        mean = dot_nn(member, buf[...]) / count
+        out_ref[:, j * width : (j + 1) * width] = mean.astype(jnp.bfloat16)
 
 
 def soft(scores):
@@ -41,41 +58,75 @@
     return top, jnp.sum(exp_terms, axis=0, keepdims=True), exp_terms.astype(jnp.bfloat16)
 
 
-def window_kernel(q_ref, k_ref, v_ref, acc_ref, stat_ref):
+def window_kernel(q_ref, k_ref, v_ref, acc_ref, stat_ref, buf, sems):
+    copies = []
     for head in range(q_ref.shape[1] // HD):
         cols = pl.ds(head * HD, HD)
         values = v_ref[:, cols].T
         for start in range(0, q_ref.shape[0], STRIP):
             rows = pl.ds(start, STRIP)
             top, total, weights = soft(dot_nt(k_ref[:, cols], q_ref[rows, cols]) * UNIT)
-            acc_ref[cols, rows] = dot_nn(values, weights)
+            buf[cols, rows] = dot_nn(values, weights)
             stat_ref[2 * head : 2 * head + 1, rows] = top
             stat_ref[2 * head + 1 : 2 * head + 2, rows] = total
-
-
-def pooled_kernel(tag_ref, slope_ref, q_ref, p_ref, acc_ref, stat_ref):
+        copies.append(pltpu.make_async_copy(buf.at[cols], acc_ref.at[cols], sems.at[head]))
+        copies[-1].start()
+    for copy in copies:
+        copy.wait()
+
+
+def pooled_kernel(tag_ref, slope_ref, q_ref, p_ref, acc_ref, stat_ref, buf, sems):
     count, width = q_ref.shape
     tags = p_ref[:, 2 * width :].astype(jnp.float32)
     dist = jnp.abs(tags - tag_ref[0].astype(jnp.float32)) * LOG2E
     dist = jnp.concatenate([dist] * (count // HD), axis=1)
+    copies = []
     for head in range(width // HD):
         cols = pl.ds(head * HD, HD)
         scores = dot_nt(p_ref[:, cols], q_ref[:, cols]) * UNIT - dist * slope_ref[head]
         top, total, weights = soft(scores)
-        acc_ref[cols, :] = dot_nn(p_ref[:, pl.ds(width + head * HD, HD)].T, weights)
+        buf[cols, :] = dot_nn(p_ref[:, pl.ds(width + head * HD, HD)].T, weights)
         stat_ref[2 * head : 2 * head + 1, :] = top
         stat_ref[2 * head + 1 : 2 * head + 2, :] = total
+        copies.append(pltpu.make_async_copy(buf.at[cols], acc_ref.at[cols], sems.at[head]))
+        copies[-1].start()
+    for copy in copies:
+        copy.wait()
 
 
 def ref_kernel(
-    core_ref, q_ref, own_ref, got_ref, acc_w_ref, stat_w_ref, acc_p_ref, stat_p_ref, out_ref
+    core_ref,
+    q_ref,
+    own_ref,
+    got_ref,
+    acc_w_ref,
+    stat_w_ref,
+    acc_p_ref,
+    stat_p_ref,
+    out_ref,
+    buf_w,
+    buf_p,
+    buf_out,
+    sems,
 ):
     first = core_ref[0] == 0
-    for head in range(q_ref.shape[1] // HD):
-        cols = pl.ds(head * HD, HD)
+    all_cols = [pl.ds(head * HD, HD) for head in range(q_ref.shape[1] // HD)]
+    fetch, store = [], []
+    for head, cols in enumerate(all_cols):
+        fetch.append(
+            (
+                pltpu.make_async_copy(acc_w_ref.at[cols], buf_w.at[cols], sems.at[0, head]),
+                pltpu.make_async_copy(acc_p_ref.at[cols], buf_p.at[cols], sems.at[1, head]),
+            )
+        )
+        for copy in fetch[-1]:
+            copy.start()
+    for head, cols in enumerate(all_cols):
         top_at, total_at = slice(2 * head, 2 * head + 1), slice(2 * head + 1, 2 * head + 2)
         keys = jnp.where(first, own_ref[:, cols], got_ref[:, cols])
         values = jnp.where(first, got_ref[:, cols], own_ref[:, cols]).T
+        for copy in fetch[head]:
+            copy.wait()
         for start in range(0, q_ref.shape[0], STRIP):
             rows = pl.ds(start, STRIP)
             top, total, weights = soft(dot_nt(keys, q_ref[rows, cols]) * UNIT)
@@ -90,15 +141,23 @@
                 + share * total
             )
             merged = (
-                (share_w * scale) * acc_w_ref[cols, rows]
-                + (share_p * scale) * acc_p_ref[cols, rows]
+                (share_w * scale) * buf_w[cols, rows]
+                + (share_p * scale) * buf_p[cols, rows]
                 + (share * scale) * num
             )
-            out_ref[rows, cols] = merged.astype(jnp.bfloat16).T
+            buf_out[rows, cols] = merged.astype(jnp.bfloat16).T
+        store.append(
+            pltpu.make_async_copy(buf_out.at[:, cols], out_ref.at[:, cols], sems.at[2, head])
+        )
+        store[-1].start()
+    for copy in store:
+        copy.wait()
 
 
 SMEM = pl.BlockSpec(memory_space=pltpu.SMEM)
 VMEM = pl.BlockSpec(memory_space=pltpu.VMEM)
+HBM = pl.BlockSpec(memory_space=pltpu.HBM)
+DMA = pltpu.SemaphoreType.DMA
 
 
 def on_device(
@@ -129,8 +188,14 @@
     pooled = pl.pallas_call(
         pool_kernel,
         out_shape=jax.ShapeDtypeStruct((POOLS, 2 * width + HD), jnp.bfloat16),
-        in_specs=[SMEM, VMEM, VMEM, VMEM],
+        in_specs=[SMEM, VMEM, HBM, HBM],
         out_specs=VMEM,
+        scratch_shapes=[
+            pltpu.VMEM((rows, width), jnp.bfloat16),
+            pltpu.VMEM((rows, width), jnp.bfloat16),
+            DMA((2, 4)),
+        ],
+        compiler_params=near,
         name="pool",
     )(window_map, pool_segments, keys, values)
     mine = jnp.where(owner_c == core, kept, jnp.where(core == 0, got_k, got_v))
@@ -147,22 +212,24 @@
         piece.reshape(n_zh * n_head, part, width), ("zh", "head"), 0, 0, tiled=True
     )
     pooled = jnp.concatenate([pooled, other], axis=0)
-    other = lax.ppermute(pooled, "c", SWAP)
-    pooled = jnp.concatenate([pooled, other], axis=0)
     other = lax.ppermute(pooled, "x", [(i, i ^ 1) for i in range(n_x)])
     pooled = jnp.concatenate([pooled, other], axis=0)
+    other = lax.ppermute(pooled, "x", [(i, i ^ 2) for i in range(n_x)])
     turned = turned.reshape(n_zh, n_head * part, width)
     block = lax.dynamic_index_in_dim(turned, owner_z, 0, keepdims=False)
     block = jnp.broadcast_to(block[None], (n_x, n_head * part, width))
-    block, pooled, queries_w = tie((block, pooled, queries))
+    block, pooled, other, queries_w = tie((block, pooled, other, queries))
 
     own = lax.all_to_all(block, "x", 0, 0, tiled=True).reshape(-1, width)
-    other = lax.ppermute(pooled, "x", [(i, i ^ 2) for i in range(n_x)])
+    pooled = jnp.concatenate([pooled, other], axis=0)
+    other = lax.ppermute(pooled, "c", SWAP)
+    scratch = [pltpu.VMEM((width, rows), jnp.float32), DMA((heads,))]
     acc_w, stat_w = pl.pallas_call(
         window_kernel,
         out_shape=state,
         in_specs=[VMEM] * 3,
-        out_specs=(VMEM, VMEM),
+        out_specs=(HBM, VMEM),
+        scratch_shapes=scratch,
         compiler_params=near,
         cost_estimate=pl.CostEstimate(
             flops=4 * rows * rows * width,
@@ -172,14 +239,12 @@
         name="window",
     )(queries_w, keys, values)
     pooled = jnp.concatenate([pooled, other], axis=0)
-    own, pooled, acc_w, stat_w = tie((own, pooled, acc_w, stat_w))
-
-    got = lax.ppermute(own, "c", SWAP)
     acc_p, stat_p = pl.pallas_call(
         pooled_kernel,
         out_shape=state,
         in_specs=[SMEM, SMEM, VMEM, VMEM],
-        out_specs=(VMEM, VMEM),
+        out_specs=(HBM, VMEM),
+        scratch_shapes=scratch,
         compiler_params=near,
         cost_estimate=pl.CostEstimate(
             flops=4 * rows * pooled.shape[0] * width,
@@ -187,12 +252,21 @@
             transcendentals=rows * pooled.shape[0] * heads,
         ),
         name="pooled",
-    )(window_map, slopes, queries, pooled)
+    )(window_map, slopes, queries_w, pooled)
+    own, stat_w, stat_p = tie((own, stat_w, stat_p))
+
+    got = lax.ppermute(own, "c", SWAP)
     return pl.pallas_call(
         ref_kernel,
         out_shape=jax.ShapeDtypeStruct((rows, width), jnp.bfloat16),
-        in_specs=[SMEM] + [VMEM] * 7,
-        out_specs=VMEM,
+        in_specs=[SMEM] + [VMEM] * 3 + [HBM, VMEM, HBM, VMEM],
+        out_specs=HBM,
+        scratch_shapes=[
+            pltpu.VMEM((width, rows), jnp.float32),
+            pltpu.VMEM((width, rows), jnp.float32),
+            pltpu.VMEM((rows, width), jnp.bfloat16),
+            DMA((3, heads)),
+        ],
         compiler_params=near,
         name="far",
     )(core.astype(jnp.int32)[None], queries, own, got, acc_w, stat_w, acc_p, stat_p)

time: 86.7 us -> 85.1 us (0.982)
  Pallas kernels: 11 us -> 16.3 us
  waiting for transfers between devices: 23.9 us -> 18.8 us
  starting transfers between devices: 42.5 us -> 38.5 us
  local copies, waits for them, and re-layouts: 4.48 us -> 6.76 us
    ppermute x1, waiting for transfers between devices: 7.6 us -> 0.01 us  [on_device(): other = lax.ppermute(pooled, 'x', [(i, i ^ 2) for i in range(n_x)])]
    ppermute x1, starting transfers between devices: 4.95 us -> 2.51 us  [on_device(): other = lax.ppermute(pooled, 'x', [(i, i ^ 2) for i in range(n_x)])]
    unnamed x14 -> x20, local copies, waits for them, and re-layouts: 2.59 us -> 4.86 us
    ppermute x1, waiting for transfers between devices: 0.01 us -> 2.25 us  [on_device(): got = lax.ppermute(own, 'c', SWAP)]
    pallas_call x1, Pallas kernels: 3.91 us -> 6 us  [on_device(): pl.pallas_call(ref_kernel, out_shape=jax.ShapeDtypeStruct((rows, width),...]
    all_to_all x1, waiting for transfers between devices: 5.38 us -> 7.38 us  [on_device(): lax.all_to_all(piece.reshape(n_zh * n_head, part, width), ('zh', 'head'),...]
    pallas_call x1, Pallas kernels: 2.58 us -> 4.43 us  [on_device(): pl.pallas_call(window_kernel, out_shape=state, in_specs=[VMEM] * 3, out_s...]
    ppermute x1, starting transfers between devices: 3.31 us -> 1.91 us  [on_device(): got = lax.ppermute(own, 'c', SWAP)]
  transfers between devices with their start and end apart: 10 -> 10, of which waited for: 5 -> 4; matrix products, arithmetic and copies ran while one was open for 2% -> 2% of each run, Pallas kernels for 8% -> 12%
where the time goes in v3:
time: 85.1 us; the launch traced here: 84.4 us
  starting transfers between devices  38.5 us (45%)
  waiting for transfers between devices  18.8 us (22%)
  Pallas kernels  16.3 us (19%)
  local copies, waits for them, and re-layouts  6.76 us (8%)
  other arithmetic  2.5 us (3%)
  between operations  1.64 us (2%)
    ppermute x1, starting transfers between devices, on_device(): got_k = lax.ppermute(slot_k, 'c', [(1, 0)])  8.86 us
    all_to_all x1, waiting for transfers between devices, on_device(): lax.all_to_all(piece.reshape(n_zh * n_head, part, width), ('zh', 'head'),...  7.38 us
    all_to_all x1, waiting for transfers between devices, on_device(): spread = lax.all_to_all(mine.reshape(n_x, part, -1), 'x', 0, 0, tiled=True)  6.17 us
    ppermute x1, starting transfers between devices, on_device(): other = lax.ppermute(pooled, 'zh', SWAP)  6.17 us
    pallas_call x1, Pallas kernels, on_device(): pl.pallas_call(ref_kernel, out_shape=jax.ShapeDtypeStruct((rows, width),...  6 us
    all_to_all x1, starting transfers between devices, on_device(): lax.all_to_all(piece.reshape(n_zh * n_head, part, width), ('zh', 'head'),...  5.99 us
    unnamed x20, local copies, waits for them, and re-layouts  4.86 us
    pallas_call x1, Pallas kernels, on_device(): pl.pallas_call(window_kernel, out_shape=state, in_specs=[VMEM] * 3, out_s...  4.43 us
  transfers between devices with their start and end apart: 10, of which 4 were waited for; matrix products, arithmetic and copies ran while one was open for 2% of the time, Pallas kernels for 12%

profile of v3, /device:TPU:1, one launch (start us, length us, event | category | flops | bytes accessed | tf_op | source)
XLA Modules:
  0.0 84.4 jit_solution(693488348220569637)
XLA Ops:
  0.0 1.4 %collective-permute-start.1 = (bf16[128,3072]{1,0:T(8,128)(2,1)}, bf16[128,3072]{1,0:T(8,128)(2,1)S(1)}, u32[]{:S(2)}, u32[]{:S(2)}) collective-permute-start(bf16[128,3072]{1,0:T(8,128)(2,1)} %bitcast.20), channel_id=1, source_target_pairs={{0,4},{1,5},{2,6},{3,7},{8,12},{9,13},{10,14},{11,15},{16,20},{17,... | collective-permute-start | bytes 2359304 | tf_op jit(solution)/shard_map/ppermute | solution.py:186
  1.4 8.9 %collective-permute-start = (bf16[128,3072]{1,0:T(8,128)(2,1)}, bf16[128,3072]{1,0:T(8,128)(2,1)S(1)}, u32[]{:S(2)}, u32[]{:S(2)}) collective-permute-start(bf16[128,3072]{1,0:T(8,128)(2,1)} %bitcast.21), channel_id=1, source_target_pairs={{4,0},{5,1},{6,2},{7,3},{12,8},{13,9},{14,10},{15,11},{20,16},{21,... | collective-permute-start | bytes 2359304 | tf_op jit(solution)/shard_map/ppermute | solution.py:185
  11.6 1.5 %broadcast_select_fusion = bf16[128,3072]{1,0:T(8,128)(2,1)S(1)} fusion(pred[]{:T(512)S(6)} %eq.11, bf16[1,128,3072]{2,1,0:T(8,128)(2,1)} %param.16, bf16[1,128,3072]{2,1,0:T(8,128)(2,1)} %param.15), kind=kLoop, calls=%fused_computation.1 | loop fusion | flops 393216 | bytes 2359297 | tf_op jit(solution)/shard_map/jit(_where)/select_n | solution.py:187
  13.1 2.7 %pool.1 = bf16[8,1664]{1,0:T(8,128)(2,1)S(1)} custom-call(s32[1]{0:T(128)S(6)} %copy.13.tag_ref, s32[1,512]{1,0:T(1,128)S(1)} %copy-done.7, bf16[512,768]{1,0:T(8,128)(2,1)S(1)} %copy-done.3, bf16[512,768]{1,0:T(8,128)(2,1)S(1)} %copy-done.5), custom_call_target="tpu_custom_call" | custom-call | tf_op jit(solution)/shard_map/pool/pallas_call | solution.py:188
  15.8 0.0 collective-permute-done.1
  15.8 1.0 %select_select_fusion = bf16[128,3072]{1,0:T(8,128)(2,1)} fusion(bf16[128,3072]{1,0:T(8,128)(2,1)S(1)} %broadcast_select_fusion, bf16[128,3072]{1,0:T(8,128)(2,1)S(1)} %collective-permute-done, bf16[128,3072]{1,0:T(8,128)(2,1)S(1)} %collective-permute-done.1, pred[]{:T(512)S(6)} %eq.11, pred[]{:T(512)S(6)} %eq.10), kind=kLoop, calls=%fused_computation | loop fusion | flops 786432 | bytes 3145730 | tf_op jit(solution)/shard_map/jit(_where)/select_n | solution.py:201
  16.8 3.5 %all-to-all-start = ((bf16[4,32,3072]{2,1,0:T(8,128)(2,1)}), bf16[4,32,3072]{2,1,0:T(8,128)(2,1)S(1)}, u32[]{:S(2)}, u32[]{:S(2)}) async-start(bf16[4,32,3072]{2,1,0:T(8,128)(2,1)} %bitcast.4), calls=%async_computation | async-start | bytes 1572864 | tf_op jit(solution)/shard_map/all_to_all | solution.py:204
  20.4 6.2 %collective-permute-start.2 = (bf16[8,1664]{1,0:T(8,128)(2,1)S(1)}, bf16[8,1664]{1,0:T(8,128)(2,1)S(1)}, u32[]{:S(2)}, u32[]{:S(2)}) collective-permute-start(bf16[8,1664]{1,0:T(8,128)(2,1)S(1)} %pool.1), channel_id=1, source_target_pairs={{0,32},{32,0},{1,33},{33,1},{2,34},{34,2},{3,35},{35,3},{4,36},{36... | collective-permute-start | bytes 79880 | tf_op jit(solution)/shard_map/ppermute | solution.py:205
  26.6 6.2 %all-to-all-done = bf16[4,32,3072]{2,1,0:T(8,128)(2,1)S(1)} async-done(((bf16[4,32,3072]{2,1,0:T(8,128)(2,1)}), bf16[4,32,3072]{2,1,0:T(8,128)(2,1)S(1)}, u32[]{:S(2)}, u32[]{:S(2)}) %all-to-all-start) | async-done | bytes 786464 | tf_op jit(solution)/shard_map/all_to_all | solution.py:204
  32.8 0.1 reshape.18
  32.9 0.0 collective-permute-done.2
  32.9 0.8 broadcast_in_dim.18
  33.7 6.0 %all-to-all-start.1 = ((bf16[8,32,768]{2,1,0:T(8,128)(2,1)}), bf16[8,32,768]{2,1,0:T(8,128)(2,1)S(1)}, u32[]{:S(2)}, u32[]{:S(2)}) async-start(bf16[8,32,768]{2,1,0:T(8,128)(2,1)} %bitcast.6), calls=%async_computation.1 | async-start | bytes 786432 | tf_op jit(solution)/shard_map/all_to_all | solution.py:211
  39.7 2.2 %collective-permute-start.3 = (bf16[16,1664]{1,0:T(8,128)(2,1)S(1)}, bf16[16,1664]{1,0:T(8,128)(2,1)S(1)}, u32[]{:S(2)}, u32[]{:S(2)}) collective-permute-start(bf16[16,1664]{1,0:T(8,128)(2,1)S(1)} %pad_maximum_fusion.2), channel_id=1, source_target_pairs={{0,8},{8,0},{16,24},{24,16},{1,9},{9,1},{17,25},{25,17},{2,10},{10... | collective-permute-start | bytes 159752 | tf_op jit(solution)/shard_map/ppermute | solution.py:215
  41.9 2.9 %collective-permute-done.3 = bf16[16,1664]{1,0:T(8,128)(2,1)S(1)} collective-permute-done((bf16[16,1664]{1,0:T(8,128)(2,1)S(1)}, bf16[16,1664]{1,0:T(8,128)(2,1)S(1)}, u32[]{:S(2)}, u32[]{:S(2)}) %collective-permute-start.3) | collective-permute-done | bytes 53280 | tf_op jit(solution)/shard_map/ppermute | solution.py:215
  44.9 2.5 %collective-permute-start.4 = (bf16[32,1664]{1,0:T(8,128)(2,1)S(1)}, bf16[32,1664]{1,0:T(8,128)(2,1)S(1)}, u32[]{:S(2)}, u32[]{:S(2)}) collective-permute-start(bf16[32,1664]{1,0:T(8,128)(2,1)S(1)} %constant_dynamic-update-slice_fusion), channel_id=1, source_target_pairs={{0,16},{8,24},{16,0},{24,8},{1,17},{9,25},{17,1},{25,9},{2,18},{10... | collective-permute-start | bytes 319496 | tf_op jit(solution)/shard_map/ppermute | solution.py:217
  47.4 7.4 %all-to-all-done.1 = bf16[8,32,768]{2,1,0:T(8,128)(2,1)S(1)} async-done(((bf16[8,32,768]{2,1,0:T(8,128)(2,1)}), bf16[8,32,768]{2,1,0:T(8,128)(2,1)S(1)}, u32[]{:S(2)}, u32[]{:S(2)}) %all-to-all-start.1) | async-done | bytes 393248 | tf_op jit(solution)/shard_map/all_to_all | solution.py:211
  54.8 0.0 copy-start
  54.8 0.0 collective-permute-done.4
  54.8 0.9 %broadcast_in_dim.20 = bf16[4,128,768]{2,1,0:T(8,128)(2,1)} broadcast(bf16[128,768]{1,0:T(8,128)(2,1)S(1)} %dynamic-slice_bitcast_fusion), dimensions={1,2} | broadcast | bytes 983040 | tf_op jit(solution)/shard_map/broadcast_in_dim | solution.py:220
  55.8 3.5 %all-to-all-start.2 = ((bf16[4,128,768]{2,1,0:T(8,128)(2,1)}), bf16[4,128,768]{2,1,0:T(8,128)(2,1)S(1)}, u32[]{:S(2)}, u32[]{:S(2)}) async-start(bf16[4,128,768]{2,1,0:T(8,128)(2,1)} %broadcast_in_dim.20), calls=%async_computation.2 | async-start | bytes 1572864 | tf_op jit(solution)/shard_map/all_to_all | solution.py:223
  59.3 2.5 %collective-permute-start.5 = (bf16[64,1664]{1,0:T(8,128)(2,1)S(1)}, bf16[64,1664]{1,0:T(8,128)(2,1)S(1)}, u32[]{:S(2)}, u32[]{:S(2)}) collective-permute-start(bf16[64,1664]{1,0:T(8,128)(2,1)S(1)} %pad_maximum_fusion.1), channel_id=1, source_target_pairs={{0,4},{4,0},{1,5},{5,1},{2,6},{6,2},{3,7},{7,3},{8,12},{12,8},{9,1... | collective-permute-start | bytes 638984 | tf_op jit(solution)/shard_map/ppermute | solution.py:225
  61.8 0.0 copy-start.4
  61.8 1.1 %copy-done.4 = bf16[512,768]{1,0:T(8,128)(2,1)S(1)} copy-done((bf16[512,768]{1,0:T(8,128)(2,1)S(1)}, bf16[512,768]{1,0:T(8,128)(2,1)}, u32[]{:S(2)}) %copy-start.4) | copy-done | bytes 786456
  62.9 1.1 %copy-done.6 = bf16[512,768]{1,0:T(8,128)(2,1)S(1)} copy-done((bf16[512,768]{1,0:T(8,128)(2,1)S(1)}, bf16[512,768]{1,0:T(8,128)(2,1)}, u32[]{:S(2)}) %copy-start.6) | copy-done | bytes 786456
  64.0 4.4 %window.1 = (f32[768,512]{1,0:T(8,128)S(1)}, f32[16,512]{1,0:T(8,128)S(1)}) custom-call(bf16[512,768]{1,0:T(8,128)(2,1)S(1)} %copy-done, bf16[512,768]{1,0:T(8,128)(2,1)S(1)} %copy-done.4, bf16[512,768]{1,0:T(8,128)(2,1)S(1)} %copy-done.6), custom_call_target="tpu_custom_call" | custom-call | flops 805306368 | bytes 3932160 | tf_op jit(solution)/shard_map/window/pallas_call | solution.py:227
  68.5 3.1 %pooled.1 = (f32[768,512]{1,0:T(8,128)S(1)}, f32[16,512]{1,0:T(8,128)S(1)}) custom-call(s32[1]{0:T(128)S(6)} %copy.13.tag_ref, f32[6]{0:T(128)S(1)} %copy-done.8, bf16[512,768]{1,0:T(8,128)(2,1)S(1)} %copy-done, bf16[128,1664]{1,0:T(8,128)(2,1)S(1)} %pad_maximum_fusion.p_ref), custom_call_target="tpu_custom_call" | custom-call | flops 201326592 | bytes 2359296 | tf_op jit(solution)/shard_map/pooled/pallas_call | solution.py:242
  71.7 1.2 %copy-done.1 = f32[768,512]{1,0:T(8,128)} copy-done((f32[768,512]{1,0:T(8,128)}, f32[768,512]{1,0:T(8,128)S(1)}, u32[]{:S(2)}) %copy-start.1) | copy-done | bytes 1572888
  72.8 1.9 %collective-permute-start.6 = (bf16[512,768]{1,0:T(8,128)(2,1)S(1)}, bf16[512,768]{1,0:T(8,128)(2,1)S(1)}, u32[]{:S(2)}, u32[]{:S(2)}) collective-permute-start(bf16[512,768]{1,0:T(8,128)(2,1)S(1)} %bitcast.17), channel_id=1, source_target_pairs={{0,4},{4,0},{1,5},{5,1},{2,6},{6,2},{3,7},{7,3},{8,12},{12,8},{9,1... | collective-permute-start | bytes 2359304 | tf_op jit(solution)/shard_map/ppermute | solution.py:258
  74.8 2.2 %collective-permute-done.6.got_ref = bf16[512,768]{1,0:T(8,128)(2,1)S(1)} collective-permute-done((bf16[512,768]{1,0:T(8,128)(2,1)S(1)}, bf16[512,768]{1,0:T(8,128)(2,1)S(1)}, u32[]{:S(2)}, u32[]{:S(2)}) %collective-permute-start.6) | collective-permute-done | bytes 786464 | tf_op jit(solution)/shard_map/ppermute | solution.py:258
  77.0 1.4 %copy-done.2 = f32[768,512]{1,0:T(8,128)S(1)} copy-done((f32[768,512]{1,0:T(8,128)S(1)}, f32[768,512]{1,0:T(8,128)}, u32[]{:S(2)}) %copy-start.2) | copy-done | bytes 1572888
  78.4 6.0 %far.1 = bf16[512,768]{1,0:T(8,128)(2,1)} custom-call(s32[1]{0:T(128)} %bitcast.core_ref, bf16[512,768]{1,0:T(8,128)(2,1)S(1)} %copy-done, bf16[512,768]{1,0:T(8,128)(2,1)S(1)} %bitcast.18, bf16[512,768]{1,0:T(8,128)(2,1)S(1)} %collective-permute-done.6.got_ref, f32[768,512]{1,0:T(8,128)S(1)} %get-tuple-element.33.acc_w_ref, ...), custom_call_target="tpu_custom_call" | custom-call | tf_op jit(solution)/shard_map/far/pallas_call | solution.py:259
  (24 shorter events, 0.2 us)
Async XLA Ops:
  0.0 13.1 %copy-start.5 = (bf16[512,768]{1,0:T(8,128)(2,1)S(1)}, bf16[512,768]{1,0:T(8,128)(2,1)}, u32[]{:S(2)}) copy-start(bf16[512,768]{1,0:T(8,128)(2,1)} %v_ref.1) | copy-start | bytes 2359300
  0.0 13.1 %copy-start.3 = (bf16[512,768]{1,0:T(8,128)(2,1)S(1)}, bf16[512,768]{1,0:T(8,128)(2,1)}, u32[]{:S(2)}) copy-start(bf16[512,768]{1,0:T(8,128)(2,1)} %k_ref.1) | copy-start | bytes 2359300
  0.0 13.1 %copy-start.7 = (s32[1,512]{1,0:T(1,128)S(1)}, s32[1,512]{1,0:T(1,128)}, u32[]{:S(2)}) copy-start(s32[1,512]{1,0:T(1,128)} %seg_ref.1) | copy-start | bytes 6148
  0.0 15.8 %collective-permute-start.1 = (bf16[128,3072]{1,0:T(8,128)(2,1)}, bf16[128,3072]{1,0:T(8,128)(2,1)S(1)}, u32[]{:S(2)}, u32[]{:S(2)}) collective-permute-start(bf16[128,3072]{1,0:T(8,128)(2,1)} %bitcast.20), channel_id=1, source_target_pairs={{0,4},{1,5},{2,6},{3,7},{8,12},{9,13},{10,14},{11,15},{16,20},{17,... | collective-permute-start | bytes 2359304 | tf_op jit(solution)/shard_map/ppermute | solution.py:186
  1.4 14.4 %collective-permute-start = (bf16[128,3072]{1,0:T(8,128)(2,1)}, bf16[128,3072]{1,0:T(8,128)(2,1)S(1)}, u32[]{:S(2)}, u32[]{:S(2)}) collective-permute-start(bf16[128,3072]{1,0:T(8,128)(2,1)} %bitcast.21), channel_id=1, source_target_pairs={{4,0},{5,1},{6,2},{7,3},{12,8},{13,9},{14,10},{15,11},{20,16},{21,... | collective-permute-start | bytes 2359304 | tf_op jit(solution)/shard_map/ppermute | solution.py:185
  16.8 15.9 %all-to-all-start = ((bf16[4,32,3072]{2,1,0:T(8,128)(2,1)}), bf16[4,32,3072]{2,1,0:T(8,128)(2,1)S(1)}, u32[]{:S(2)}, u32[]{:S(2)}) async-start(bf16[4,32,3072]{2,1,0:T(8,128)(2,1)} %bitcast.4), calls=%async_computation | async-start | bytes 1572864 | tf_op jit(solution)/shard_map/all_to_all | solution.py:204
  20.4 12.5 %collective-permute-start.2 = (bf16[8,1664]{1,0:T(8,128)(2,1)S(1)}, bf16[8,1664]{1,0:T(8,128)(2,1)S(1)}, u32[]{:S(2)}, u32[]{:S(2)}) collective-permute-start(bf16[8,1664]{1,0:T(8,128)(2,1)S(1)} %pool.1), channel_id=1, source_target_pairs={{0,32},{32,0},{1,33},{33,1},{2,34},{34,2},{3,35},{35,3},{4,36},{36... | collective-permute-start | bytes 79880 | tf_op jit(solution)/shard_map/ppermute | solution.py:205
  33.7 21.1 %all-to-all-start.1 = ((bf16[8,32,768]{2,1,0:T(8,128)(2,1)}), bf16[8,32,768]{2,1,0:T(8,128)(2,1)S(1)}, u32[]{:S(2)}, u32[]{:S(2)}) async-start(bf16[8,32,768]{2,1,0:T(8,128)(2,1)} %bitcast.6), calls=%async_computation.1 | async-start | bytes 786432 | tf_op jit(solution)/shard_map/all_to_all | solution.py:211
  39.7 5.2 %collective-permute-start.3 = (bf16[16,1664]{1,0:T(8,128)(2,1)S(1)}, bf16[16,1664]{1,0:T(8,128)(2,1)S(1)}, u32[]{:S(2)}, u32[]{:S(2)}) collective-permute-start(bf16[16,1664]{1,0:T(8,128)(2,1)S(1)} %pad_maximum_fusion.2), channel_id=1, source_target_pairs={{0,8},{8,0},{16,24},{24,16},{1,9},{9,1},{17,25},{25,17},{2,10},{10... | collective-permute-start | bytes 159752 | tf_op jit(solution)/shard_map/ppermute | solution.py:215
  44.9 9.9 %collective-permute-start.4 = (bf16[32,1664]{1,0:T(8,128)(2,1)S(1)}, bf16[32,1664]{1,0:T(8,128)(2,1)S(1)}, u32[]{:S(2)}, u32[]{:S(2)}) collective-permute-start(bf16[32,1664]{1,0:T(8,128)(2,1)S(1)} %constant_dynamic-update-slice_fusion), channel_id=1, source_target_pairs={{0,16},{8,24},{16,0},{24,8},{1,17},{9,25},{17,1},{25,9},{2,18},{10... | collective-permute-start | bytes 319496 | tf_op jit(solution)/shard_map/ppermute | solution.py:217
  54.8 6.9 %copy-start = (bf16[512,768]{1,0:T(8,128)(2,1)S(1)}, bf16[512,768]{1,0:T(8,128)(2,1)}, u32[]{:S(2)}) copy-start(bf16[512,768]{1,0:T(8,128)(2,1)} %q_ref.3) | copy-start | bytes 2359300
  55.8 17.1 %all-to-all-start.2 = ((bf16[4,128,768]{2,1,0:T(8,128)(2,1)}), bf16[4,128,768]{2,1,0:T(8,128)(2,1)S(1)}, u32[]{:S(2)}, u32[]{:S(2)}) async-start(bf16[4,128,768]{2,1,0:T(8,128)(2,1)} %broadcast_in_dim.20), calls=%async_computation.2 | async-start | bytes 1572864 | tf_op jit(solution)/shard_map/all_to_all | solution.py:223
  59.3 9.2 %collective-permute-start.5 = (bf16[64,1664]{1,0:T(8,128)(2,1)S(1)}, bf16[64,1664]{1,0:T(8,128)(2,1)S(1)}, u32[]{:S(2)}, u32[]{:S(2)}) collective-permute-start(bf16[64,1664]{1,0:T(8,128)(2,1)S(1)} %pad_maximum_fusion.1), channel_id=1, source_target_pairs={{0,4},{4,0},{1,5},{5,1},{2,6},{6,2},{3,7},{7,3},{8,12},{12,8},{9,1... | collective-permute-start | bytes 638984 | tf_op jit(solution)/shard_map/ppermute | solution.py:225
  61.8 1.1 %copy-start.4 = (bf16[512,768]{1,0:T(8,128)(2,1)S(1)}, bf16[512,768]{1,0:T(8,128)(2,1)}, u32[]{:S(2)}) copy-start(bf16[512,768]{1,0:T(8,128)(2,1)} %k_ref.1) | copy-start | bytes 2359300
  62.9 1.1 %copy-start.6 = (bf16[512,768]{1,0:T(8,128)(2,1)S(1)}, bf16[512,768]{1,0:T(8,128)(2,1)}, u32[]{:S(2)}) copy-start(bf16[512,768]{1,0:T(8,128)(2,1)} %v_ref.1) | copy-start | bytes 2359300
  64.0 4.5 %copy-start.8 = (f32[6]{0:T(128)S(1)}, f32[6]{0:T(128)}, u32[]{:S(2)}) copy-start(f32[6]{0:T(128)} %slope_ref.1) | copy-start | bytes 76
  71.7 1.2 %copy-start.1 = (f32[768,512]{1,0:T(8,128)}, f32[768,512]{1,0:T(8,128)S(1)}, u32[]{:S(2)}) copy-start(f32[768,512]{1,0:T(8,128)S(1)} %get-tuple-element.35.acc_p_ref) | copy-start | bytes 4718596
  72.8 4.2 %collective-permute-start.6 = (bf16[512,768]{1,0:T(8,128)(2,1)S(1)}, bf16[512,768]{1,0:T(8,128)(2,1)S(1)}, u32[]{:S(2)}, u32[]{:S(2)}) collective-permute-start(bf16[512,768]{1,0:T(8,128)(2,1)S(1)} %bitcast.17), channel_id=1, source_target_pairs={{0,4},{4,0},{1,5},{5,1},{2,6},{6,2},{3,7},{7,3},{8,12},{12,8},{9,1... | collective-permute-start | bytes 2359304 | tf_op jit(solution)/shard_map/ppermute | solution.py:258
  77.0 1.4 %copy-start.2 = (f32[768,512]{1,0:T(8,128)S(1)}, f32[768,512]{1,0:T(8,128)}, u32[]{:S(2)}) copy-start(f32[768,512]{1,0:T(8,128)} %copy-done.1) | copy-start | bytes 4718596

commit v4 on v2

--- a/solution.py
+++ b/solution.py
@@ -53,7 +53,9 @@
             stat_ref[2 * head + 1 : 2 * head + 2, rows] = total
 
 
-def pooled_kernel(tag_ref, slope_ref, q_ref, p_ref, acc_ref, stat_ref):
+def pooled_kernel(
+    tag_ref, slope_ref, q_ref, p_ref, acc_ref, stat_ref, acc_out_ref, stat_out_ref
+):
     count, width = q_ref.shape
     tags = p_ref[:, 2 * width :].astype(jnp.float32)
     dist = jnp.abs(tags - tag_ref[0].astype(jnp.float32)) * LOG2E
@@ -62,38 +64,32 @@
         cols = pl.ds(head * HD, HD)
         scores = dot_nt(p_ref[:, cols], q_ref[:, cols]) * UNIT - dist * slope_ref[head]
         top, total, weights = soft(scores)
-        acc_ref[cols, :] = dot_nn(p_ref[:, pl.ds(width + head * HD, HD)].T, weights)
-        stat_ref[2 * head : 2 * head + 1, :] = top
-        stat_ref[2 * head + 1 : 2 * head + 2, :] = total
-
-
-def ref_kernel(
-    core_ref, q_ref, own_ref, got_ref, acc_w_ref, stat_w_ref, acc_p_ref, stat_p_ref, out_ref
-):
+        num = dot_nn(p_ref[:, pl.ds(width + head * HD, HD)].T, weights)
+        top_n = stat_ref[2 * head : 2 * head + 1, :]
+        total_n = stat_ref[2 * head + 1 : 2 * head + 2, :]
+        ceiling = jnp.maximum(top_n, top)
+        share_n, share = jnp.exp2(top_n - ceiling), jnp.exp2(top - ceiling)
+        acc_out_ref[cols, :] = share_n * acc_ref[cols, :] + share * num
+        stat_out_ref[2 * head : 2 * head + 1, :] = ceiling
+        stat_out_ref[2 * head + 1 : 2 * head + 2, :] = share_n * total_n + share * total
+
+
+def ref_kernel(core_ref, q_ref, own_ref, got_ref, acc_ref, stat_ref, out_ref):
     first = core_ref[0] == 0
     for head in range(q_ref.shape[1] // HD):
         cols = pl.ds(head * HD, HD)
-        top_at, total_at = slice(2 * head, 2 * head + 1), slice(2 * head + 1, 2 * head + 2)
         keys = jnp.where(first, own_ref[:, cols], got_ref[:, cols])
         values = jnp.where(first, got_ref[:, cols], own_ref[:, cols]).T
         for start in range(0, q_ref.shape[0], STRIP):
             rows = pl.ds(start, STRIP)
             top, total, weights = soft(dot_nt(keys, q_ref[rows, cols]) * UNIT)
             num = dot_nn(values, weights)
-            top_w, top_p = stat_w_ref[top_at, rows], stat_p_ref[top_at, rows]
-            ceiling = jnp.maximum(jnp.maximum(top_w, top_p), top)
-            share_w, share_p = jnp.exp2(top_w - ceiling), jnp.exp2(top_p - ceiling)
-            share = jnp.exp2(top - ceiling)
-            scale = 1.0 / (
-                share_w * stat_w_ref[total_at, rows]
-                + share_p * stat_p_ref[total_at, rows]
-                + share * total
-            )
-            merged = (
-                (share_w * scale) * acc_w_ref[cols, rows]
-                + (share_p * scale) * acc_p_ref[cols, rows]
-                + (share * scale) * num
-            )
+            top_n = stat_ref[2 * head : 2 * head + 1, rows]
+            total_n = stat_ref[2 * head + 1 : 2 * head + 2, rows]
+            ceiling = jnp.maximum(top_n, top)
+            share_n, share = jnp.exp2(top_n - ceiling), jnp.exp2(top - ceiling)
+            scale = 1.0 / (share_n * total_n + share * total)
+            merged = (share_n * scale) * acc_ref[cols, rows] + (share * scale) * num
             out_ref[rows, cols] = merged.astype(jnp.bfloat16).T
 
 
@@ -116,7 +112,7 @@
     owner_z = owner // (2 * n_x)
 
     tie = lax.optimization_barrier
-    near = pltpu.CompilerParams(vmem_limit_bytes=16 * 1024 * 1024)
+    near = pltpu.CompilerParams(vmem_limit_bytes=10 * 1024 * 1024)
     state = (
         jax.ShapeDtypeStruct((width, rows), jnp.float32),
         jax.ShapeDtypeStruct((16, rows), jnp.float32),
@@ -131,33 +127,14 @@
         out_shape=jax.ShapeDtypeStruct((POOLS, 2 * width + HD), jnp.bfloat16),
         in_specs=[SMEM, VMEM, VMEM, VMEM],
         out_specs=VMEM,
+        compiler_params=near,
         name="pool",
     )(window_map, pool_segments, keys, values)
     mine = jnp.where(owner_c == core, kept, jnp.where(core == 0, got_k, got_v))
-    mine, pooled = tie((mine, pooled))
+    mine, pooled, queries_w = tie((mine, pooled, queries))
 
     spread = lax.all_to_all(mine.reshape(n_x, part, -1), "x", 0, 0, tiled=True)
     other = lax.ppermute(pooled, "zh", SWAP)
-    piece = lax.dynamic_index_in_dim(spread, owner_x, 0, keepdims=False)
-    piece = piece.reshape(part, n_head, width).transpose(1, 0, 2)
-    piece = jnp.broadcast_to(piece[None], (n_zh, n_head, part, width))
-    piece, pooled, other = tie((piece, pooled, other))
-
-    turned = lax.all_to_all(
-        piece.reshape(n_zh * n_head, part, width), ("zh", "head"), 0, 0, tiled=True
-    )
-    pooled = jnp.concatenate([pooled, other], axis=0)
-    other = lax.ppermute(pooled, "c", SWAP)
-    pooled = jnp.concatenate([pooled, other], axis=0)
-    other = lax.ppermute(pooled, "x", [(i, i ^ 1) for i in range(n_x)])
-    pooled = jnp.concatenate([pooled, other], axis=0)
-    turned = turned.reshape(n_zh, n_head * part, width)
-    block = lax.dynamic_index_in_dim(turned, owner_z, 0, keepdims=False)
-    block = jnp.broadcast_to(block[None], (n_x, n_head * part, width))
-    block, pooled, queries_w = tie((block, pooled, queries))
-
-    own = lax.all_to_all(block, "x", 0, 0, tiled=True).reshape(-1, width)
-    other = lax.ppermute(pooled, "x", [(i, i ^ 2) for i in range(n_x)])
     acc_w, stat_w = pl.pallas_call(
         window_kernel,
         out_shape=state,
@@ -171,31 +148,52 @@
         ),
         name="window",
     )(queries_w, keys, values)
-    pooled = jnp.concatenate([pooled, other], axis=0)
-    own, pooled, acc_w, stat_w = tie((own, pooled, acc_w, stat_w))
-
-    got = lax.ppermute(own, "c", SWAP)
-    acc_p, stat_p = pl.pallas_call(
+    other, stat_w = tie((other, stat_w))
+    pooled = jnp.concatenate([pooled, other], axis=0)
+    other = lax.ppermute(pooled, "x", [(i, i ^ 1) for i in range(n_x)])
+    piece = lax.dynamic_index_in_dim(spread, owner_x, 0, keepdims=False)
+    piece = piece.reshape(part, n_head, width).transpose(1, 0, 2)
+    piece = jnp.broadcast_to(piece[None], (n_zh, n_head, part, width))
+    piece, pooled, other = tie((piece, pooled, other))
+
+    turned = lax.all_to_all(
+        piece.reshape(n_zh * n_head, part, width), ("zh", "head"), 0, 0, tiled=True
+    )
+    pooled = jnp.concatenate([pooled, other], axis=0)
+    other = lax.ppermute(pooled, "x", [(i, i ^ 2) for i in range(n_x)])
+    turned = turned.reshape(n_zh, n_head * part, width)
+    block = lax.dynamic_index_in_dim(turned, owner_z, 0, keepdims=False)
+    block = jnp.broadcast_to(block[None], (n_x, n_head * part, width))
+    block, pooled, other = tie((block, pooled, other))
+
+    own = lax.all_to_all(block, "x", 0, 0, tiled=True).reshape(-1, width)
+    pooled = jnp.concatenate([pooled, other], axis=0)
+    other = lax.ppermute(pooled, "c", SWAP)
+    pooled = jnp.concatenate([pooled, other], axis=0)
+    acc, stat = pl.pallas_call(
         pooled_kernel,
         out_shape=state,
-        in_specs=[SMEM, SMEM, VMEM, VMEM],
+        in_specs=[SMEM, SMEM] + [VMEM] * 4,
         out_specs=(VMEM, VMEM),
         compiler_params=near,
         cost_estimate=pl.CostEstimate(
             flops=4 * rows * pooled.shape[0] * width,
-            bytes_accessed=6 * rows * width,
+            bytes_accessed=12 * rows * width,
             transcendentals=rows * pooled.shape[0] * heads,
         ),
         name="pooled",
-    )(window_map, slopes, queries, pooled)
+    )(window_map, slopes, queries, pooled, acc_w, stat_w)
+    own, stat = tie((own, stat))
+
+    got = lax.ppermute(own, "c", SWAP)
     return pl.pallas_call(
         ref_kernel,
         out_shape=jax.ShapeDtypeStruct((rows, width), jnp.bfloat16),
-        in_specs=[SMEM] + [VMEM] * 7,
+        in_specs=[SMEM] + [VMEM] * 5,
         out_specs=VMEM,
         compiler_params=near,
         name="far",
-    )(core.astype(jnp.int32)[None], queries, own, got, acc_w, stat_w, acc_p, stat_p)
+    )(core.astype(jnp.int32)[None], queries, own, got, acc, stat)
 
 
 def solution(mesh):

time: 86.7 us -> 78.2 us (0.902)
  waiting for transfers between devices: 23.9 us -> 12 us
  starting transfers between devices: 42.5 us -> 47.2 us
  Pallas kernels: 11 us -> 8.84 us
  local copies, waits for them, and re-layouts: 4.48 us -> 5.43 us
    ppermute x1, waiting for transfers between devices: 7.6 us -> 0.01 us  [on_device(): other = lax.ppermute(pooled, 'x', [(i, i ^ 2) for i in range(n_x)])]
    all_to_all x1, waiting for transfers between devices: 6.18 us -> 0.01 us  [on_device(): spread = lax.all_to_all(mine.reshape(n_x, part, -1), 'x', 0, 0, tiled=True)]
    ppermute x1, waiting for transfers between devices: 3.87 us -> 0.89 us  [on_device(): other = lax.ppermute(pooled, 'x', [(i, i ^ 1) for i in range(n_x)])]
    ppermute x1, starting transfers between devices: 2.67 us -> 5.55 us  [on_device(): other = lax.ppermute(pooled, 'c', SWAP)]
    all_to_all x1, waiting for transfers between devices: 5.38 us -> 8.1 us  [on_device(): lax.all_to_all(piece.reshape(n_zh * n_head, part, width), ('zh', 'head'),...]
    pallas_call x1, Pallas kernels: 2.31 us -> 0.32 us  [on_device(): pl.pallas_call(pool_kernel, out_shape=jax.ShapeDtypeStruct((POOLS, 2 * wi...]
    ppermute x1, waiting for transfers between devices: 0.01 us -> 1.89 us  [on_device(): got = lax.ppermute(own, 'c', SWAP)]
    ppermute x1, starting transfers between devices: 3.31 us -> 4.76 us  [on_device(): got = lax.ppermute(own, 'c', SWAP)]
  transfers between devices with their start and end apart: 10 -> 10, of which waited for: 5 -> 4; matrix products, arithmetic and copies ran while one was open for 2% -> 3% of each run, Pallas kernels for 8% -> 6%
where the time goes in v4:
time: 78.2 us; the launch traced here: 77.5 us
  starting transfers between devices  47.2 us (60%)
  waiting for transfers between devices  12 us (15%)
  Pallas kernels  8.84 us (11%)
  local copies, waits for them, and re-layouts  5.43 us (7%)
  other arithmetic  2.5 us (3%)
  between operations  1.59 us (2%)
    ppermute x1, starting transfers between devices, on_device(): got_k = lax.ppermute(slot_k, 'c', [(1, 0)])  9.7 us
    all_to_all x1, waiting for transfers between devices, on_device(): lax.all_to_all(piece.reshape(n_zh * n_head, part, width), ('zh', 'head'),...  8.1 us
    ppermute x1, starting transfers between devices, on_device(): other = lax.ppermute(pooled, 'zh', SWAP)  5.73 us
    ppermute x1, starting transfers between devices, on_device(): other = lax.ppermute(pooled, 'c', SWAP)  5.55 us
    ppermute x1, starting transfers between devices, on_device(): got = lax.ppermute(own, 'c', SWAP)  4.76 us
    all_to_all x1, starting transfers between devices, on_device(): lax.all_to_all(piece.reshape(n_zh * n_head, part, width), ('zh', 'head'),...  4.72 us
    all_to_all x1, starting transfers between devices, on_device(): spread = lax.all_to_all(mine.reshape(n_x, part, -1), 'x', 0, 0, tiled=True)  4.32 us
    ppermute x1, starting transfers between devices, on_device(): other = lax.ppermute(pooled, 'x', [(i, i ^ 2) for i in range(n_x)])  4.11 us
  transfers between devices with their start and end apart: 10, of which 4 were waited for; matrix products, arithmetic and copies ran while one was open for 3% of the time, Pallas kernels for 6%

profile of v4, /device:TPU:1, one launch (start us, length us, event | category | flops | bytes accessed | tf_op | source)
XLA Modules:
  0.0 77.5 jit_solution(1643042411550011767)
XLA Ops:
  0.0 1.4 %collective-permute-start.1 = (bf16[128,3072]{1,0:T(8,128)(2,1)}, bf16[128,3072]{1,0:T(8,128)(2,1)S(1)}, u32[]{:S(2)}, u32[]{:S(2)}) collective-permute-start(bf16[128,3072]{1,0:T(8,128)(2,1)} %bitcast.20), channel_id=1, source_target_pairs={{0,4},{1,5},{2,6},{3,7},{8,12},{9,13},{10,14},{11,15},{16,20},{17,... | collective-permute-start | bytes 2359304 | tf_op jit(solution)/shard_map/ppermute | solution.py:123
  1.4 9.7 %collective-permute-start = (bf16[128,3072]{1,0:T(8,128)(2,1)}, bf16[128,3072]{1,0:T(8,128)(2,1)}, u32[]{:S(2)}, u32[]{:S(2)}) collective-permute-start(bf16[128,3072]{1,0:T(8,128)(2,1)} %bitcast.21), channel_id=1, source_target_pairs={{4,0},{5,1},{6,2},{7,3},{12,8},{13,9},{14,10},{15,11},{20,16},{21,... | collective-permute-start | bytes 2359304 | tf_op jit(solution)/shard_map/ppermute | solution.py:122
  12.5 1.5 %broadcast_select_fusion = bf16[128,3072]{1,0:T(8,128)(2,1)S(1)} fusion(pred[]{:T(512)S(6)} %eq.11, bf16[1,128,3072]{2,1,0:T(8,128)(2,1)} %param.16, bf16[1,128,3072]{2,1,0:T(8,128)(2,1)} %param.15), kind=kLoop, calls=%fused_computation.1 | loop fusion | flops 393216 | bytes 2359297 | tf_op jit(solution)/shard_map/jit(_where)/select_n | solution.py:124
  14.0 0.3 pool.1
  14.3 0.0 collective-permute-done.1
  14.3 0.0 collective-permute-done
  14.3 1.0 %select_select_fusion = bf16[128,3072]{1,0:T(8,128)(2,1)} fusion(bf16[128,3072]{1,0:T(8,128)(2,1)S(1)} %broadcast_select_fusion, bf16[128,3072]{1,0:T(8,128)(2,1)} %collective-permute-done, bf16[128,3072]{1,0:T(8,128)(2,1)S(1)} %collective-permute-done.1, pred[]{:T(512)S(6)} %eq.11, pred[]{:T(512)S(6)} %eq.10), kind=kLoop, calls=%fused_computation | loop fusion | flops 786432 | bytes 3145730 | tf_op jit(solution)/shard_map/jit(_where)/select_n | solution.py:133
  15.3 4.3 %all-to-all-start = ((bf16[4,32,3072]{2,1,0:T(8,128)(2,1)}), bf16[4,32,3072]{2,1,0:T(8,128)(2,1)}, u32[]{:S(2)}, u32[]{:S(2)}) async-start(bf16[4,32,3072]{2,1,0:T(8,128)(2,1)} %bitcast.4), calls=%async_computation | async-start | bytes 1572864 | tf_op jit(solution)/shard_map/all_to_all | solution.py:136
  19.7 5.7 %collective-permute-start.2 = (bf16[8,1664]{1,0:T(8,128)(2,1)S(1)}, bf16[8,1664]{1,0:T(8,128)(2,1)S(1)}, u32[]{:S(2)}, u32[]{:S(2)}) collective-permute-start(bf16[8,1664]{1,0:T(8,128)(2,1)S(1)} %pool.1), channel_id=1, source_target_pairs={{0,32},{32,0},{1,33},{33,1},{2,34},{34,2},{3,35},{35,3},{4,36},{36... | collective-permute-start | bytes 79880 | tf_op jit(solution)/shard_map/ppermute | solution.py:137
  25.4 2.5 %window.1 = (f32[768,512]{1,0:T(8,128)S(1)}, f32[16,512]{1,0:T(8,128)S(1)}) custom-call(bf16[512,768]{1,0:T(8,128)(2,1)S(1)} %copy-done, bf16[512,768]{1,0:T(8,128)(2,1)S(1)} %copy-done.3, bf16[512,768]{1,0:T(8,128)(2,1)S(1)} %copy-done.4), custom_call_target="tpu_custom_call" | custom-call | flops 805306368 | bytes 3932160 | tf_op jit(solution)/shard_map/window/pallas_call | solution.py:138
  27.9 1.2 %copy-done.1 = f32[768,512]{1,0:T(8,128)} copy-done((f32[768,512]{1,0:T(8,128)}, f32[768,512]{1,0:T(8,128)S(1)}, u32[]{:S(2)}) %copy-start.1) | copy-done | bytes 1572888
  29.1 0.0 collective-permute-done.2
  29.1 3.3 %collective-permute-start.3 = (bf16[16,1664]{1,0:T(8,128)(2,1)S(1)}, bf16[16,1664]{1,0:T(8,128)(2,1)S(1)}, u32[]{:S(2)}, u32[]{:S(2)}) collective-permute-start(bf16[16,1664]{1,0:T(8,128)(2,1)S(1)} %constant_dynamic-update-slice_fusion), channel_id=1, source_target_pairs={{0,8},{8,0},{16,24},{24,16},{1,9},{9,1},{17,25},{25,17},{2,10},{10... | collective-permute-start | bytes 159752 | tf_op jit(solution)/shard_map/ppermute | solution.py:153
  32.4 0.0 all-to-all-done
  32.4 0.9 %constant_dynamic-slice_fusion = bf16[1,32,3072]{2,1,0:T(8,128)(2,1)S(1)} fusion(bf16[4,32,3072]{2,1,0:T(8,128)(2,1)} %all-to-all-done, s32[]{:T(128)S(6)} %select_n.52), kind=kLoop, calls=%fused_computation.9 | loop fusion | bytes 393220 | tf_op jit(solution)/shard_map/jit(dynamic_index_in_dim)/dynamic_slice | solution.py:154
  33.3 0.1 reshape.18
  33.5 0.9 %collective-permute-done.3 = bf16[16,1664]{1,0:T(8,128)(2,1)S(1)} collective-permute-done((bf16[16,1664]{1,0:T(8,128)(2,1)S(1)}, bf16[16,1664]{1,0:T(8,128)(2,1)S(1)}, u32[]{:S(2)}, u32[]{:S(2)}) %collective-permute-start.3) | collective-permute-done | bytes 53280 | tf_op jit(solution)/shard_map/ppermute | solution.py:153
  34.4 0.8 %broadcast_in_dim.18 = bf16[2,4,32,768]{3,2,1,0:T(8,128)(2,1)} broadcast(bf16[4,32,768]{2,1,0:T(8,128)(2,1)S(1)} %copy.10), dimensions={1,2,3} | broadcast | bytes 589824 | tf_op jit(solution)/shard_map/broadcast_in_dim | solution.py:156
  35.2 4.7 %all-to-all-start.1 = ((bf16[8,32,768]{2,1,0:T(8,128)(2,1)}), bf16[8,32,768]{2,1,0:T(8,128)(2,1)S(1)}, u32[]{:S(2)}, u32[]{:S(2)}) async-start(bf16[8,32,768]{2,1,0:T(8,128)(2,1)} %bitcast.6), calls=%async_computation.1 | async-start | bytes 786432 | tf_op jit(solution)/shard_map/all_to_all | solution.py:159
  39.9 4.1 %collective-permute-start.4 = (bf16[32,1664]{1,0:T(8,128)(2,1)S(1)}, bf16[32,1664]{1,0:T(8,128)(2,1)S(1)}, u32[]{:S(2)}, u32[]{:S(2)}) collective-permute-start(bf16[32,1664]{1,0:T(8,128)(2,1)S(1)} %constant_dynamic-update-slice_fusion.2), channel_id=1, source_target_pairs={{0,16},{8,24},{16,0},{24,8},{1,17},{9,25},{17,1},{25,9},{2,18},{10... | collective-permute-start | bytes 319496 | tf_op jit(solution)/shard_map/ppermute | solution.py:163
  44.0 8.1 %all-to-all-done.1 = bf16[8,32,768]{2,1,0:T(8,128)(2,1)S(1)} async-done(((bf16[8,32,768]{2,1,0:T(8,128)(2,1)}), bf16[8,32,768]{2,1,0:T(8,128)(2,1)S(1)}, u32[]{:S(2)}, u32[]{:S(2)}) %all-to-all-start.1) | async-done | bytes 393248 | tf_op jit(solution)/shard_map/all_to_all | solution.py:159
  52.1 0.0 collective-permute-done.4
  52.2 0.9 %broadcast_in_dim.20 = bf16[4,128,768]{2,1,0:T(8,128)(2,1)} broadcast(bf16[128,768]{1,0:T(8,128)(2,1)S(1)} %dynamic-slice_bitcast_fusion), dimensions={1,2} | broadcast | bytes 983040 | tf_op jit(solution)/shard_map/broadcast_in_dim | solution.py:166
  53.1 3.6 %all-to-all-start.2 = ((bf16[4,128,768]{2,1,0:T(8,128)(2,1)}), bf16[4,128,768]{2,1,0:T(8,128)(2,1)S(1)}, u32[]{:S(2)}, u32[]{:S(2)}) async-start(bf16[4,128,768]{2,1,0:T(8,128)(2,1)} %broadcast_in_dim.20), calls=%async_computation.2 | async-start | bytes 1572864 | tf_op jit(solution)/shard_map/all_to_all | solution.py:169
  56.8 5.6 %collective-permute-start.5 = (bf16[64,1664]{1,0:T(8,128)(2,1)S(1)}, bf16[64,1664]{1,0:T(8,128)(2,1)S(1)}, u32[]{:S(2)}, u32[]{:S(2)}) collective-permute-start(bf16[64,1664]{1,0:T(8,128)(2,1)S(1)} %pad_maximum_fusion.1), channel_id=1, source_target_pairs={{0,4},{4,0},{1,5},{5,1},{2,6},{6,2},{3,7},{7,3},{8,12},{12,8},{9,1... | collective-permute-start | bytes 638984 | tf_op jit(solution)/shard_map/ppermute | solution.py:171
  62.3 1.1 %collective-permute-done.5 = bf16[64,1664]{1,0:T(8,128)(2,1)S(1)} collective-permute-done((bf16[64,1664]{1,0:T(8,128)(2,1)S(1)}, bf16[64,1664]{1,0:T(8,128)(2,1)S(1)}, u32[]{:S(2)}, u32[]{:S(2)}) %collective-permute-start.5) | collective-permute-done | bytes 213024 | tf_op jit(solution)/shard_map/ppermute | solution.py:171
  63.4 1.4 %copy-done.2 = f32[768,512]{1,0:T(8,128)S(1)} copy-done((f32[768,512]{1,0:T(8,128)S(1)}, f32[768,512]{1,0:T(8,128)}, u32[]{:S(2)}) %copy-start.2) | copy-done | bytes 1572888
  64.8 2.2 %pooled.1 = (f32[768,512]{1,0:T(8,128)S(1)}, f32[16,512]{1,0:T(8,128)S(1)}) custom-call(s32[1]{0:T(128)S(6)} %copy.13.tag_ref, f32[6]{0:T(128)S(1)} %copy-done.6, bf16[512,768]{1,0:T(8,128)(2,1)S(1)} %copy-done, bf16[128,1664]{1,0:T(8,128)(2,1)S(1)} %pad_maximum_fusion.p_ref, f32[768,512]{1,0:T(8,128)S(1)} %copy-done.2, f32[16,512]{1,0:T(8,128)S(1)} %get-tuple-element.34.stat_ref), custom_call_target="tpu_custom_call" | custom-call | flops 201326592 | bytes 4718592 | tf_op jit(solution)/shard_map/pooled/pallas_call | solution.py:173
  67.1 0.0 all-to-all-done.2
  67.1 4.8 %collective-permute-start.6 = (bf16[512,768]{1,0:T(8,128)(2,1)S(1)}, bf16[512,768]{1,0:T(8,128)(2,1)S(1)}, u32[]{:S(2)}, u32[]{:S(2)}) collective-permute-start(bf16[512,768]{1,0:T(8,128)(2,1)S(1)} %bitcast.17), channel_id=1, source_target_pairs={{0,4},{4,0},{1,5},{5,1},{2,6},{6,2},{3,7},{7,3},{8,12},{12,8},{9,1... | collective-permute-start | bytes 2359304 | tf_op jit(solution)/shard_map/ppermute | solution.py:188
  71.8 1.9 %collective-permute-done.6.got_ref = bf16[512,768]{1,0:T(8,128)(2,1)S(1)} collective-permute-done((bf16[512,768]{1,0:T(8,128)(2,1)S(1)}, bf16[512,768]{1,0:T(8,128)(2,1)S(1)}, u32[]{:S(2)}, u32[]{:S(2)}) %collective-permute-start.6) | collective-permute-done | bytes 786464 | tf_op jit(solution)/shard_map/ppermute | solution.py:188
  73.7 3.8 %far.1 = bf16[512,768]{1,0:T(8,128)(2,1)} custom-call(s32[1]{0:T(128)} %bitcast.core_ref, bf16[512,768]{1,0:T(8,128)(2,1)S(1)} %copy-done, bf16[512,768]{1,0:T(8,128)(2,1)S(1)} %bitcast.18, bf16[512,768]{1,0:T(8,128)(2,1)S(1)} %collective-permute-done.6.got_ref, f32[768,512]{1,0:T(8,128)S(1)} %get-tuple-element.37.acc_ref, ...), custom_call_target="tpu_custom_call" | custom-call | tf_op jit(solution)/shard_map/far/pallas_call | solution.py:189
  (20 shorter events, 0.1 us)
Async XLA Ops:
  0.0 13.9 %copy-start.4 = (bf16[512,768]{1,0:T(8,128)(2,1)S(1)}, bf16[512,768]{1,0:T(8,128)(2,1)}, u32[]{:S(2)}) copy-start(bf16[512,768]{1,0:T(8,128)(2,1)} %v_ref.1) | copy-start | bytes 2359300
  0.0 13.9 %copy-start.3 = (bf16[512,768]{1,0:T(8,128)(2,1)S(1)}, bf16[512,768]{1,0:T(8,128)(2,1)}, u32[]{:S(2)}) copy-start(bf16[512,768]{1,0:T(8,128)(2,1)} %k_ref.1) | copy-start | bytes 2359300
  0.0 13.9 %copy-start.5 = (s32[1,512]{1,0:T(1,128)S(1)}, s32[1,512]{1,0:T(1,128)}, u32[]{:S(2)}) copy-start(s32[1,512]{1,0:T(1,128)} %seg_ref.1) | copy-start | bytes 6148
  0.0 14.3 %collective-permute-start.1 = (bf16[128,3072]{1,0:T(8,128)(2,1)}, bf16[128,3072]{1,0:T(8,128)(2,1)S(1)}, u32[]{:S(2)}, u32[]{:S(2)}) collective-permute-start(bf16[128,3072]{1,0:T(8,128)(2,1)} %bitcast.20), channel_id=1, source_target_pairs={{0,4},{1,5},{2,6},{3,7},{8,12},{9,13},{10,14},{11,15},{16,20},{17,... | collective-permute-start | bytes 2359304 | tf_op jit(solution)/shard_map/ppermute | solution.py:123
  1.4 12.8 %collective-permute-start = (bf16[128,3072]{1,0:T(8,128)(2,1)}, bf16[128,3072]{1,0:T(8,128)(2,1)}, u32[]{:S(2)}, u32[]{:S(2)}) collective-permute-start(bf16[128,3072]{1,0:T(8,128)(2,1)} %bitcast.21), channel_id=1, source_target_pairs={{4,0},{5,1},{6,2},{7,3},{12,8},{13,9},{14,10},{15,11},{20,16},{21,... | collective-permute-start | bytes 2359304 | tf_op jit(solution)/shard_map/ppermute | solution.py:122
  15.3 10.1 %copy-start = (bf16[512,768]{1,0:T(8,128)(2,1)S(1)}, bf16[512,768]{1,0:T(8,128)(2,1)}, u32[]{:S(2)}) copy-start(bf16[512,768]{1,0:T(8,128)(2,1)} %q_ref.4) | copy-start | bytes 2359300
  15.3 17.1 %all-to-all-start = ((bf16[4,32,3072]{2,1,0:T(8,128)(2,1)}), bf16[4,32,3072]{2,1,0:T(8,128)(2,1)}, u32[]{:S(2)}, u32[]{:S(2)}) async-start(bf16[4,32,3072]{2,1,0:T(8,128)(2,1)} %bitcast.4), calls=%async_computation | async-start | bytes 1572864 | tf_op jit(solution)/shard_map/all_to_all | solution.py:136
  19.7 9.4 %collective-permute-start.2 = (bf16[8,1664]{1,0:T(8,128)(2,1)S(1)}, bf16[8,1664]{1,0:T(8,128)(2,1)S(1)}, u32[]{:S(2)}, u32[]{:S(2)}) collective-permute-start(bf16[8,1664]{1,0:T(8,128)(2,1)S(1)} %pool.1), channel_id=1, source_target_pairs={{0,32},{32,0},{1,33},{33,1},{2,34},{34,2},{3,35},{35,3},{4,36},{36... | collective-permute-start | bytes 79880 | tf_op jit(solution)/shard_map/ppermute | solution.py:137
  27.9 1.2 %copy-start.1 = (f32[768,512]{1,0:T(8,128)}, f32[768,512]{1,0:T(8,128)S(1)}, u32[]{:S(2)}) copy-start(f32[768,512]{1,0:T(8,128)S(1)} %get-tuple-element.33.acc_ref) | copy-start | bytes 4718596
  29.1 5.3 %collective-permute-start.3 = (bf16[16,1664]{1,0:T(8,128)(2,1)S(1)}, bf16[16,1664]{1,0:T(8,128)(2,1)S(1)}, u32[]{:S(2)}, u32[]{:S(2)}) collective-permute-start(bf16[16,1664]{1,0:T(8,128)(2,1)S(1)} %constant_dynamic-update-slice_fusion), channel_id=1, source_target_pairs={{0,8},{8,0},{16,24},{24,16},{1,9},{9,1},{17,25},{25,17},{2,10},{10... | collective-permute-start | bytes 159752 | tf_op jit(solution)/shard_map/ppermute | solution.py:153
  35.2 17.0 %all-to-all-start.1 = ((bf16[8,32,768]{2,1,0:T(8,128)(2,1)}), bf16[8,32,768]{2,1,0:T(8,128)(2,1)S(1)}, u32[]{:S(2)}, u32[]{:S(2)}) async-start(bf16[8,32,768]{2,1,0:T(8,128)(2,1)} %bitcast.6), calls=%async_computation.1 | async-start | bytes 786432 | tf_op jit(solution)/shard_map/all_to_all | solution.py:159
  39.9 12.2 %collective-permute-start.4 = (bf16[32,1664]{1,0:T(8,128)(2,1)S(1)}, bf16[32,1664]{1,0:T(8,128)(2,1)S(1)}, u32[]{:S(2)}, u32[]{:S(2)}) collective-permute-start(bf16[32,1664]{1,0:T(8,128)(2,1)S(1)} %constant_dynamic-update-slice_fusion.2), channel_id=1, source_target_pairs={{0,16},{8,24},{16,0},{24,8},{1,17},{9,25},{17,1},{25,9},{2,18},{10... | collective-permute-start | bytes 319496 | tf_op jit(solution)/shard_map/ppermute | solution.py:163
  53.1 10.3 %copy-start.6 = (f32[6]{0:T(128)S(1)}, f32[6]{0:T(128)}, u32[]{:S(2)}) copy-start(f32[6]{0:T(128)} %slope_ref.1) | copy-start | bytes 76
  53.1 14.0 %all-to-all-start.2 = ((bf16[4,128,768]{2,1,0:T(8,128)(2,1)}), bf16[4,128,768]{2,1,0:T(8,128)(2,1)S(1)}, u32[]{:S(2)}, u32[]{:S(2)}) async-start(bf16[4,128,768]{2,1,0:T(8,128)(2,1)} %broadcast_in_dim.20), calls=%async_computation.2 | async-start | bytes 1572864 | tf_op jit(solution)/shard_map/all_to_all | solution.py:169
  56.8 6.6 %collective-permute-start.5 = (bf16[64,1664]{1,0:T(8,128)(2,1)S(1)}, bf16[64,1664]{1,0:T(8,128)(2,1)S(1)}, u32[]{:S(2)}, u32[]{:S(2)}) collective-permute-start(bf16[64,1664]{1,0:T(8,128)(2,1)S(1)} %pad_maximum_fusion.1), channel_id=1, source_target_pairs={{0,4},{4,0},{1,5},{5,1},{2,6},{6,2},{3,7},{7,3},{8,12},{12,8},{9,1... | collective-permute-start | bytes 638984 | tf_op jit(solution)/shard_map/ppermute | solution.py:171
  63.4 1.4 %copy-start.2 = (f32[768,512]{1,0:T(8,128)S(1)}, f32[768,512]{1,0:T(8,128)}, u32[]{:S(2)}) copy-start(f32[768,512]{1,0:T(8,128)} %copy-done.1) | copy-start | bytes 4718596
  67.1 6.7 %collective-permute-start.6 = (bf16[512,768]{1,0:T(8,128)(2,1)S(1)}, bf16[512,768]{1,0:T(8,128)(2,1)S(1)}, u32[]{:S(2)}, u32[]{:S(2)}) collective-permute-start(bf16[512,768]{1,0:T(8,128)(2,1)S(1)} %bitcast.17), channel_id=1, source_target_pairs={{0,4},{4,0},{1,5},{5,1},{2,6},{6,2},{3,7},{7,3},{8,12},{12,8},{9,1... | collective-permute-start | bytes 2359304 | tf_op jit(solution)/shard_map/ppermute | solution.py:188

commit v5 on v4

--- a/solution.py
+++ b/solution.py
@@ -23,16 +23,12 @@
     return jnp.dot(a, b, preferred_element_type=jnp.float32)
 
 
-def pool_kernel(tag_ref, seg_ref, key_ref, value_ref, out_ref):
+def pool_kernel(seg_ref, token_ref, out_ref):
     seg = seg_ref[...]
     member = seg == lax.broadcasted_iota(jnp.int32, (POOLS, seg.shape[1]), 0)
     count = jnp.sum(member.astype(jnp.float32), axis=1, keepdims=True)
     member = member.astype(jnp.float32).astype(jnp.bfloat16)
-    width = key_ref.shape[1]
-    out_ref[:, :width] = (dot_nn(member, key_ref[...]) / count).astype(jnp.bfloat16)
-    out_ref[:, width : 2 * width] = (dot_nn(member, value_ref[...]) / count).astype(jnp.bfloat16)
-    tag = jnp.full((POOLS, HD), tag_ref[0], jnp.int32)
-    out_ref[:, 2 * width :] = tag.astype(jnp.float32).astype(jnp.bfloat16)
+    out_ref[...] = (dot_nn(member, token_ref[...]) / count).astype(jnp.bfloat16)
 
 
 def soft(scores):
@@ -122,19 +118,36 @@
     got_k = lax.ppermute(slot_k, "c", [(1, 0)])
     got_v = lax.ppermute(slot_v, "c", [(0, 1)])
     kept = tie(jnp.where(core == 0, slot_k, slot_v))
-    pooled = pl.pallas_call(
+    pool = pl.pallas_call(
         pool_kernel,
-        out_shape=jax.ShapeDtypeStruct((POOLS, 2 * width + HD), jnp.bfloat16),
-        in_specs=[SMEM, VMEM, VMEM, VMEM],
+        out_shape=jax.ShapeDtypeStruct((POOLS, width), jnp.bfloat16),
+        in_specs=[VMEM, VMEM],
         out_specs=VMEM,
         compiler_params=near,
         name="pool",
-    )(window_map, pool_segments, keys, values)
+    )
+    pooled_k = pool(pool_segments, keys)
+    pooled_k, values_p = tie((pooled_k, values))
+    pooled_v = pool(pool_segments, values_p)
+    tag = jnp.broadcast_to(window_map.astype(jnp.bfloat16)[:, None], (POOLS, HD))
+    pooled = jnp.concatenate([pooled_k, pooled_v, tag], axis=1)
     mine = jnp.where(owner_c == core, kept, jnp.where(core == 0, got_k, got_v))
-    mine, pooled, queries_w = tie((mine, pooled, queries))
+    mine, pooled = tie((mine, pooled))
 
     spread = lax.all_to_all(mine.reshape(n_x, part, -1), "x", 0, 0, tiled=True)
+    other = lax.ppermute(pooled, "x", [(i, i ^ 1) for i in range(n_x)])
+    pooled = jnp.concatenate([pooled, other], axis=0)
     other = lax.ppermute(pooled, "zh", SWAP)
+    piece = lax.dynamic_index_in_dim(spread, owner_x, 0, keepdims=False)
+    piece = piece.reshape(part, n_head, width).transpose(1, 0, 2)
+    piece = jnp.broadcast_to(piece[None], (n_zh, n_head, part, width))
+    piece, pooled, other, queries_w = tie((piece, pooled, other, queries))
+
+    turned = lax.all_to_all(
+        piece.reshape(n_zh * n_head, part, width), ("zh", "head"), 0, 0, tiled=True
+    )
+    pooled = jnp.concatenate([pooled, other], axis=0)
+    other = lax.ppermute(pooled, "x", [(i, i ^ 2) for i in range(n_x)])
     acc_w, stat_w = pl.pallas_call(
         window_kernel,
         out_shape=state,
@@ -148,23 +161,10 @@
         ),
         name="window",
     )(queries_w, keys, values)
-    other, stat_w = tie((other, stat_w))
-    pooled = jnp.concatenate([pooled, other], axis=0)
-    other = lax.ppermute(pooled, "x", [(i, i ^ 1) for i in range(n_x)])
-    piece = lax.dynamic_index_in_dim(spread, owner_x, 0, keepdims=False)
-    piece = piece.reshape(part, n_head, width).transpose(1, 0, 2)
-    piece = jnp.broadcast_to(piece[None], (n_zh, n_head, part, width))
-    piece, pooled, other = tie((piece, pooled, other))
-
-    turned = lax.all_to_all(
-        piece.reshape(n_zh * n_head, part, width), ("zh", "head"), 0, 0, tiled=True
-    )
-    pooled = jnp.concatenate([pooled, other], axis=0)
-    other = lax.ppermute(pooled, "x", [(i, i ^ 2) for i in range(n_x)])
     turned = turned.reshape(n_zh, n_head * part, width)
     block = lax.dynamic_index_in_dim(turned, owner_z, 0, keepdims=False)
     block = jnp.broadcast_to(block[None], (n_x, n_head * part, width))
-    block, pooled, other = tie((block, pooled, other))
+    block, pooled, other, stat_w = tie((block, pooled, other, stat_w))
 
     own = lax.all_to_all(block, "x", 0, 0, tiled=True).reshape(-1, width)
     pooled = jnp.concatenate([pooled, other], axis=0)

time: 78.2 us -> 90.3 us (1.15)
  waiting for transfers between devices: 12 us -> 24.8 us
  other arithmetic: 2.5 us -> 3.73 us
  starting transfers between devices: 47.2 us -> 46 us
    ppermute x1, waiting for transfers between devices: 0.89 us -> 7.29 us  [on_device(): other = lax.ppermute(pooled, 'x', [(i, i ^ 1) for i in range(n_x)])]
    all_to_all x1, waiting for transfers between devices: 0.01 us -> 4.44 us  [on_device(): own = lax.all_to_all(block, 'x', 0, 0, tiled=True).reshape(-1, width)]
    ppermute x1, starting transfers between devices: 5.55 us -> 2.52 us  [on_device(): other = lax.ppermute(pooled, 'c', SWAP)]
    ppermute x1, waiting for transfers between devices: 0.01 us -> 2.65 us  [on_device(): other = lax.ppermute(pooled, 'zh', SWAP)]
    all_to_all x1, starting transfers between devices: 4.72 us -> 7.18 us  [on_device(): lax.all_to_all(piece.reshape(n_zh * n_head, part, width), ('zh', 'head'),...]
    ppermute x1, starting transfers between devices: 4.76 us -> 3.37 us  [on_device(): got = lax.ppermute(own, 'c', SWAP)]
    select_n x1, other arithmetic: 1 us -> 2.13 us  [on_device(): mine = jnp.where(owner_c == core, kept, jnp.where(core == 0, got_k, got_v))]
    dynamic_slice x1, local copies, waits for them, and re-layouts: 0.95 us -> 0.02 us  [on_device(): piece = lax.dynamic_index_in_dim(spread, owner_x, 0, keepdims=False)]
  transfers between devices with their start and end apart: 10 -> 10, of which waited for: 4 -> 6; matrix products, arithmetic and copies ran while one was open for 3% -> 2% of each run, Pallas kernels for 6% -> 6%
where the time goes in v5:
time: 90.3 us; the launch traced here: 89.7 us
  starting transfers between devices  46 us (51%)
  waiting for transfers between devices  24.8 us (27%)
  Pallas kernels  8.95 us (10%)
  local copies, waits for them, and re-layouts  4.53 us (5%)
  other arithmetic  3.73 us (4%)
  between operations  1.61 us (2%)
    ppermute x1, starting transfers between devices, on_device(): got_k = lax.ppermute(slot_k, 'c', [(1, 0)])  10.6 us
    all_to_all x1, waiting for transfers between devices, on_device(): lax.all_to_all(piece.reshape(n_zh * n_head, part, width), ('zh', 'head'),...  7.49 us
    ppermute x1, waiting for transfers between devices, on_device(): other = lax.ppermute(pooled, 'x', [(i, i ^ 1) for i in range(n_x)])  7.29 us
    all_to_all x1, starting transfers between devices, on_device(): lax.all_to_all(piece.reshape(n_zh * n_head, part, width), ('zh', 'head'),...  7.18 us
    ppermute x1, starting transfers between devices, on_device(): other = lax.ppermute(pooled, 'zh', SWAP)  6.61 us
    all_to_all x1, waiting for transfers between devices, on_device(): own = lax.all_to_all(block, 'x', 0, 0, tiled=True).reshape(-1, width)  4.44 us
    ppermute x1, starting transfers between devices, on_device(): other = lax.ppermute(pooled, 'x', [(i, i ^ 2) for i in range(n_x)])  3.82 us
    pallas_call x1, Pallas kernels, on_device(): pl.pallas_call(ref_kernel, out_shape=jax.ShapeDtypeStruct((rows, width),...  3.81 us
  transfers between devices with their start and end apart: 10, of which 6 were waited for; matrix products, arithmetic and copies ran while one was open for 2% of the time, Pallas kernels for 6%

profile of v5, /device:TPU:1, one launch (start us, length us, event | category | flops | bytes accessed | tf_op | source)
XLA Modules:
  0.0 89.7 jit_solution(6054145889490975293)
XLA Ops:
  0.0 1.4 %collective-permute-start.1 = (bf16[128,3072]{1,0:T(8,128)(2,1)}, bf16[128,3072]{1,0:T(8,128)(2,1)}, u32[]{:S(2)}, u32[]{:S(2)}) collective-permute-start(bf16[128,3072]{1,0:T(8,128)(2,1)} %bitcast.21), channel_id=1, source_target_pairs={{0,4},{1,5},{2,6},{3,7},{8,12},{9,13},{10,14},{11,15},{16,20},{17,... | collective-permute-start | bytes 2359304 | tf_op jit(solution)/shard_map/ppermute | solution.py:119
  1.4 10.6 %collective-permute-start = (bf16[128,3072]{1,0:T(8,128)(2,1)}, bf16[128,3072]{1,0:T(8,128)(2,1)}, u32[]{:S(2)}, u32[]{:S(2)}) collective-permute-start(bf16[128,3072]{1,0:T(8,128)(2,1)} %bitcast.22), channel_id=1, source_target_pairs={{4,0},{5,1},{6,2},{7,3},{12,8},{13,9},{14,10},{15,11},{20,16},{21,... | collective-permute-start | bytes 2359304 | tf_op jit(solution)/shard_map/ppermute | solution.py:118
  12.0 1.5 %broadcast_select_fusion = bf16[128,3072]{1,0:T(8,128)(2,1)S(1)} fusion(pred[]{:T(512)S(6)} %eq.11, bf16[1,128,3072]{2,1,0:T(8,128)(2,1)} %param.16, bf16[1,128,3072]{2,1,0:T(8,128)(2,1)} %param.15), kind=kLoop, calls=%fused_computation.1 | loop fusion | flops 393216 | bytes 2359297 | tf_op jit(solution)/shard_map/jit(_where)/select_n | solution.py:120
  14.9 0.2 pool.2
  15.1 0.2 pool.3
  15.3 0.0 collective-permute-done.1
  15.4 0.0 collective-permute-done
  15.4 2.1 %select_select_fusion = bf16[128,3072]{1,0:T(8,128)(2,1)} fusion(bf16[128,3072]{1,0:T(8,128)(2,1)S(1)} %broadcast_select_fusion, bf16[128,3072]{1,0:T(8,128)(2,1)} %collective-permute-done, bf16[128,3072]{1,0:T(8,128)(2,1)} %collective-permute-done.1, pred[]{:T(512)S(6)} %eq.11, pred[]{:T(512)S(6)} %eq.10), kind=kLoop, calls=%fused_computation | loop fusion | flops 786432 | bytes 3145730 | tf_op jit(solution)/shard_map/jit(_where)/select_n | solution.py:134
  17.5 3.5 %all-to-all-start = ((bf16[4,32,3072]{2,1,0:T(8,128)(2,1)}), bf16[4,32,3072]{2,1,0:T(8,128)(2,1)S(1)}, u32[]{:S(2)}, u32[]{:S(2)}) async-start(bf16[4,32,3072]{2,1,0:T(8,128)(2,1)} %bitcast.5), calls=%async_computation | async-start | bytes 1572864 | tf_op jit(solution)/shard_map/all_to_all | solution.py:137
  21.0 0.0 copy-start
  21.1 3.4 %collective-permute-start.2 = (bf16[8,1664]{1,0:T(8,128)(2,1)S(1)}, bf16[8,1664]{1,0:T(8,128)(2,1)S(1)}, u32[]{:S(2)}, u32[]{:S(2)}) collective-permute-start(bf16[8,1664]{1,0:T(8,128)(2,1)S(1)} %maximum_maximum_fusion), channel_id=1, source_target_pairs={{0,8},{8,0},{16,24},{24,16},{1,9},{9,1},{17,25},{25,17},{2,10},{10... | collective-permute-start | bytes 79880 | tf_op jit(solution)/shard_map/ppermute | solution.py:138
  24.5 7.3 %collective-permute-done.2 = bf16[8,1664]{1,0:T(8,128)(2,1)S(1)} collective-permute-done((bf16[8,1664]{1,0:T(8,128)(2,1)S(1)}, bf16[8,1664]{1,0:T(8,128)(2,1)S(1)}, u32[]{:S(2)}, u32[]{:S(2)}) %collective-permute-start.2) | collective-permute-done | bytes 26656 | tf_op jit(solution)/shard_map/ppermute | solution.py:138
  31.8 6.6 %collective-permute-start.3 = (bf16[16,1664]{1,0:T(8,128)(2,1)S(1)}, bf16[16,1664]{1,0:T(8,128)(2,1)S(1)}, u32[]{:S(2)}, u32[]{:S(2)}) collective-permute-start(bf16[16,1664]{1,0:T(8,128)(2,1)S(1)} %constant_dynamic-update-slice_fusion), channel_id=1, source_target_pairs={{0,32},{32,0},{1,33},{33,1},{2,34},{34,2},{3,35},{35,3},{4,36},{36... | collective-permute-start | bytes 159752 | tf_op jit(solution)/shard_map/ppermute | solution.py:140
  38.4 0.0 all-to-all-done
  38.4 0.1 reshape.19
  38.6 2.6 %collective-permute-done.3 = bf16[16,1664]{1,0:T(8,128)(2,1)S(1)} collective-permute-done((bf16[16,1664]{1,0:T(8,128)(2,1)S(1)}, bf16[16,1664]{1,0:T(8,128)(2,1)S(1)}, u32[]{:S(2)}, u32[]{:S(2)}) %collective-permute-start.3) | collective-permute-done | bytes 53280 | tf_op jit(solution)/shard_map/ppermute | solution.py:140
  41.3 0.8 broadcast_in_dim.28
  42.0 7.2 %all-to-all-start.1 = ((bf16[8,32,768]{2,1,0:T(8,128)(2,1)}), bf16[8,32,768]{2,1,0:T(8,128)(2,1)S(1)}, u32[]{:S(2)}, u32[]{:S(2)}) async-start(bf16[8,32,768]{2,1,0:T(8,128)(2,1)} %bitcast.7), calls=%async_computation.1 | async-start | bytes 786432 | tf_op jit(solution)/shard_map/all_to_all | solution.py:146
  49.2 3.8 %collective-permute-start.4 = (bf16[32,1664]{1,0:T(8,128)(2,1)S(1)}, bf16[32,1664]{1,0:T(8,128)(2,1)S(1)}, u32[]{:S(2)}, u32[]{:S(2)}) collective-permute-start(bf16[32,1664]{1,0:T(8,128)(2,1)S(1)} %constant_dynamic-update-slice_fusion.2), channel_id=1, source_target_pairs={{0,16},{8,24},{16,0},{24,8},{1,17},{9,25},{17,1},{25,9},{2,18},{10... | collective-permute-start | bytes 319496 | tf_op jit(solution)/shard_map/ppermute | solution.py:150
  53.1 2.5 %window.1 = (f32[768,512]{1,0:T(8,128)S(1)}, f32[16,512]{1,0:T(8,128)S(1)}) custom-call(bf16[512,768]{1,0:T(8,128)(2,1)S(1)} %copy-done, bf16[512,768]{1,0:T(8,128)(2,1)S(1)} %copy-done.4, bf16[512,768]{1,0:T(8,128)(2,1)S(1)} %copy-done.3), custom_call_target="tpu_custom_call" | custom-call | flops 805306368 | bytes 3932160 | tf_op jit(solution)/shard_map/window/pallas_call | solution.py:151
  55.6 1.2 %copy-done.1 = f32[768,512]{1,0:T(8,128)} copy-done((f32[768,512]{1,0:T(8,128)}, f32[768,512]{1,0:T(8,128)S(1)}, u32[]{:S(2)}) %copy-start.1) | copy-done | bytes 1572888
  56.8 7.5 %all-to-all-done.1 = bf16[8,32,768]{2,1,0:T(8,128)(2,1)S(1)} async-done(((bf16[8,32,768]{2,1,0:T(8,128)(2,1)}), bf16[8,32,768]{2,1,0:T(8,128)(2,1)S(1)}, u32[]{:S(2)}, u32[]{:S(2)}) %all-to-all-start.1) | async-done | bytes 393248 | tf_op jit(solution)/shard_map/all_to_all | solution.py:146
  64.3 0.9 %broadcast_in_dim.30 = bf16[4,128,768]{2,1,0:T(8,128)(2,1)} broadcast(bf16[128,768]{1,0:T(8,128)(2,1)S(1)} %dynamic-slice_bitcast_fusion), dimensions={1,2} | broadcast | bytes 983040 | tf_op jit(solution)/shard_map/broadcast_in_dim | solution.py:166
  65.2 3.6 %all-to-all-start.2 = ((bf16[4,128,768]{2,1,0:T(8,128)(2,1)}), bf16[4,128,768]{2,1,0:T(8,128)(2,1)S(1)}, u32[]{:S(2)}, u32[]{:S(2)}) async-start(bf16[4,128,768]{2,1,0:T(8,128)(2,1)} %broadcast_in_dim.30), calls=%async_computation.2 | async-start | bytes 1572864 | tf_op jit(solution)/shard_map/all_to_all | solution.py:169
  68.9 2.5 %collective-permute-start.5 = (bf16[64,1664]{1,0:T(8,128)(2,1)S(1)}, bf16[64,1664]{1,0:T(8,128)(2,1)S(1)}, u32[]{:S(2)}, u32[]{:S(2)}) collective-permute-start(bf16[64,1664]{1,0:T(8,128)(2,1)S(1)} %pad_maximum_fusion.1), channel_id=1, source_target_pairs={{0,4},{4,0},{1,5},{5,1},{2,6},{6,2},{3,7},{7,3},{8,12},{12,8},{9,1... | collective-permute-start | bytes 638984 | tf_op jit(solution)/shard_map/ppermute | solution.py:171
  71.4 1.1 %collective-permute-done.5 = bf16[64,1664]{1,0:T(8,128)(2,1)S(1)} collective-permute-done((bf16[64,1664]{1,0:T(8,128)(2,1)S(1)}, bf16[64,1664]{1,0:T(8,128)(2,1)S(1)}, u32[]{:S(2)}, u32[]{:S(2)}) %collective-permute-start.5) | collective-permute-done | bytes 213024 | tf_op jit(solution)/shard_map/ppermute | solution.py:171
  72.5 1.4 %copy-done.2 = f32[768,512]{1,0:T(8,128)S(1)} copy-done((f32[768,512]{1,0:T(8,128)S(1)}, f32[768,512]{1,0:T(8,128)}, u32[]{:S(2)}) %copy-start.2) | copy-done | bytes 1572888
  73.9 2.2 %pooled.1 = (f32[768,512]{1,0:T(8,128)S(1)}, f32[16,512]{1,0:T(8,128)S(1)}) custom-call(s32[1]{0:T(128)S(6)} %copy.13.tag_ref, f32[6]{0:T(128)S(1)} %copy-done.6, bf16[512,768]{1,0:T(8,128)(2,1)S(1)} %copy-done, bf16[128,1664]{1,0:T(8,128)(2,1)S(1)} %pad_maximum_fusion.p_ref, f32[768,512]{1,0:T(8,128)S(1)} %copy-done.2, f32[16,512]{1,0:T(8,128)S(1)} %get-tuple-element.36.stat_ref), custom_call_target="tpu_custom_call" | custom-call | flops 201326592 | bytes 4718592 | tf_op jit(solution)/shard_map/pooled/pallas_call | solution.py:173
  76.1 4.4 %all-to-all-done.2 = bf16[4,128,768]{2,1,0:T(8,128)(2,1)S(1)} async-done(((bf16[4,128,768]{2,1,0:T(8,128)(2,1)}), bf16[4,128,768]{2,1,0:T(8,128)(2,1)S(1)}, u32[]{:S(2)}, u32[]{:S(2)}) %all-to-all-start.2) | async-done | bytes 786464 | tf_op jit(solution)/shard_map/all_to_all | solution.py:169
  80.6 3.4 %collective-permute-start.6 = (bf16[512,768]{1,0:T(8,128)(2,1)S(1)}, bf16[512,768]{1,0:T(8,128)(2,1)S(1)}, u32[]{:S(2)}, u32[]{:S(2)}) collective-permute-start(bf16[512,768]{1,0:T(8,128)(2,1)S(1)} %bitcast.18), channel_id=1, source_target_pairs={{0,4},{4,0},{1,5},{5,1},{2,6},{6,2},{3,7},{7,3},{8,12},{12,8},{9,1... | collective-permute-start | bytes 2359304 | tf_op jit(solution)/shard_map/ppermute | solution.py:188
  84.0 1.9 %collective-permute-done.6.got_ref = bf16[512,768]{1,0:T(8,128)(2,1)S(1)} collective-permute-done((bf16[512,768]{1,0:T(8,128)(2,1)S(1)}, bf16[512,768]{1,0:T(8,128)(2,1)S(1)}, u32[]{:S(2)}, u32[]{:S(2)}) %collective-permute-start.6) | collective-permute-done | bytes 786464 | tf_op jit(solution)/shard_map/ppermute | solution.py:188
  85.8 3.8 %far.1 = bf16[512,768]{1,0:T(8,128)(2,1)} custom-call(s32[1]{0:T(128)} %bitcast.core_ref, bf16[512,768]{1,0:T(8,128)(2,1)S(1)} %copy-done, bf16[512,768]{1,0:T(8,128)(2,1)S(1)} %bitcast.19, bf16[512,768]{1,0:T(8,128)(2,1)S(1)} %collective-permute-done.6.got_ref, f32[768,512]{1,0:T(8,128)S(1)} %get-tuple-element.39.acc_ref, ...), custom_call_target="tpu_custom_call" | custom-call | tf_op jit(solution)/shard_map/far/pallas_call | solution.py:189
  (24 shorter events, 0.2 us)
Async XLA Ops:
  0.0 14.9 %copy-start.5 = (s32[1,512]{1,0:T(1,128)S(1)}, s32[1,512]{1,0:T(1,128)}, u32[]{:S(2)}) copy-start(s32[1,512]{1,0:T(1,128)} %seg_ref.3) | copy-start | bytes 6148
  0.0 14.9 %copy-start.4 = (bf16[512,768]{1,0:T(8,128)(2,1)S(1)}, bf16[512,768]{1,0:T(8,128)(2,1)}, u32[]{:S(2)}) copy-start(bf16[512,768]{1,0:T(8,128)(2,1)} %k_ref.1) | copy-start | bytes 2359300
  0.0 15.3 %collective-permute-start.1 = (bf16[128,3072]{1,0:T(8,128)(2,1)}, bf16[128,3072]{1,0:T(8,128)(2,1)}, u32[]{:S(2)}, u32[]{:S(2)}) collective-permute-start(bf16[128,3072]{1,0:T(8,128)(2,1)} %bitcast.21), channel_id=1, source_target_pairs={{0,4},{1,5},{2,6},{3,7},{8,12},{9,13},{10,14},{11,15},{16,20},{17,... | collective-permute-start | bytes 2359304 | tf_op jit(solution)/shard_map/ppermute | solution.py:119
  1.4 13.9 %collective-permute-start = (bf16[128,3072]{1,0:T(8,128)(2,1)}, bf16[128,3072]{1,0:T(8,128)(2,1)}, u32[]{:S(2)}, u32[]{:S(2)}) collective-permute-start(bf16[128,3072]{1,0:T(8,128)(2,1)} %bitcast.22), channel_id=1, source_target_pairs={{4,0},{5,1},{6,2},{7,3},{12,8},{13,9},{14,10},{15,11},{20,16},{21,... | collective-permute-start | bytes 2359304 | tf_op jit(solution)/shard_map/ppermute | solution.py:118
  12.0 3.1 %copy-start.3 = (bf16[512,768]{1,0:T(8,128)(2,1)S(1)}, bf16[512,768]{1,0:T(8,128)(2,1)}, u32[]{:S(2)}) copy-start(bf16[512,768]{1,0:T(8,128)(2,1)} %v_ref.1) | copy-start | bytes 2359300
  17.5 20.9 %all-to-all-start = ((bf16[4,32,3072]{2,1,0:T(8,128)(2,1)}), bf16[4,32,3072]{2,1,0:T(8,128)(2,1)S(1)}, u32[]{:S(2)}, u32[]{:S(2)}) async-start(bf16[4,32,3072]{2,1,0:T(8,128)(2,1)} %bitcast.5), calls=%async_computation | async-start | bytes 1572864 | tf_op jit(solution)/shard_map/all_to_all | solution.py:137
  21.0 32.1 %copy-start = (bf16[512,768]{1,0:T(8,128)(2,1)S(1)}, bf16[512,768]{1,0:T(8,128)(2,1)}, u32[]{:S(2)}) copy-start(bf16[512,768]{1,0:T(8,128)(2,1)} %q_ref.4) | copy-start | bytes 2359300
  21.1 10.7 %collective-permute-start.2 = (bf16[8,1664]{1,0:T(8,128)(2,1)S(1)}, bf16[8,1664]{1,0:T(8,128)(2,1)S(1)}, u32[]{:S(2)}, u32[]{:S(2)}) collective-permute-start(bf16[8,1664]{1,0:T(8,128)(2,1)S(1)} %maximum_maximum_fusion), channel_id=1, source_target_pairs={{0,8},{8,0},{16,24},{24,16},{1,9},{9,1},{17,25},{25,17},{2,10},{10... | collective-permute-start | bytes 79880 | tf_op jit(solution)/shard_map/ppermute | solution.py:138
  31.8 9.5 %collective-permute-start.3 = (bf16[16,1664]{1,0:T(8,128)(2,1)S(1)}, bf16[16,1664]{1,0:T(8,128)(2,1)S(1)}, u32[]{:S(2)}, u32[]{:S(2)}) collective-permute-start(bf16[16,1664]{1,0:T(8,128)(2,1)S(1)} %constant_dynamic-update-slice_fusion), channel_id=1, source_target_pairs={{0,32},{32,0},{1,33},{33,1},{2,34},{34,2},{3,35},{35,3},{4,36},{36... | collective-permute-start | bytes 159752 | tf_op jit(solution)/shard_map/ppermute | solution.py:140
  42.0 22.2 %all-to-all-start.1 = ((bf16[8,32,768]{2,1,0:T(8,128)(2,1)}), bf16[8,32,768]{2,1,0:T(8,128)(2,1)S(1)}, u32[]{:S(2)}, u32[]{:S(2)}) async-start(bf16[8,32,768]{2,1,0:T(8,128)(2,1)} %bitcast.7), calls=%async_computation.1 | async-start | bytes 786432 | tf_op jit(solution)/shard_map/all_to_all | solution.py:146
  49.2 15.0 %collective-permute-start.4 = (bf16[32,1664]{1,0:T(8,128)(2,1)S(1)}, bf16[32,1664]{1,0:T(8,128)(2,1)S(1)}, u32[]{:S(2)}, u32[]{:S(2)}) collective-permute-start(bf16[32,1664]{1,0:T(8,128)(2,1)S(1)} %constant_dynamic-update-slice_fusion.2), channel_id=1, source_target_pairs={{0,16},{8,24},{16,0},{24,8},{1,17},{9,25},{17,1},{25,9},{2,18},{10... | collective-permute-start | bytes 319496 | tf_op jit(solution)/shard_map/ppermute | solution.py:150
  55.6 1.2 %copy-start.1 = (f32[768,512]{1,0:T(8,128)}, f32[768,512]{1,0:T(8,128)S(1)}, u32[]{:S(2)}) copy-start(f32[768,512]{1,0:T(8,128)S(1)} %get-tuple-element.35.acc_ref) | copy-start | bytes 4718596
  65.2 7.3 %copy-start.6 = (f32[6]{0:T(128)S(1)}, f32[6]{0:T(128)}, u32[]{:S(2)}) copy-start(f32[6]{0:T(128)} %slope_ref.1) | copy-start | bytes 76
  65.2 15.4 %all-to-all-start.2 = ((bf16[4,128,768]{2,1,0:T(8,128)(2,1)}), bf16[4,128,768]{2,1,0:T(8,128)(2,1)S(1)}, u32[]{:S(2)}, u32[]{:S(2)}) async-start(bf16[4,128,768]{2,1,0:T(8,128)(2,1)} %broadcast_in_dim.30), calls=%async_computation.2 | async-start | bytes 1572864 | tf_op jit(solution)/shard_map/all_to_all | solution.py:169
  68.9 3.6 %collective-permute-start.5 = (bf16[64,1664]{1,0:T(8,128)(2,1)S(1)}, bf16[64,1664]{1,0:T(8,128)(2,1)S(1)}, u32[]{:S(2)}, u32[]{:S(2)}) collective-permute-start(bf16[64,1664]{1,0:T(8,128)(2,1)S(1)} %pad_maximum_fusion.1), channel_id=1, source_target_pairs={{0,4},{4,0},{1,5},{5,1},{2,6},{6,2},{3,7},{7,3},{8,12},{12,8},{9,1... | collective-permute-start | bytes 638984 | tf_op jit(solution)/shard_map/ppermute | solution.py:171
  72.5 1.4 %copy-start.2 = (f32[768,512]{1,0:T(8,128)S(1)}, f32[768,512]{1,0:T(8,128)}, u32[]{:S(2)}) copy-start(f32[768,512]{1,0:T(8,128)} %copy-done.1) | copy-start | bytes 4718596
  80.6 5.3 %collective-permute-start.6 = (bf16[512,768]{1,0:T(8,128)(2,1)S(1)}, bf16[512,768]{1,0:T(8,128)(2,1)S(1)}, u32[]{:S(2)}, u32[]{:S(2)}) collective-permute-start(bf16[512,768]{1,0:T(8,128)(2,1)S(1)} %bitcast.18), channel_id=1, source_target_pairs={{0,4},{4,0},{1,5},{5,1},{2,6},{6,2},{3,7},{7,3},{8,12},{12,8},{9,1... | collective-permute-start | bytes 2359304 | tf_op jit(solution)/shard_map/ppermute | solution.py:188

commit v6 on v4

--- a/solution.py
+++ b/solution.py
@@ -131,10 +131,20 @@
         name="pool",
     )(window_map, pool_segments, keys, values)
     mine = jnp.where(owner_c == core, kept, jnp.where(core == 0, got_k, got_v))
-    mine, pooled, queries_w = tie((mine, pooled, queries))
+    mine, pooled = tie((mine, pooled))
 
     spread = lax.all_to_all(mine.reshape(n_x, part, -1), "x", 0, 0, tiled=True)
     other = lax.ppermute(pooled, "zh", SWAP)
+    piece = lax.dynamic_index_in_dim(spread, owner_x, 0, keepdims=False)
+    piece = piece.reshape(part, n_head, width).transpose(1, 0, 2)
+    piece = jnp.broadcast_to(piece[None], (n_zh, n_head, part, width))
+    piece, pooled, other, queries_w = tie((piece, pooled, other, queries))
+
+    turned = lax.all_to_all(
+        piece.reshape(n_zh * n_head, part, width), ("zh", "head"), 0, 0, tiled=True
+    )
+    pooled = jnp.concatenate([pooled, other], axis=0)
+    other = lax.ppermute(pooled, "x", [(i, i ^ 1) for i in range(n_x)])
     acc_w, stat_w = pl.pallas_call(
         window_kernel,
         out_shape=state,
@@ -150,21 +160,10 @@
     )(queries_w, keys, values)
     other, stat_w = tie((other, stat_w))
     pooled = jnp.concatenate([pooled, other], axis=0)
-    other = lax.ppermute(pooled, "x", [(i, i ^ 1) for i in range(n_x)])
-    piece = lax.dynamic_index_in_dim(spread, owner_x, 0, keepdims=False)
-    piece = piece.reshape(part, n_head, width).transpose(1, 0, 2)
-    piece = jnp.broadcast_to(piece[None], (n_zh, n_head, part, width))
-    piece, pooled, other = tie((piece, pooled, other))
-
-    turned = lax.all_to_all(
-        piece.reshape(n_zh * n_head, part, width), ("zh", "head"), 0, 0, tiled=True
-    )
-    pooled = jnp.concatenate([pooled, other], axis=0)
-    other = lax.ppermute(pooled, "x", [(i, i ^ 2) for i in range(n_x)])
     turned = turned.reshape(n_zh, n_head * part, width)
     block = lax.dynamic_index_in_dim(turned, owner_z, 0, keepdims=False)
     block = jnp.broadcast_to(block[None], (n_x, n_head * part, width))
-    block, pooled, other = tie((block, pooled, other))
+    other = lax.ppermute(pooled, "x", [(i, i ^ 2) for i in range(n_x)])
 
     own = lax.all_to_all(block, "x", 0, 0, tiled=True).reshape(-1, width)
     pooled = jnp.concatenate([pooled, other], axis=0)

time: 78.2 us -> 77.6 us (level)
  starting transfers between devices: 47.2 us -> 42.4 us
  local copies, waits for them, and re-layouts: 5.43 us -> 7.25 us
  other arithmetic: 2.5 us -> 3.7 us
  waiting for transfers between devices: 12 us -> 13.2 us
    all_to_all x1, waiting for transfers between devices: 0.01 us -> 5.58 us  [on_device(): spread = lax.all_to_all(mine.reshape(n_x, part, -1), 'x', 0, 0, tiled=True)]
    all_to_all x1, waiting for transfers between devices: 8.1 us -> 4.54 us  [on_device(): lax.all_to_all(piece.reshape(n_zh * n_head, part, width), ('zh', 'head'),...]
    ppermute x1, starting transfers between devices: 4.76 us -> 2.86 us  [on_device(): got = lax.ppermute(own, 'c', SWAP)]
    unnamed x16 -> x22, local copies, waits for them, and re-layouts: 2.59 us -> 4.42 us
    select_n x1, other arithmetic: 1 us -> 2.21 us  [on_device(): mine = jnp.where(owner_c == core, kept, jnp.where(core == 0, got_k, got_v))]
    ppermute x1, starting transfers between devices: 3.26 us -> 2.2 us  [on_device(): other = lax.ppermute(pooled, 'x', [(i, i ^ 1) for i in range(n_x)])]
    dynamic_slice x1, local copies, waits for them, and re-layouts: 0.95 us -> 0.01 us  [on_device(): piece = lax.dynamic_index_in_dim(spread, owner_x, 0, keepdims=False)]
    broadcast_in_dim x2, local copies, waits for them, and re-layouts: 0.94 us -> 1.87 us  [on_device(): block = jnp.broadcast_to(block[None], (n_x, n_head * part, width))]
  transfers between devices with their start and end apart: 10 -> 10, of which waited for: 4 -> 5; matrix products, arithmetic and copies ran while one was open for 3% -> 5% of each run, Pallas kernels for 6% -> 7%
where the time goes in v6:
time: 77.6 us; the launch traced here: 77 us
  starting transfers between devices  42.4 us (55%)
  waiting for transfers between devices  13.2 us (17%)
  Pallas kernels  8.83 us (11%)
  local copies, waits for them, and re-layouts  7.25 us (9%)
  other arithmetic  3.7 us (5%)
  between operations  1.61 us (2%)
    ppermute x1, starting transfers between devices, on_device(): got_k = lax.ppermute(slot_k, 'c', [(1, 0)])  8.95 us
    ppermute x1, starting transfers between devices, on_device(): other = lax.ppermute(pooled, 'zh', SWAP)  5.84 us
    ppermute x1, starting transfers between devices, on_device(): other = lax.ppermute(pooled, 'c', SWAP)  5.69 us
    all_to_all x1, waiting for transfers between devices, on_device(): spread = lax.all_to_all(mine.reshape(n_x, part, -1), 'x', 0, 0, tiled=True)  5.58 us
    all_to_all x1, starting transfers between devices, on_device(): lax.all_to_all(piece.reshape(n_zh * n_head, part, width), ('zh', 'head'),...  4.93 us
    all_to_all x1, waiting for transfers between devices, on_device(): lax.all_to_all(piece.reshape(n_zh * n_head, part, width), ('zh', 'head'),...  4.54 us
    unnamed x22, local copies, waits for them, and re-layouts  4.42 us
    pallas_call x1, Pallas kernels, on_device(): pl.pallas_call(ref_kernel, out_shape=jax.ShapeDtypeStruct((rows, width),...  3.8 us
  transfers between devices with their start and end apart: 10, of which 5 were waited for; matrix products, arithmetic and copies ran while one was open for 5% of the time, Pallas kernels for 7%

profile of v6, /device:TPU:1, one launch (start us, length us, event | category | flops | bytes accessed | tf_op | source)
XLA Modules:
  0.0 77.0 jit_solution(13714486941705298406)
XLA Ops:
  0.0 8.9 %collective-permute-start = (bf16[128,3072]{1,0:T(8,128)(2,1)}, bf16[128,3072]{1,0:T(8,128)(2,1)S(1)}, u32[]{:S(2)}, u32[]{:S(2)}) collective-permute-start(bf16[128,3072]{1,0:T(8,128)(2,1)} %bitcast.19), channel_id=1, source_target_pairs={{4,0},{5,1},{6,2},{7,3},{12,8},{13,9},{14,10},{15,11},{20,16},{21,... | collective-permute-start | bytes 2359304 | tf_op jit(solution)/shard_map/ppermute | solution.py:122
  9.0 1.3 %collective-permute-start.1 = (bf16[128,3072]{1,0:T(8,128)(2,1)}, bf16[128,3072]{1,0:T(8,128)(2,1)}, u32[]{:S(2)}, u32[]{:S(2)}) collective-permute-start(bf16[128,3072]{1,0:T(8,128)(2,1)} %bitcast.20), channel_id=1, source_target_pairs={{0,4},{1,5},{2,6},{3,7},{8,12},{9,13},{10,14},{11,15},{16,20},{17,... | collective-permute-start | bytes 2359304 | tf_op jit(solution)/shard_map/ppermute | solution.py:123
  10.9 1.5 %broadcast_select_fusion = bf16[128,3072]{1,0:T(8,128)(2,1)S(1)} fusion(pred[]{:T(512)S(6)} %eq.11, bf16[1,128,3072]{2,1,0:T(8,128)(2,1)} %param.16, bf16[1,128,3072]{2,1,0:T(8,128)(2,1)} %param.15), kind=kLoop, calls=%fused_computation.1 | loop fusion | flops 393216 | bytes 2359297 | tf_op jit(solution)/shard_map/jit(_where)/select_n | solution.py:124
  13.1 0.3 pool.1
  13.4 0.0 collective-permute-done
  13.4 0.1 collective-permute-done.1
  13.5 2.2 %select_select_fusion = bf16[128,3072]{1,0:T(8,128)(2,1)} fusion(bf16[128,3072]{1,0:T(8,128)(2,1)S(1)} %broadcast_select_fusion, bf16[128,3072]{1,0:T(8,128)(2,1)S(1)} %collective-permute-done, bf16[128,3072]{1,0:T(8,128)(2,1)} %collective-permute-done.1, pred[]{:T(512)S(6)} %eq.11, pred[]{:T(512)S(6)} %eq.10), kind=kLoop, calls=%fused_computation | loop fusion | flops 786432 | bytes 3145730 | tf_op jit(solution)/shard_map/jit(_where)/select_n | solution.py:133
  15.7 3.5 %all-to-all-start = ((bf16[4,32,3072]{2,1,0:T(8,128)(2,1)}), bf16[4,32,3072]{2,1,0:T(8,128)(2,1)S(1)}, u32[]{:S(2)}, u32[]{:S(2)}) async-start(bf16[4,32,3072]{2,1,0:T(8,128)(2,1)} %bitcast.4), calls=%async_computation | async-start | bytes 1572864 | tf_op jit(solution)/shard_map/all_to_all | solution.py:136
  19.2 0.0 copy-start
  19.3 5.8 %collective-permute-start.2 = (bf16[8,1664]{1,0:T(8,128)(2,1)S(1)}, bf16[8,1664]{1,0:T(8,128)(2,1)S(1)}, u32[]{:S(2)}, u32[]{:S(2)}) collective-permute-start(bf16[8,1664]{1,0:T(8,128)(2,1)S(1)} %pool.1), channel_id=1, source_target_pairs={{0,32},{32,0},{1,33},{33,1},{2,34},{34,2},{3,35},{35,3},{4,36},{36... | collective-permute-start | bytes 79880 | tf_op jit(solution)/shard_map/ppermute | solution.py:137
  25.1 5.6 %all-to-all-done = bf16[4,32,3072]{2,1,0:T(8,128)(2,1)S(1)} async-done(((bf16[4,32,3072]{2,1,0:T(8,128)(2,1)}), bf16[4,32,3072]{2,1,0:T(8,128)(2,1)S(1)}, u32[]{:S(2)}, u32[]{:S(2)}) %all-to-all-start) | async-done | bytes 786464 | tf_op jit(solution)/shard_map/all_to_all | solution.py:136
  30.7 0.1 reshape.18
  30.9 0.8 %broadcast_in_dim.18 = bf16[2,4,32,768]{3,2,1,0:T(8,128)(2,1)} broadcast(bf16[4,32,768]{2,1,0:T(8,128)(2,1)S(1)} %copy.10), dimensions={1,2,3} | broadcast | bytes 589824 | tf_op jit(solution)/shard_map/broadcast_in_dim | solution.py:140
  31.7 2.2 %collective-permute-start.3 = (bf16[16,1664]{1,0:T(8,128)(2,1)S(1)}, bf16[16,1664]{1,0:T(8,128)(2,1)S(1)}, u32[]{:S(2)}, u32[]{:S(2)}) collective-permute-start(bf16[16,1664]{1,0:T(8,128)(2,1)S(1)} %pad_maximum_fusion.2), channel_id=1, source_target_pairs={{0,8},{8,0},{16,24},{24,16},{1,9},{9,1},{17,25},{25,17},{2,10},{10... | collective-permute-start | bytes 159752 | tf_op jit(solution)/shard_map/ppermute | solution.py:147
  33.9 4.9 %all-to-all-start.1 = ((bf16[8,32,768]{2,1,0:T(8,128)(2,1)}), bf16[8,32,768]{2,1,0:T(8,128)(2,1)}, u32[]{:S(2)}, u32[]{:S(2)}) async-start(bf16[8,32,768]{2,1,0:T(8,128)(2,1)} %bitcast.6), calls=%async_computation.1 | async-start | bytes 786432 | tf_op jit(solution)/shard_map/all_to_all | solution.py:143
  38.8 2.5 %window.1 = (f32[768,512]{1,0:T(8,128)S(1)}, f32[16,512]{1,0:T(8,128)S(1)}) custom-call(bf16[512,768]{1,0:T(8,128)(2,1)S(1)} %copy-done, bf16[512,768]{1,0:T(8,128)(2,1)S(1)} %copy-done.3, bf16[512,768]{1,0:T(8,128)(2,1)S(1)} %copy-done.4), custom_call_target="tpu_custom_call" | custom-call | flops 805306368 | bytes 3932160 | tf_op jit(solution)/shard_map/window/pallas_call | solution.py:148
  41.3 1.2 %copy-done.1 = f32[768,512]{1,0:T(8,128)} copy-done((f32[768,512]{1,0:T(8,128)}, f32[768,512]{1,0:T(8,128)S(1)}, u32[]{:S(2)}) %copy-start.1) | copy-done | bytes 1572888
  42.5 3.7 %collective-permute-start.4 = (bf16[32,1664]{1,0:T(8,128)(2,1)S(1)}, bf16[32,1664]{1,0:T(8,128)(2,1)S(1)}, u32[]{:S(2)}, u32[]{:S(2)}) collective-permute-start(bf16[32,1664]{1,0:T(8,128)(2,1)S(1)} %pad_maximum_fusion.1), channel_id=1, source_target_pairs={{0,16},{8,24},{16,0},{24,8},{1,17},{9,25},{17,1},{25,9},{2,18},{10... | collective-permute-start | bytes 319496 | tf_op jit(solution)/shard_map/ppermute | solution.py:166
  46.2 4.5 %all-to-all-done.1 = bf16[8,32,768]{2,1,0:T(8,128)(2,1)} async-done(((bf16[8,32,768]{2,1,0:T(8,128)(2,1)}), bf16[8,32,768]{2,1,0:T(8,128)(2,1)}, u32[]{:S(2)}, u32[]{:S(2)}) %all-to-all-start.1) | async-done | bytes 393248 | tf_op jit(solution)/shard_map/all_to_all | solution.py:143
  50.8 0.9 %dynamic-slice_bitcast_fusion = bf16[128,768]{1,0:T(8,128)(2,1)S(1)} fusion(bf16[2,128,768]{2,1,0:T(8,128)(2,1)} %bitcast.7, s32[]{:T(128)S(6)} %select_n.54), kind=kLoop, calls=%fused_computation.3 | loop fusion | bytes 393220 | tf_op jit(solution)/shard_map/broadcast_in_dim | solution.py:165
  51.7 0.0 copy-start.8
  51.7 0.9 %broadcast_in_dim.20 = bf16[4,128,768]{2,1,0:T(8,128)(2,1)} broadcast(bf16[128,768]{1,0:T(8,128)(2,1)S(1)} %dynamic-slice_bitcast_fusion), dimensions={1,2} | broadcast | bytes 983040 | tf_op jit(solution)/shard_map/broadcast_in_dim | solution.py:165
  52.7 3.5 %all-to-all-start.2 = ((bf16[4,128,768]{2,1,0:T(8,128)(2,1)}), bf16[4,128,768]{2,1,0:T(8,128)(2,1)S(1)}, u32[]{:S(2)}, u32[]{:S(2)}) async-start(bf16[4,128,768]{2,1,0:T(8,128)(2,1)} %broadcast_in_dim.20), calls=%async_computation.2 | async-start | bytes 1572864 | tf_op jit(solution)/shard_map/all_to_all | solution.py:168
  56.2 5.7 %collective-permute-start.5 = (bf16[64,1664]{1,0:T(8,128)(2,1)S(1)}, bf16[64,1664]{1,0:T(8,128)(2,1)S(1)}, u32[]{:S(2)}, u32[]{:S(2)}) collective-permute-start(bf16[64,1664]{1,0:T(8,128)(2,1)S(1)} %pad_maximum_fusion), channel_id=1, source_target_pairs={{0,4},{4,0},{1,5},{5,1},{2,6},{6,2},{3,7},{7,3},{8,12},{12,8},{9,1... | collective-permute-start | bytes 638984 | tf_op jit(solution)/shard_map/ppermute | solution.py:170
  61.9 1.0 %collective-permute-done.5 = bf16[64,1664]{1,0:T(8,128)(2,1)S(1)} collective-permute-done((bf16[64,1664]{1,0:T(8,128)(2,1)S(1)}, bf16[64,1664]{1,0:T(8,128)(2,1)S(1)}, u32[]{:S(2)}, u32[]{:S(2)}) %collective-permute-start.5) | collective-permute-done | bytes 213024 | tf_op jit(solution)/shard_map/ppermute | solution.py:170
  63.0 0.8 %copy-done.5 = bf16[128,1664]{1,0:T(8,128)(2,1)} copy-done((bf16[128,1664]{1,0:T(8,128)(2,1)}, bf16[128,1664]{1,0:T(8,128)(2,1)S(1)}, u32[]{:S(2)}) %copy-start.5) | copy-done | bytes 426008
  63.8 1.4 %copy-done.2 = f32[768,512]{1,0:T(8,128)S(1)} copy-done((f32[768,512]{1,0:T(8,128)S(1)}, f32[768,512]{1,0:T(8,128)}, u32[]{:S(2)}) %copy-start.2) | copy-done | bytes 1572888
  65.2 1.0 %copy-done.6 = bf16[128,1664]{1,0:T(8,128)(2,1)S(1)} copy-done((bf16[128,1664]{1,0:T(8,128)(2,1)S(1)}, bf16[128,1664]{1,0:T(8,128)(2,1)}, u32[]{:S(2)}) %copy-start.6) | copy-done | bytes 426008
  66.2 2.2 %pooled.1 = (f32[768,512]{1,0:T(8,128)S(1)}, f32[16,512]{1,0:T(8,128)S(1)}) custom-call(s32[1]{0:T(128)S(6)} %copy.15.tag_ref, f32[6]{0:T(128)S(1)} %copy-done.8, bf16[512,768]{1,0:T(8,128)(2,1)S(1)} %copy-done, bf16[128,1664]{1,0:T(8,128)(2,1)S(1)} %copy-done.6, f32[768,512]{1,0:T(8,128)S(1)} %copy-done.2, f32[16,512]{1,0:T(8,128)S(1)} %get-tuple-element.28.stat_ref), custom_call_target="tpu_custom_call" | custom-call | flops 201326592 | bytes 4718592 | tf_op jit(solution)/shard_map/pooled/pallas_call | solution.py:172
  68.4 2.9 %collective-permute-start.6 = (bf16[512,768]{1,0:T(8,128)(2,1)S(1)}, bf16[512,768]{1,0:T(8,128)(2,1)S(1)}, u32[]{:S(2)}, u32[]{:S(2)}) collective-permute-start(bf16[512,768]{1,0:T(8,128)(2,1)S(1)} %bitcast.17), channel_id=1, source_target_pairs={{0,4},{4,0},{1,5},{5,1},{2,6},{6,2},{3,7},{7,3},{8,12},{12,8},{9,1... | collective-permute-start | bytes 2359304 | tf_op jit(solution)/shard_map/ppermute | solution.py:187
  71.3 1.9 %collective-permute-done.6.got_ref = bf16[512,768]{1,0:T(8,128)(2,1)S(1)} collective-permute-done((bf16[512,768]{1,0:T(8,128)(2,1)S(1)}, bf16[512,768]{1,0:T(8,128)(2,1)S(1)}, u32[]{:S(2)}, u32[]{:S(2)}) %collective-permute-start.6) | collective-permute-done | bytes 786464 | tf_op jit(solution)/shard_map/ppermute | solution.py:187
  73.2 3.8 %far.1 = bf16[512,768]{1,0:T(8,128)(2,1)} custom-call(s32[1]{0:T(128)} %bitcast.core_ref, bf16[512,768]{1,0:T(8,128)(2,1)S(1)} %copy-done, bf16[512,768]{1,0:T(8,128)(2,1)S(1)} %bitcast.18, bf16[512,768]{1,0:T(8,128)(2,1)S(1)} %collective-permute-done.6.got_ref, f32[768,512]{1,0:T(8,128)S(1)} %get-tuple-element.31.acc_ref, ...), custom_call_target="tpu_custom_call" | custom-call | tf_op jit(solution)/shard_map/far/pallas_call | solution.py:188
  (26 shorter events, 0.2 us)
Async XLA Ops:
  0.0 13.0 %copy-start.3 = (bf16[512,768]{1,0:T(8,128)(2,1)S(1)}, bf16[512,768]{1,0:T(8,128)(2,1)}, u32[]{:S(2)}) copy-start(bf16[512,768]{1,0:T(8,128)(2,1)} %k_ref.1) | copy-start | bytes 2359300
  0.0 13.1 %copy-start.4 = (bf16[512,768]{1,0:T(8,128)(2,1)S(1)}, bf16[512,768]{1,0:T(8,128)(2,1)}, u32[]{:S(2)}) copy-start(bf16[512,768]{1,0:T(8,128)(2,1)} %v_ref.1) | copy-start | bytes 2359300
  0.0 13.1 %copy-start.7 = (s32[1,512]{1,0:T(1,128)S(1)}, s32[1,512]{1,0:T(1,128)}, u32[]{:S(2)}) copy-start(s32[1,512]{1,0:T(1,128)} %seg_ref.1) | copy-start | bytes 6148
  0.0 13.4 %collective-permute-start = (bf16[128,3072]{1,0:T(8,128)(2,1)}, bf16[128,3072]{1,0:T(8,128)(2,1)S(1)}, u32[]{:S(2)}, u32[]{:S(2)}) collective-permute-start(bf16[128,3072]{1,0:T(8,128)(2,1)} %bitcast.19), channel_id=1, source_target_pairs={{4,0},{5,1},{6,2},{7,3},{12,8},{13,9},{14,10},{15,11},{20,16},{21,... | collective-permute-start | bytes 2359304 | tf_op jit(solution)/shard_map/ppermute | solution.py:122
  9.0 4.5 %collective-permute-start.1 = (bf16[128,3072]{1,0:T(8,128)(2,1)}, bf16[128,3072]{1,0:T(8,128)(2,1)}, u32[]{:S(2)}, u32[]{:S(2)}) collective-permute-start(bf16[128,3072]{1,0:T(8,128)(2,1)} %bitcast.20), channel_id=1, source_target_pairs={{0,4},{1,5},{2,6},{3,7},{8,12},{9,13},{10,14},{11,15},{16,20},{17,... | collective-permute-start | bytes 2359304 | tf_op jit(solution)/shard_map/ppermute | solution.py:123
  15.7 15.0 %all-to-all-start = ((bf16[4,32,3072]{2,1,0:T(8,128)(2,1)}), bf16[4,32,3072]{2,1,0:T(8,128)(2,1)S(1)}, u32[]{:S(2)}, u32[]{:S(2)}) async-start(bf16[4,32,3072]{2,1,0:T(8,128)(2,1)} %bitcast.4), calls=%async_computation | async-start | bytes 1572864 | tf_op jit(solution)/shard_map/all_to_all | solution.py:136
  19.2 19.6 %copy-start = (bf16[512,768]{1,0:T(8,128)(2,1)S(1)}, bf16[512,768]{1,0:T(8,128)(2,1)}, u32[]{:S(2)}) copy-start(bf16[512,768]{1,0:T(8,128)(2,1)} %q_ref.4) | copy-start | bytes 2359300
  19.3 11.6 %collective-permute-start.2 = (bf16[8,1664]{1,0:T(8,128)(2,1)S(1)}, bf16[8,1664]{1,0:T(8,128)(2,1)S(1)}, u32[]{:S(2)}, u32[]{:S(2)}) collective-permute-start(bf16[8,1664]{1,0:T(8,128)(2,1)S(1)} %pool.1), channel_id=1, source_target_pairs={{0,32},{32,0},{1,33},{33,1},{2,34},{34,2},{3,35},{35,3},{4,36},{36... | collective-permute-start | bytes 79880 | tf_op jit(solution)/shard_map/ppermute | solution.py:137
  31.7 10.8 %collective-permute-start.3 = (bf16[16,1664]{1,0:T(8,128)(2,1)S(1)}, bf16[16,1664]{1,0:T(8,128)(2,1)S(1)}, u32[]{:S(2)}, u32[]{:S(2)}) collective-permute-start(bf16[16,1664]{1,0:T(8,128)(2,1)S(1)} %pad_maximum_fusion.2), channel_id=1, source_target_pairs={{0,8},{8,0},{16,24},{24,16},{1,9},{9,1},{17,25},{25,17},{2,10},{10... | collective-permute-start | bytes 159752 | tf_op jit(solution)/shard_map/ppermute | solution.py:147
  33.9 16.9 %all-to-all-start.1 = ((bf16[8,32,768]{2,1,0:T(8,128)(2,1)}), bf16[8,32,768]{2,1,0:T(8,128)(2,1)}, u32[]{:S(2)}, u32[]{:S(2)}) async-start(bf16[8,32,768]{2,1,0:T(8,128)(2,1)} %bitcast.6), calls=%async_computation.1 | async-start | bytes 786432 | tf_op jit(solution)/shard_map/all_to_all | solution.py:143
  41.3 1.2 %copy-start.1 = (f32[768,512]{1,0:T(8,128)}, f32[768,512]{1,0:T(8,128)S(1)}, u32[]{:S(2)}) copy-start(f32[768,512]{1,0:T(8,128)S(1)} %get-tuple-element.27.acc_ref) | copy-start | bytes 4718596
  42.5 13.7 %collective-permute-start.4 = (bf16[32,1664]{1,0:T(8,128)(2,1)S(1)}, bf16[32,1664]{1,0:T(8,128)(2,1)S(1)}, u32[]{:S(2)}, u32[]{:S(2)}) collective-permute-start(bf16[32,1664]{1,0:T(8,128)(2,1)S(1)} %pad_maximum_fusion.1), channel_id=1, source_target_pairs={{0,16},{8,24},{16,0},{24,8},{1,17},{9,25},{17,1},{25,9},{2,18},{10... | collective-permute-start | bytes 319496 | tf_op jit(solution)/shard_map/ppermute | solution.py:166
  51.7 12.1 %copy-start.8 = (f32[6]{0:T(128)S(1)}, f32[6]{0:T(128)}, u32[]{:S(2)}) copy-start(f32[6]{0:T(128)} %slope_ref.1) | copy-start | bytes 76
  52.7 15.8 %all-to-all-start.2 = ((bf16[4,128,768]{2,1,0:T(8,128)(2,1)}), bf16[4,128,768]{2,1,0:T(8,128)(2,1)S(1)}, u32[]{:S(2)}, u32[]{:S(2)}) async-start(bf16[4,128,768]{2,1,0:T(8,128)(2,1)} %broadcast_in_dim.20), calls=%async_computation.2 | async-start | bytes 1572864 | tf_op jit(solution)/shard_map/all_to_all | solution.py:168
  56.2 6.8 %collective-permute-start.5 = (bf16[64,1664]{1,0:T(8,128)(2,1)S(1)}, bf16[64,1664]{1,0:T(8,128)(2,1)S(1)}, u32[]{:S(2)}, u32[]{:S(2)}) collective-permute-start(bf16[64,1664]{1,0:T(8,128)(2,1)S(1)} %pad_maximum_fusion), channel_id=1, source_target_pairs={{0,4},{4,0},{1,5},{5,1},{2,6},{6,2},{3,7},{7,3},{8,12},{12,8},{9,1... | collective-permute-start | bytes 638984 | tf_op jit(solution)/shard_map/ppermute | solution.py:170
  63.0 0.8 %copy-start.5 = (bf16[128,1664]{1,0:T(8,128)(2,1)}, bf16[128,1664]{1,0:T(8,128)(2,1)S(1)}, u32[]{:S(2)}) copy-start(bf16[128,1664]{1,0:T(8,128)(2,1)S(1)} %constant_dynamic-update-slice_fusion.p_ref) | copy-start | bytes 1277956
  63.8 1.4 %copy-start.2 = (f32[768,512]{1,0:T(8,128)S(1)}, f32[768,512]{1,0:T(8,128)}, u32[]{:S(2)}) copy-start(f32[768,512]{1,0:T(8,128)} %copy-done.1) | copy-start | bytes 4718596
  65.2 1.0 %copy-start.6 = (bf16[128,1664]{1,0:T(8,128)(2,1)S(1)}, bf16[128,1664]{1,0:T(8,128)(2,1)}, u32[]{:S(2)}) copy-start(bf16[128,1664]{1,0:T(8,128)(2,1)} %copy-done.5) | copy-start | bytes 1277956
  68.4 4.8 %collective-permute-start.6 = (bf16[512,768]{1,0:T(8,128)(2,1)S(1)}, bf16[512,768]{1,0:T(8,128)(2,1)S(1)}, u32[]{:S(2)}, u32[]{:S(2)}) collective-permute-start(bf16[512,768]{1,0:T(8,128)(2,1)S(1)} %bitcast.17), channel_id=1, source_target_pairs={{0,4},{4,0},{1,5},{5,1},{2,6},{6,2},{3,7},{7,3},{8,12},{12,8},{9,1... | collective-permute-start | bytes 2359304 | tf_op jit(solution)/shard_map/ppermute | solution.py:187

commit v7 on v6

--- a/solution.py
+++ b/solution.py
@@ -54,17 +54,22 @@
 
 
 def pooled_kernel(
-    tag_ref, slope_ref, q_ref, p_ref, acc_ref, stat_ref, acc_out_ref, stat_out_ref
+    tag_ref, slope_ref, q_ref, pa_ref, pb_ref, acc_ref, stat_ref, acc_out_ref, stat_out_ref
 ):
     count, width = q_ref.shape
-    tags = p_ref[:, 2 * width :].astype(jnp.float32)
+
+    def both(first):
+        cols = pl.ds(first, HD)
+        return jnp.concatenate([pa_ref[:, cols], pb_ref[:, cols]], axis=0)
+
+    tags = both(2 * width).astype(jnp.float32)
     dist = jnp.abs(tags - tag_ref[0].astype(jnp.float32)) * LOG2E
     dist = jnp.concatenate([dist] * (count // HD), axis=1)
     for head in range(width // HD):
         cols = pl.ds(head * HD, HD)
-        scores = dot_nt(p_ref[:, cols], q_ref[:, cols]) * UNIT - dist * slope_ref[head]
+        scores = dot_nt(both(head * HD), q_ref[:, cols]) * UNIT - dist * slope_ref[head]
         top, total, weights = soft(scores)
-        num = dot_nn(p_ref[:, pl.ds(width + head * HD, HD)].T, weights)
+        num = dot_nn(both(width + head * HD).T, weights)
         top_n = stat_ref[2 * head : 2 * head + 1, :]
         total_n = stat_ref[2 * head + 1 : 2 * head + 2, :]
         ceiling = jnp.maximum(top_n, top)
@@ -119,8 +124,9 @@
     )
 
     slot_k, slot_v = ref_keys[0], ref_values[0]
-    got_k = lax.ppermute(slot_k, "c", [(1, 0)])
-    got_v = lax.ppermute(slot_v, "c", [(0, 1)])
+    given = jnp.where(core == 0, slot_v, slot_k)
+    given, slot_k, slot_v, keys_p, values_p = tie((given, slot_k, slot_v, keys, values))
+    got = lax.ppermute(given, "c", SWAP)
     kept = tie(jnp.where(core == 0, slot_k, slot_v))
     pooled = pl.pallas_call(
         pool_kernel,
@@ -130,7 +136,7 @@
         compiler_params=near,
         name="pool",
     )(window_map, pool_segments, keys, values)
-    mine = jnp.where(owner_c == core, kept, jnp.where(core == 0, got_k, got_v))
+    mine = jnp.where(owner_c == core, kept, got)
     mine, pooled = tie((mine, pooled))
 
     spread = lax.all_to_all(mine.reshape(n_x, part, -1), "x", 0, 0, tiled=True)
@@ -138,13 +144,24 @@
     piece = lax.dynamic_index_in_dim(spread, owner_x, 0, keepdims=False)
     piece = piece.reshape(part, n_head, width).transpose(1, 0, 2)
     piece = jnp.broadcast_to(piece[None], (n_zh, n_head, part, width))
-    piece, pooled, other, queries_w = tie((piece, pooled, other, queries))
+    piece, pooled, other = tie((piece, pooled, other))
 
     turned = lax.all_to_all(
         piece.reshape(n_zh * n_head, part, width), ("zh", "head"), 0, 0, tiled=True
     )
     pooled = jnp.concatenate([pooled, other], axis=0)
     other = lax.ppermute(pooled, "x", [(i, i ^ 1) for i in range(n_x)])
+    pooled = jnp.concatenate([pooled, other], axis=0)
+    turned = turned.reshape(n_zh, n_head * part, width)
+    block = lax.dynamic_index_in_dim(turned, owner_z, 0, keepdims=False)
+    block = jnp.broadcast_to(block[None], (n_x, n_head * part, width))
+    other = lax.ppermute(pooled, "x", [(i, i ^ 2) for i in range(n_x)])
+
+    block, queries_w = tie((block, queries))
+
+    own = lax.all_to_all(block, "x", 0, 0, tiled=True).reshape(-1, width)
+    pooled = jnp.concatenate([pooled, other], axis=0)
+    other = lax.ppermute(pooled, "c", SWAP)
     acc_w, stat_w = pl.pallas_call(
         window_kernel,
         out_shape=state,
@@ -158,30 +175,19 @@
         ),
         name="window",
     )(queries_w, keys, values)
-    other, stat_w = tie((other, stat_w))
-    pooled = jnp.concatenate([pooled, other], axis=0)
-    turned = turned.reshape(n_zh, n_head * part, width)
-    block = lax.dynamic_index_in_dim(turned, owner_z, 0, keepdims=False)
-    block = jnp.broadcast_to(block[None], (n_x, n_head * part, width))
-    other = lax.ppermute(pooled, "x", [(i, i ^ 2) for i in range(n_x)])
-
-    own = lax.all_to_all(block, "x", 0, 0, tiled=True).reshape(-1, width)
-    pooled = jnp.concatenate([pooled, other], axis=0)
-    other = lax.ppermute(pooled, "c", SWAP)
-    pooled = jnp.concatenate([pooled, other], axis=0)
     acc, stat = pl.pallas_call(
         pooled_kernel,
         out_shape=state,
-        in_specs=[SMEM, SMEM] + [VMEM] * 4,
+        in_specs=[SMEM, SMEM] + [VMEM] * 5,
         out_specs=(VMEM, VMEM),
         compiler_params=near,
         cost_estimate=pl.CostEstimate(
-            flops=4 * rows * pooled.shape[0] * width,
+            flops=8 * rows * pooled.shape[0] * width,
             bytes_accessed=12 * rows * width,
-            transcendentals=rows * pooled.shape[0] * heads,
+            transcendentals=2 * rows * pooled.shape[0] * heads,
         ),
         name="pooled",
-    )(window_map, slopes, queries, pooled, acc_w, stat_w)
+    )(window_map, slopes, queries, pooled, other, acc_w, stat_w)
     own, stat = tie((own, stat))
 
     got = lax.ppermute(own, "c", SWAP)

time: 77.6 us -> 78.3 us (level)
  the two profiles are of different devices: /device:TPU:1 before, /device:TPU:57 now
where the time goes in v7:
time: 78.3 us; the launch traced here: 77.7 us
  starting transfers between devices  41.2 us (53%)
  waiting for transfers between devices  18.6 us (24%)
  Pallas kernels  8.81 us (11%)
  other arithmetic  4.64 us (6%)
  local copies, waits for them, and re-layouts  2.86 us (4%)
  between operations  1.54 us (2%)
    ppermute x1, starting transfers between devices, on_device(): other = lax.ppermute(pooled, 'zh', SWAP)  10.6 us
    all_to_all x1, starting transfers between devices, on_device(): lax.all_to_all(piece.reshape(n_zh * n_head, part, width), ('zh', 'head'),...  10 us
    all_to_all x1, waiting for transfers between devices, on_device(): lax.all_to_all(piece.reshape(n_zh * n_head, part, width), ('zh', 'head'),...  7.42 us
    all_to_all x1, starting transfers between devices, on_device(): spread = lax.all_to_all(mine.reshape(n_x, part, -1), 'x', 0, 0, tiled=True)  4.01 us
    pallas_call x1, Pallas kernels, on_device(): pl.pallas_call(ref_kernel, out_shape=jax.ShapeDtypeStruct((rows, width),...  3.77 us
    all_to_all x1, waiting for transfers between devices, on_device(): own = lax.all_to_all(block, 'x', 0, 0, tiled=True).reshape(-1, width)  3.74 us
    all_to_all x1, starting transfers between devices, on_device(): own = lax.all_to_all(block, 'x', 0, 0, tiled=True).reshape(-1, width)  3.49 us
    ppermute x1, starting transfers between devices, on_device(): got = lax.ppermute(own, 'c', SWAP)  3.24 us
  transfers between devices with their start and end apart: 9, of which 6 were waited for; matrix products, arithmetic and copies ran while one was open for 3% of the time, Pallas kernels for 6%

profile of v7, /device:TPU:57, one launch (start us, length us, event | category | flops | bytes accessed | tf_op | source)
XLA Modules:
  0.0 77.7 jit_solution(9269360497190181049)
XLA Ops:
  0.0 2.5 %broadcast_select_fusion.1 = bf16[128,3072]{1,0:T(8,128)(2,1)} fusion(pred[]{:T(512)S(6)} %eq.11, bf16[1,128,3072]{2,1,0:T(8,128)(2,1)} %param.15, bf16[1,128,3072]{2,1,0:T(8,128)(2,1)} %param.16), kind=kLoop, calls=%fused_computation.1 | loop fusion | flops 393216 | bytes 2359297 | tf_op jit(solution)/shard_map/jit(_where)/select_n | solution.py:127
  2.5 2.7 %collective-permute-start = (bf16[128,3072]{1,0:T(8,128)(2,1)}, bf16[128,3072]{1,0:T(8,128)(2,1)}, u32[]{:S(2)}, u32[]{:S(2)}) collective-permute-start(bf16[128,3072]{1,0:T(8,128)(2,1)} %broadcast_select_fusion.1), channel_id=1, source_target_pairs={{0,4},{4,0},{1,5},{5,1},{2,6},{6,2},{3,7},{7,3},{8,12},{12,8},{9,1... | collective-permute-start | bytes 2359304 | tf_op jit(solution)/shard_map/ppermute | solution.py:129
  6.5 0.0 copy-done.6
  6.5 0.0 copy-done.5
  6.5 0.1 broadcast_select_fusion
  6.6 0.3 pool.1
  7.0 0.5 collective-permute-done
  7.4 2.1 %broadcast_select_fusion.2 = bf16[128,3072]{1,0:T(8,128)(2,1)} fusion(bf16[128,3072]{1,0:T(8,128)(2,1)S(1)} %broadcast_select_fusion, bf16[128,3072]{1,0:T(8,128)(2,1)} %collective-permute-done, pred[]{:T(512)S(6)} %eq.10), kind=kLoop, calls=%fused_computation.2 | loop fusion | flops 393216 | bytes 2359297 | tf_op jit(solution)/shard_map/jit(_where)/select_n | solution.py:139
  9.5 4.0 %all-to-all-start = ((bf16[4,32,3072]{2,1,0:T(8,128)(2,1)}), bf16[4,32,3072]{2,1,0:T(8,128)(2,1)S(1)}, u32[]{:S(2)}, u32[]{:S(2)}) async-start(bf16[4,32,3072]{2,1,0:T(8,128)(2,1)} %bitcast.4), calls=%async_computation | async-start | bytes 1572864 | tf_op jit(solution)/shard_map/all_to_all | solution.py:142
  13.5 10.6 %collective-permute-start.1 = (bf16[8,1664]{1,0:T(8,128)(2,1)S(1)}, bf16[8,1664]{1,0:T(8,128)(2,1)S(1)}, u32[]{:S(2)}, u32[]{:S(2)}) collective-permute-start(bf16[8,1664]{1,0:T(8,128)(2,1)S(1)} %pool.1), channel_id=1, source_target_pairs={{0,32},{32,0},{1,33},{33,1},{2,34},{34,2},{3,35},{35,3},{4,36},{36... | collective-permute-start | bytes 79880 | tf_op jit(solution)/shard_map/ppermute | solution.py:143
  24.1 2.2 %all-to-all-done = bf16[4,32,3072]{2,1,0:T(8,128)(2,1)S(1)} async-done(((bf16[4,32,3072]{2,1,0:T(8,128)(2,1)}), bf16[4,32,3072]{2,1,0:T(8,128)(2,1)S(1)}, u32[]{:S(2)}, u32[]{:S(2)}) %all-to-all-start) | async-done | bytes 786464 | tf_op jit(solution)/shard_map/all_to_all | solution.py:142
  26.3 0.1 reshape.18
  26.5 0.0 collective-permute-done.1
  26.5 0.8 %broadcast_in_dim.18 = bf16[2,4,32,768]{3,2,1,0:T(8,128)(2,1)} broadcast(bf16[4,32,768]{2,1,0:T(8,128)(2,1)S(1)} %copy.10), dimensions={1,2,3} | broadcast | bytes 589824 | tf_op jit(solution)/shard_map/broadcast_in_dim | solution.py:146
  27.3 10.0 %all-to-all-start.1 = ((bf16[8,32,768]{2,1,0:T(8,128)(2,1)}), bf16[8,32,768]{2,1,0:T(8,128)(2,1)S(1)}, u32[]{:S(2)}, u32[]{:S(2)}) async-start(bf16[8,32,768]{2,1,0:T(8,128)(2,1)} %bitcast.6), calls=%async_computation.1 | async-start | bytes 786432 | tf_op jit(solution)/shard_map/all_to_all | solution.py:149
  37.3 2.2 %collective-permute-start.2 = (bf16[16,1664]{1,0:T(8,128)(2,1)S(1)}, bf16[16,1664]{1,0:T(8,128)(2,1)S(1)}, u32[]{:S(2)}, u32[]{:S(2)}) collective-permute-start(bf16[16,1664]{1,0:T(8,128)(2,1)S(1)} %pad_maximum_fusion.1), channel_id=1, source_target_pairs={{0,8},{8,0},{16,24},{24,16},{1,9},{9,1},{17,25},{25,17},{2,10},{10... | collective-permute-start | bytes 159752 | tf_op jit(solution)/shard_map/ppermute | solution.py:153
  39.6 2.9 %collective-permute-done.2 = bf16[16,1664]{1,0:T(8,128)(2,1)S(1)} collective-permute-done((bf16[16,1664]{1,0:T(8,128)(2,1)S(1)}, bf16[16,1664]{1,0:T(8,128)(2,1)S(1)}, u32[]{:S(2)}, u32[]{:S(2)}) %collective-permute-start.2) | collective-permute-done | bytes 53280 | tf_op jit(solution)/shard_map/ppermute | solution.py:153
  42.5 2.5 %collective-permute-start.3 = (bf16[32,1664]{1,0:T(8,128)(2,1)S(1)}, bf16[32,1664]{1,0:T(8,128)(2,1)}, u32[]{:S(2)}, u32[]{:S(2)}) collective-permute-start(bf16[32,1664]{1,0:T(8,128)(2,1)S(1)} %pad_maximum_fusion), channel_id=1, source_target_pairs={{0,16},{8,24},{16,0},{24,8},{1,17},{9,25},{17,1},{25,9},{2,18},{10... | collective-permute-start | bytes 319496 | tf_op jit(solution)/shard_map/ppermute | solution.py:158
  45.1 7.4 %all-to-all-done.1 = bf16[8,32,768]{2,1,0:T(8,128)(2,1)S(1)} async-done(((bf16[8,32,768]{2,1,0:T(8,128)(2,1)}), bf16[8,32,768]{2,1,0:T(8,128)(2,1)S(1)}, u32[]{:S(2)}, u32[]{:S(2)}) %all-to-all-start.1) | async-done | bytes 393248 | tf_op jit(solution)/shard_map/all_to_all | solution.py:149
  52.5 0.9 %broadcast_in_dim.20 = bf16[4,128,768]{2,1,0:T(8,128)(2,1)} broadcast(bf16[128,768]{1,0:T(8,128)(2,1)S(1)} %dynamic-slice_bitcast_fusion), dimensions={1,2} | broadcast | bytes 983040 | tf_op jit(solution)/shard_map/broadcast_in_dim | solution.py:157
  53.4 3.5 %all-to-all-start.2 = ((bf16[4,128,768]{2,1,0:T(8,128)(2,1)}), bf16[4,128,768]{2,1,0:T(8,128)(2,1)S(1)}, u32[]{:S(2)}, u32[]{:S(2)}) async-start(bf16[4,128,768]{2,1,0:T(8,128)(2,1)} %broadcast_in_dim.20), calls=%async_computation.2 | async-start | bytes 1572864 | tf_op jit(solution)/shard_map/all_to_all | solution.py:162
  57.0 0.0 copy-start.4
  57.0 0.0 collective-permute-done.3
  57.0 0.9 %constant_dynamic-update-slice_fusion.pa_ref = bf16[64,1664]{1,0:T(8,128)(2,1)S(1)} fusion(bf16[64,1664]{1,0:T(8,128)(2,1)S(1)} %constant_dynamic-update-slice_fusion.1, bf16[32,1664]{1,0:T(8,128)(2,1)} %collective-permute-done.3), kind=kLoop, calls=%fused_computation.6 | loop fusion | bytes 212992 | tf_op jit(solution)/shard_map/concatenate | solution.py:163
  57.9 2.4 %collective-permute-start.4 = (bf16[64,1664]{1,0:T(8,128)(2,1)S(1)}, bf16[64,1664]{1,0:T(8,128)(2,1)S(1)}, u32[]{:S(2)}, u32[]{:S(2)}) collective-permute-start(bf16[64,1664]{1,0:T(8,128)(2,1)S(1)} %constant_dynamic-update-slice_fusion.pa_ref), channel_id=1, source_target_pairs={{0,4},{4,0},{1,5},{5,1},{2,6},{6,2},{3,7},{7,3},{8,12},{12,8},{9,1... | collective-permute-start | bytes 638984 | tf_op jit(solution)/shard_map/ppermute | solution.py:164
  60.3 2.5 %window.1 = (f32[768,512]{1,0:T(8,128)S(1)}, f32[16,512]{1,0:T(8,128)S(1)}) custom-call(bf16[512,768]{1,0:T(8,128)(2,1)S(1)} %copy-done, bf16[512,768]{1,0:T(8,128)(2,1)S(1)} %copy-done.1, bf16[512,768]{1,0:T(8,128)(2,1)S(1)} %copy-done.2), custom_call_target="tpu_custom_call" | custom-call | flops 805306368 | bytes 3932160 | tf_op jit(solution)/shard_map/window/pallas_call | solution.py:165
  62.8 0.0 collective-permute-done.4.pb_ref
  62.8 2.2 %pooled.1 = (f32[768,512]{1,0:T(8,128)S(1)}, f32[16,512]{1,0:T(8,128)S(1)}) custom-call(s32[1]{0:T(128)S(6)} %copy.14.tag_ref, f32[6]{0:T(128)S(1)} %copy-done.4, bf16[512,768]{1,0:T(8,128)(2,1)S(1)} %copy-done, bf16[64,1664]{1,0:T(8,128)(2,1)S(1)} %constant_dynamic-update-slice_fusion.pa_ref, bf16[64,1664]{1,0:T(8,128)(2,1)S(1)} %collective-permute-done.4.pb_ref, ...), custom_call_target="tpu_custom_call" | custom-call | flops 201326592 | bytes 4718592 | tf_op jit(solution)/shard_map/pooled/pallas_call | solution.py:178
  65.1 3.7 %all-to-all-done.2 = bf16[4,128,768]{2,1,0:T(8,128)(2,1)S(1)} async-done(((bf16[4,128,768]{2,1,0:T(8,128)(2,1)}), bf16[4,128,768]{2,1,0:T(8,128)(2,1)S(1)}, u32[]{:S(2)}, u32[]{:S(2)}) %all-to-all-start.2) | async-done | bytes 786464 | tf_op jit(solution)/shard_map/all_to_all | solution.py:162
  68.8 3.2 %collective-permute-start.5 = (bf16[512,768]{1,0:T(8,128)(2,1)S(1)}, bf16[512,768]{1,0:T(8,128)(2,1)S(1)}, u32[]{:S(2)}, u32[]{:S(2)}) collective-permute-start(bf16[512,768]{1,0:T(8,128)(2,1)S(1)} %bitcast.17), channel_id=1, source_target_pairs={{0,4},{4,0},{1,5},{5,1},{2,6},{6,2},{3,7},{7,3},{8,12},{12,8},{9,1... | collective-permute-start | bytes 2359304 | tf_op jit(solution)/shard_map/ppermute | solution.py:193
  72.0 1.9 %collective-permute-done.5.got_ref = bf16[512,768]{1,0:T(8,128)(2,1)S(1)} collective-permute-done((bf16[512,768]{1,0:T(8,128)(2,1)S(1)}, bf16[512,768]{1,0:T(8,128)(2,1)S(1)}, u32[]{:S(2)}, u32[]{:S(2)}) %collective-permute-start.5) | collective-permute-done | bytes 786464 | tf_op jit(solution)/shard_map/ppermute | solution.py:193
  73.9 3.8 %far.1 = bf16[512,768]{1,0:T(8,128)(2,1)} custom-call(s32[1]{0:T(128)} %bitcast.core_ref, bf16[512,768]{1,0:T(8,128)(2,1)S(1)} %copy-done, bf16[512,768]{1,0:T(8,128)(2,1)S(1)} %bitcast.18, bf16[512,768]{1,0:T(8,128)(2,1)S(1)} %collective-permute-done.5.got_ref, f32[768,512]{1,0:T(8,128)S(1)} %get-tuple-element.35.acc_ref, ...), custom_call_target="tpu_custom_call" | custom-call | tf_op jit(solution)/shard_map/far/pallas_call | solution.py:194
  (19 shorter events, 0.1 us)
Async XLA Ops:
  0.0 6.5 %copy-start.6 = (bf16[1,128,3072]{2,1,0:T(8,128)(2,1)S(1)}, bf16[1,128,3072]{2,1,0:T(8,128)(2,1)}, u32[]{:S(2)}) copy-start(bf16[1,128,3072]{2,1,0:T(8,128)(2,1)} %param.16) | copy-start | bytes 2359300
  0.0 6.5 %copy-start.5 = (bf16[1,128,3072]{2,1,0:T(8,128)(2,1)S(1)}, bf16[1,128,3072]{2,1,0:T(8,128)(2,1)}, u32[]{:S(2)}) copy-start(bf16[1,128,3072]{2,1,0:T(8,128)(2,1)} %param.15) | copy-start | bytes 2359300
  2.5 4.2 %copy-start.1 = (bf16[512,768]{1,0:T(8,128)(2,1)S(1)}, bf16[512,768]{1,0:T(8,128)(2,1)}, u32[]{:S(2)}) copy-start(bf16[512,768]{1,0:T(8,128)(2,1)} %k_ref.1) | copy-start | bytes 2359300
  2.5 4.2 %copy-start.2 = (bf16[512,768]{1,0:T(8,128)(2,1)S(1)}, bf16[512,768]{1,0:T(8,128)(2,1)}, u32[]{:S(2)}) copy-start(bf16[512,768]{1,0:T(8,128)(2,1)} %v_ref.1) | copy-start | bytes 2359300
  2.5 4.2 %copy-start.3 = (s32[1,512]{1,0:T(1,128)S(1)}, s32[1,512]{1,0:T(1,128)}, u32[]{:S(2)}) copy-start(s32[1,512]{1,0:T(1,128)} %seg_ref.1) | copy-start | bytes 6148
  2.5 4.9 %collective-permute-start = (bf16[128,3072]{1,0:T(8,128)(2,1)}, bf16[128,3072]{1,0:T(8,128)(2,1)}, u32[]{:S(2)}, u32[]{:S(2)}) collective-permute-start(bf16[128,3072]{1,0:T(8,128)(2,1)} %broadcast_select_fusion.1), channel_id=1, source_target_pairs={{0,4},{4,0},{1,5},{5,1},{2,6},{6,2},{3,7},{7,3},{8,12},{12,8},{9,1... | collective-permute-start | bytes 2359304 | tf_op jit(solution)/shard_map/ppermute | solution.py:129
  9.5 16.8 %all-to-all-start = ((bf16[4,32,3072]{2,1,0:T(8,128)(2,1)}), bf16[4,32,3072]{2,1,0:T(8,128)(2,1)S(1)}, u32[]{:S(2)}, u32[]{:S(2)}) async-start(bf16[4,32,3072]{2,1,0:T(8,128)(2,1)} %bitcast.4), calls=%async_computation | async-start | bytes 1572864 | tf_op jit(solution)/shard_map/all_to_all | solution.py:142
  13.5 13.0 %collective-permute-start.1 = (bf16[8,1664]{1,0:T(8,128)(2,1)S(1)}, bf16[8,1664]{1,0:T(8,128)(2,1)S(1)}, u32[]{:S(2)}, u32[]{:S(2)}) collective-permute-start(bf16[8,1664]{1,0:T(8,128)(2,1)S(1)} %pool.1), channel_id=1, source_target_pairs={{0,32},{32,0},{1,33},{33,1},{2,34},{34,2},{3,35},{35,3},{4,36},{36... | collective-permute-start | bytes 79880 | tf_op jit(solution)/shard_map/ppermute | solution.py:143
  27.3 25.2 %all-to-all-start.1 = ((bf16[8,32,768]{2,1,0:T(8,128)(2,1)}), bf16[8,32,768]{2,1,0:T(8,128)(2,1)S(1)}, u32[]{:S(2)}, u32[]{:S(2)}) async-start(bf16[8,32,768]{2,1,0:T(8,128)(2,1)} %bitcast.6), calls=%async_computation.1 | async-start | bytes 786432 | tf_op jit(solution)/shard_map/all_to_all | solution.py:149
  37.3 5.2 %collective-permute-start.2 = (bf16[16,1664]{1,0:T(8,128)(2,1)S(1)}, bf16[16,1664]{1,0:T(8,128)(2,1)S(1)}, u32[]{:S(2)}, u32[]{:S(2)}) collective-permute-start(bf16[16,1664]{1,0:T(8,128)(2,1)S(1)} %pad_maximum_fusion.1), channel_id=1, source_target_pairs={{0,8},{8,0},{16,24},{24,16},{1,9},{9,1},{17,25},{25,17},{2,10},{10... | collective-permute-start | bytes 159752 | tf_op jit(solution)/shard_map/ppermute | solution.py:153
  42.5 14.4 %collective-permute-start.3 = (bf16[32,1664]{1,0:T(8,128)(2,1)S(1)}, bf16[32,1664]{1,0:T(8,128)(2,1)}, u32[]{:S(2)}, u32[]{:S(2)}) collective-permute-start(bf16[32,1664]{1,0:T(8,128)(2,1)S(1)} %pad_maximum_fusion), channel_id=1, source_target_pairs={{0,16},{8,24},{16,0},{24,8},{1,17},{9,25},{17,1},{25,9},{2,18},{10... | collective-permute-start | bytes 319496 | tf_op jit(solution)/shard_map/ppermute | solution.py:158
  52.5 7.8 %copy-start = (bf16[512,768]{1,0:T(8,128)(2,1)S(1)}, bf16[512,768]{1,0:T(8,128)(2,1)}, u32[]{:S(2)}) copy-start(bf16[512,768]{1,0:T(8,128)(2,1)} %q_ref.4) | copy-start | bytes 2359300
  53.4 15.4 %all-to-all-start.2 = ((bf16[4,128,768]{2,1,0:T(8,128)(2,1)}), bf16[4,128,768]{2,1,0:T(8,128)(2,1)S(1)}, u32[]{:S(2)}, u32[]{:S(2)}) async-start(bf16[4,128,768]{2,1,0:T(8,128)(2,1)} %broadcast_in_dim.20), calls=%async_computation.2 | async-start | bytes 1572864 | tf_op jit(solution)/shard_map/all_to_all | solution.py:162
  57.0 5.9 %copy-start.4 = (f32[6]{0:T(128)S(1)}, f32[6]{0:T(128)}, u32[]{:S(2)}) copy-start(f32[6]{0:T(128)} %slope_ref.1) | copy-start | bytes 76
  57.9 4.9 %collective-permute-start.4 = (bf16[64,1664]{1,0:T(8,128)(2,1)S(1)}, bf16[64,1664]{1,0:T(8,128)(2,1)S(1)}, u32[]{:S(2)}, u32[]{:S(2)}) collective-permute-start(bf16[64,1664]{1,0:T(8,128)(2,1)S(1)} %constant_dynamic-update-slice_fusion.pa_ref), channel_id=1, source_target_pairs={{0,4},{4,0},{1,5},{5,1},{2,6},{6,2},{3,7},{7,3},{8,12},{12,8},{9,1... | collective-permute-start | bytes 638984 | tf_op jit(solution)/shard_map/ppermute | solution.py:164
  68.8 5.1 %collective-permute-start.5 = (bf16[512,768]{1,0:T(8,128)(2,1)S(1)}, bf16[512,768]{1,0:T(8,128)(2,1)S(1)}, u32[]{:S(2)}, u32[]{:S(2)}) collective-permute-start(bf16[512,768]{1,0:T(8,128)(2,1)S(1)} %bitcast.17), channel_id=1, source_target_pairs={{0,4},{4,0},{1,5},{5,1},{2,6},{6,2},{3,7},{7,3},{8,12},{12,8},{9,1... | collective-permute-start | bytes 2359304 | tf_op jit(solution)/shard_map/ppermute | solution.py:193

commit v8 on v7

--- a/solution.py
+++ b/solution.py
@@ -124,10 +124,14 @@
     )
 
     slot_k, slot_v = ref_keys[0], ref_values[0]
-    given = jnp.where(core == 0, slot_v, slot_k)
-    given, slot_k, slot_v, keys_p, values_p = tie((given, slot_k, slot_v, keys, values))
+    given = tie(jnp.where(core == 0, slot_v, slot_k))
     got = lax.ppermute(given, "c", SWAP)
+    given, slot_k, slot_v = tie((given, slot_k, slot_v))
     kept = tie(jnp.where(core == 0, slot_k, slot_v))
+    mine = jnp.where(owner_c == core, kept, got)
+    mine, keys_p, values_p = tie((mine, keys, values))
+
+    spread = lax.all_to_all(mine.reshape(n_x, part, -1), "x", 0, 0, tiled=True)
     pooled = pl.pallas_call(
         pool_kernel,
         out_shape=jax.ShapeDtypeStruct((POOLS, 2 * width + HD), jnp.bfloat16),
@@ -135,11 +139,7 @@
         out_specs=VMEM,
         compiler_params=near,
         name="pool",
-    )(window_map, pool_segments, keys, values)
-    mine = jnp.where(owner_c == core, kept, got)
-    mine, pooled = tie((mine, pooled))
-
-    spread = lax.all_to_all(mine.reshape(n_x, part, -1), "x", 0, 0, tiled=True)
+    )(window_map, pool_segments, keys_p, values_p)
     other = lax.ppermute(pooled, "zh", SWAP)
     piece = lax.dynamic_index_in_dim(spread, owner_x, 0, keepdims=False)
     piece = piece.reshape(part, n_head, width).transpose(1, 0, 2)

time: 78.3 us -> 72.7 us (0.928)
  the two profiles are of different devices: /device:TPU:57 before, /device:TPU:1 now
where the time goes in v8:
time: 72.7 us; the launch traced here: 72.2 us
  starting transfers between devices  40.7 us (56%)
  waiting for transfers between devices  15.6 us (21%)
  Pallas kernels  8.81 us (12%)
  local copies, waits for them, and re-layouts  2.87 us (4%)
  other arithmetic  2.65 us (4%)
  between operations  1.63 us (2%)
    ppermute x1, starting transfers between devices, on_device(): got = lax.ppermute(given, 'c', SWAP)  8.79 us
    ppermute x1, starting transfers between devices, on_device(): other = lax.ppermute(pooled, 'zh', SWAP)  5.72 us
    all_to_all x1, waiting for transfers between devices, on_device(): spread = lax.all_to_all(mine.reshape(n_x, part, -1), 'x', 0, 0, tiled=True)  5.22 us
    ppermute x1, starting transfers between devices, on_device(): other = lax.ppermute(pooled, 'c', SWAP)  5.18 us
    all_to_all x1, starting transfers between devices, on_device(): lax.all_to_all(piece.reshape(n_zh * n_head, part, width), ('zh', 'head'),...  4.89 us
    all_to_all x1, waiting for transfers between devices, on_device(): lax.all_to_all(piece.reshape(n_zh * n_head, part, width), ('zh', 'head'),...  4.72 us
    ppermute x1, starting transfers between devices, on_device(): got = lax.ppermute(own, 'c', SWAP)  4.19 us
    pallas_call x1, Pallas kernels, on_device(): pl.pallas_call(ref_kernel, out_shape=jax.ShapeDtypeStruct((rows, width),...  3.77 us
  transfers between devices with their start and end apart: 9, of which 5 were waited for; matrix products, arithmetic and copies ran while one was open for 3% of the time, Pallas kernels for 7%

profile of v8, /device:TPU:1, one launch (start us, length us, event | category | flops | bytes accessed | tf_op | source)
XLA Modules:
  0.0 72.2 jit_solution(15079575575567540694)
XLA Ops:
  0.0 1.6 %broadcast_select_fusion.1 = bf16[128,3072]{1,0:T(8,128)(2,1)S(1)} fusion(pred[]{:T(512)S(6)} %eq.11, bf16[1,128,3072]{2,1,0:T(8,128)(2,1)} %param.15, bf16[1,128,3072]{2,1,0:T(8,128)(2,1)} %param.16), kind=kLoop, calls=%fused_computation.1 | loop fusion | flops 393216 | bytes 2359297 | tf_op jit(solution)/shard_map/jit(_where)/select_n | solution.py:127
  1.6 8.8 %collective-permute-start = (bf16[128,3072]{1,0:T(8,128)(2,1)S(1)}, bf16[128,3072]{1,0:T(8,128)(2,1)S(1)}, u32[]{:S(2)}, u32[]{:S(2)}) collective-permute-start(bf16[128,3072]{1,0:T(8,128)(2,1)S(1)} %broadcast_select_fusion.1), channel_id=1, source_target_pairs={{0,4},{4,0},{1,5},{5,1},{2,6},{6,2},{3,7},{7,3},{8,12},{12,8},{9,1... | collective-permute-start | bytes 2359304 | tf_op jit(solution)/shard_map/ppermute | solution.py:128
  11.1 0.1 broadcast_select_fusion
  11.2 0.0 copy-start.1
  11.2 0.0 copy-start.2
  11.2 0.0 copy-start.3
  11.2 1.1 %collective-permute-done = bf16[128,3072]{1,0:T(8,128)(2,1)S(1)} collective-permute-done((bf16[128,3072]{1,0:T(8,128)(2,1)S(1)}, bf16[128,3072]{1,0:T(8,128)(2,1)S(1)}, u32[]{:S(2)}, u32[]{:S(2)}) %collective-permute-start) | collective-permute-done | bytes 786464 | tf_op jit(solution)/shard_map/ppermute | solution.py:128
  12.3 1.0 %broadcast_select_fusion.2 = bf16[128,3072]{1,0:T(8,128)(2,1)} fusion(bf16[128,3072]{1,0:T(8,128)(2,1)S(1)} %broadcast_select_fusion, bf16[128,3072]{1,0:T(8,128)(2,1)S(1)} %collective-permute-done, pred[]{:T(512)S(6)} %eq.10), kind=kLoop, calls=%fused_computation.2 | loop fusion | flops 393216 | bytes 2359297 | tf_op jit(solution)/shard_map/jit(_where)/select_n | solution.py:131
  13.2 3.5 %all-to-all-start = ((bf16[4,32,3072]{2,1,0:T(8,128)(2,1)}), bf16[4,32,3072]{2,1,0:T(8,128)(2,1)S(1)}, u32[]{:S(2)}, u32[]{:S(2)}) async-start(bf16[4,32,3072]{2,1,0:T(8,128)(2,1)} %bitcast.4), calls=%async_computation | async-start | bytes 1572864 | tf_op jit(solution)/shard_map/all_to_all | solution.py:134
  17.5 0.3 pool.1
  17.8 5.7 %collective-permute-start.1 = (bf16[8,1664]{1,0:T(8,128)(2,1)S(1)}, bf16[8,1664]{1,0:T(8,128)(2,1)S(1)}, u32[]{:S(2)}, u32[]{:S(2)}) collective-permute-start(bf16[8,1664]{1,0:T(8,128)(2,1)S(1)} %pool.1), channel_id=1, source_target_pairs={{0,32},{32,0},{1,33},{33,1},{2,34},{34,2},{3,35},{35,3},{4,36},{36... | collective-permute-start | bytes 79880 | tf_op jit(solution)/shard_map/ppermute | solution.py:143
  23.5 5.2 %all-to-all-done = bf16[4,32,3072]{2,1,0:T(8,128)(2,1)S(1)} async-done(((bf16[4,32,3072]{2,1,0:T(8,128)(2,1)}), bf16[4,32,3072]{2,1,0:T(8,128)(2,1)S(1)}, u32[]{:S(2)}, u32[]{:S(2)}) %all-to-all-start) | async-done | bytes 786464 | tf_op jit(solution)/shard_map/all_to_all | solution.py:134
  28.8 0.1 reshape.18
  28.9 0.0 collective-permute-done.1
  28.9 0.8 %broadcast_in_dim.18 = bf16[2,4,32,768]{3,2,1,0:T(8,128)(2,1)} broadcast(bf16[4,32,768]{2,1,0:T(8,128)(2,1)S(1)} %copy.10), dimensions={1,2,3} | broadcast | bytes 589824 | tf_op jit(solution)/shard_map/broadcast_in_dim | solution.py:146
  29.7 4.9 %all-to-all-start.1 = ((bf16[8,32,768]{2,1,0:T(8,128)(2,1)}), bf16[8,32,768]{2,1,0:T(8,128)(2,1)S(1)}, u32[]{:S(2)}, u32[]{:S(2)}) async-start(bf16[8,32,768]{2,1,0:T(8,128)(2,1)} %bitcast.6), calls=%async_computation.1 | async-start | bytes 786432 | tf_op jit(solution)/shard_map/all_to_all | solution.py:149
  34.6 2.2 %collective-permute-start.2 = (bf16[16,1664]{1,0:T(8,128)(2,1)S(1)}, bf16[16,1664]{1,0:T(8,128)(2,1)S(1)}, u32[]{:S(2)}, u32[]{:S(2)}) collective-permute-start(bf16[16,1664]{1,0:T(8,128)(2,1)S(1)} %pad_maximum_fusion.1), channel_id=1, source_target_pairs={{0,8},{8,0},{16,24},{24,16},{1,9},{9,1},{17,25},{25,17},{2,10},{10... | collective-permute-start | bytes 159752 | tf_op jit(solution)/shard_map/ppermute | solution.py:153
  36.8 2.7 %collective-permute-done.2 = bf16[16,1664]{1,0:T(8,128)(2,1)S(1)} collective-permute-done((bf16[16,1664]{1,0:T(8,128)(2,1)S(1)}, bf16[16,1664]{1,0:T(8,128)(2,1)S(1)}, u32[]{:S(2)}, u32[]{:S(2)}) %collective-permute-start.2) | collective-permute-done | bytes 53280 | tf_op jit(solution)/shard_map/ppermute | solution.py:153
  39.5 2.7 %collective-permute-start.3 = (bf16[32,1664]{1,0:T(8,128)(2,1)S(1)}, bf16[32,1664]{1,0:T(8,128)(2,1)}, u32[]{:S(2)}, u32[]{:S(2)}) collective-permute-start(bf16[32,1664]{1,0:T(8,128)(2,1)S(1)} %pad_maximum_fusion), channel_id=1, source_target_pairs={{0,16},{8,24},{16,0},{24,8},{1,17},{9,25},{17,1},{25,9},{2,18},{10... | collective-permute-start | bytes 319496 | tf_op jit(solution)/shard_map/ppermute | solution.py:158
  42.3 4.7 %all-to-all-done.1 = bf16[8,32,768]{2,1,0:T(8,128)(2,1)S(1)} async-done(((bf16[8,32,768]{2,1,0:T(8,128)(2,1)}), bf16[8,32,768]{2,1,0:T(8,128)(2,1)S(1)}, u32[]{:S(2)}, u32[]{:S(2)}) %all-to-all-start.1) | async-done | bytes 393248 | tf_op jit(solution)/shard_map/all_to_all | solution.py:149
  47.0 0.9 %broadcast_in_dim.20 = bf16[4,128,768]{2,1,0:T(8,128)(2,1)} broadcast(bf16[128,768]{1,0:T(8,128)(2,1)S(1)} %dynamic-slice_bitcast_fusion), dimensions={1,2} | broadcast | bytes 983040 | tf_op jit(solution)/shard_map/broadcast_in_dim | solution.py:157
  47.9 3.5 %all-to-all-start.2 = ((bf16[4,128,768]{2,1,0:T(8,128)(2,1)}), bf16[4,128,768]{2,1,0:T(8,128)(2,1)S(1)}, u32[]{:S(2)}, u32[]{:S(2)}) async-start(bf16[4,128,768]{2,1,0:T(8,128)(2,1)} %broadcast_in_dim.20), calls=%async_computation.2 | async-start | bytes 1572864 | tf_op jit(solution)/shard_map/all_to_all | solution.py:162
  51.5 0.0 copy-start.4
  51.5 0.0 collective-permute-done.3
  51.5 0.9 %constant_dynamic-update-slice_fusion.pa_ref = bf16[64,1664]{1,0:T(8,128)(2,1)S(1)} fusion(bf16[64,1664]{1,0:T(8,128)(2,1)S(1)} %constant_dynamic-update-slice_fusion.1, bf16[32,1664]{1,0:T(8,128)(2,1)} %collective-permute-done.3), kind=kLoop, calls=%fused_computation.6 | loop fusion | bytes 212992 | tf_op jit(solution)/shard_map/concatenate | solution.py:163
  52.4 5.2 %collective-permute-start.4 = (bf16[64,1664]{1,0:T(8,128)(2,1)S(1)}, bf16[64,1664]{1,0:T(8,128)(2,1)S(1)}, u32[]{:S(2)}, u32[]{:S(2)}) collective-permute-start(bf16[64,1664]{1,0:T(8,128)(2,1)S(1)} %constant_dynamic-update-slice_fusion.pa_ref), channel_id=1, source_target_pairs={{0,4},{4,0},{1,5},{5,1},{2,6},{6,2},{3,7},{7,3},{8,12},{12,8},{9,1... | collective-permute-start | bytes 638984 | tf_op jit(solution)/shard_map/ppermute | solution.py:164
  57.6 2.5 %window.1 = (f32[768,512]{1,0:T(8,128)S(1)}, f32[16,512]{1,0:T(8,128)S(1)}) custom-call(bf16[512,768]{1,0:T(8,128)(2,1)S(1)} %copy-done, bf16[512,768]{1,0:T(8,128)(2,1)S(1)} %copy-done.1, bf16[512,768]{1,0:T(8,128)(2,1)S(1)} %copy-done.2), custom_call_target="tpu_custom_call" | custom-call | flops 805306368 | bytes 3932160 | tf_op jit(solution)/shard_map/window/pallas_call | solution.py:165
  60.1 0.0 collective-permute-done.4.pb_ref
  60.1 2.2 %pooled.1 = (f32[768,512]{1,0:T(8,128)S(1)}, f32[16,512]{1,0:T(8,128)S(1)}) custom-call(s32[1]{0:T(128)S(6)} %copy.14.tag_ref, f32[6]{0:T(128)S(1)} %copy-done.4, bf16[512,768]{1,0:T(8,128)(2,1)S(1)} %copy-done, bf16[64,1664]{1,0:T(8,128)(2,1)S(1)} %constant_dynamic-update-slice_fusion.pa_ref, bf16[64,1664]{1,0:T(8,128)(2,1)S(1)} %collective-permute-done.4.pb_ref, ...), custom_call_target="tpu_custom_call" | custom-call | flops 201326592 | bytes 4718592 | tf_op jit(solution)/shard_map/pooled/pallas_call | solution.py:178
  62.4 4.2 %collective-permute-start.5 = (bf16[512,768]{1,0:T(8,128)(2,1)S(1)}, bf16[512,768]{1,0:T(8,128)(2,1)S(1)}, u32[]{:S(2)}, u32[]{:S(2)}) collective-permute-start(bf16[512,768]{1,0:T(8,128)(2,1)S(1)} %bitcast.17), channel_id=1, source_target_pairs={{0,4},{4,0},{1,5},{5,1},{2,6},{6,2},{3,7},{7,3},{8,12},{12,8},{9,1... | collective-permute-start | bytes 2359304 | tf_op jit(solution)/shard_map/ppermute | solution.py:193
  66.5 1.9 %collective-permute-done.5.got_ref = bf16[512,768]{1,0:T(8,128)(2,1)S(1)} collective-permute-done((bf16[512,768]{1,0:T(8,128)(2,1)S(1)}, bf16[512,768]{1,0:T(8,128)(2,1)S(1)}, u32[]{:S(2)}, u32[]{:S(2)}) %collective-permute-start.5) | collective-permute-done | bytes 786464 | tf_op jit(solution)/shard_map/ppermute | solution.py:193
  68.4 3.8 %far.1 = bf16[512,768]{1,0:T(8,128)(2,1)} custom-call(s32[1]{0:T(128)} %bitcast.core_ref, bf16[512,768]{1,0:T(8,128)(2,1)S(1)} %copy-done, bf16[512,768]{1,0:T(8,128)(2,1)S(1)} %bitcast.18, bf16[512,768]{1,0:T(8,128)(2,1)S(1)} %collective-permute-done.5.got_ref, f32[768,512]{1,0:T(8,128)S(1)} %get-tuple-element.35.acc_ref, ...), custom_call_target="tpu_custom_call" | custom-call | tf_op jit(solution)/shard_map/far/pallas_call | solution.py:194
  (19 shorter events, 0.1 us)
Async XLA Ops:
  0.0 11.0 %copy-start.6 = (bf16[1,128,3072]{2,1,0:T(8,128)(2,1)S(1)}, bf16[1,128,3072]{2,1,0:T(8,128)(2,1)}, u32[]{:S(2)}) copy-start(bf16[1,128,3072]{2,1,0:T(8,128)(2,1)} %param.16) | copy-start | bytes 2359300
  0.0 11.1 %copy-start.5 = (bf16[1,128,3072]{2,1,0:T(8,128)(2,1)S(1)}, bf16[1,128,3072]{2,1,0:T(8,128)(2,1)}, u32[]{:S(2)}) copy-start(bf16[1,128,3072]{2,1,0:T(8,128)(2,1)} %param.15) | copy-start | bytes 2359300
  1.6 10.7 %collective-permute-start = (bf16[128,3072]{1,0:T(8,128)(2,1)S(1)}, bf16[128,3072]{1,0:T(8,128)(2,1)S(1)}, u32[]{:S(2)}, u32[]{:S(2)}) collective-permute-start(bf16[128,3072]{1,0:T(8,128)(2,1)S(1)} %broadcast_select_fusion.1), channel_id=1, source_target_pairs={{0,4},{4,0},{1,5},{5,1},{2,6},{6,2},{3,7},{7,3},{8,12},{12,8},{9,1... | collective-permute-start | bytes 2359304 | tf_op jit(solution)/shard_map/ppermute | solution.py:128
  11.2 6.3 %copy-start.1 = (bf16[512,768]{1,0:T(8,128)(2,1)S(1)}, bf16[512,768]{1,0:T(8,128)(2,1)}, u32[]{:S(2)}) copy-start(bf16[512,768]{1,0:T(8,128)(2,1)} %k_ref.1) | copy-start | bytes 2359300
  11.2 6.3 %copy-start.2 = (bf16[512,768]{1,0:T(8,128)(2,1)S(1)}, bf16[512,768]{1,0:T(8,128)(2,1)}, u32[]{:S(2)}) copy-start(bf16[512,768]{1,0:T(8,128)(2,1)} %v_ref.1) | copy-start | bytes 2359300
  11.2 6.3 %copy-start.3 = (s32[1,512]{1,0:T(1,128)S(1)}, s32[1,512]{1,0:T(1,128)}, u32[]{:S(2)}) copy-start(s32[1,512]{1,0:T(1,128)} %seg_ref.1) | copy-start | bytes 6148
  13.2 15.5 %all-to-all-start = ((bf16[4,32,3072]{2,1,0:T(8,128)(2,1)}), bf16[4,32,3072]{2,1,0:T(8,128)(2,1)S(1)}, u32[]{:S(2)}, u32[]{:S(2)}) async-start(bf16[4,32,3072]{2,1,0:T(8,128)(2,1)} %bitcast.4), calls=%async_computation | async-start | bytes 1572864 | tf_op jit(solution)/shard_map/all_to_all | solution.py:134
  17.8 11.1 %collective-permute-start.1 = (bf16[8,1664]{1,0:T(8,128)(2,1)S(1)}, bf16[8,1664]{1,0:T(8,128)(2,1)S(1)}, u32[]{:S(2)}, u32[]{:S(2)}) collective-permute-start(bf16[8,1664]{1,0:T(8,128)(2,1)S(1)} %pool.1), channel_id=1, source_target_pairs={{0,32},{32,0},{1,33},{33,1},{2,34},{34,2},{3,35},{35,3},{4,36},{36... | collective-permute-start | bytes 79880 | tf_op jit(solution)/shard_map/ppermute | solution.py:143
  29.7 17.3 %all-to-all-start.1 = ((bf16[8,32,768]{2,1,0:T(8,128)(2,1)}), bf16[8,32,768]{2,1,0:T(8,128)(2,1)S(1)}, u32[]{:S(2)}, u32[]{:S(2)}) async-start(bf16[8,32,768]{2,1,0:T(8,128)(2,1)} %bitcast.6), calls=%async_computation.1 | async-start | bytes 786432 | tf_op jit(solution)/shard_map/all_to_all | solution.py:149
  34.6 4.9 %collective-permute-start.2 = (bf16[16,1664]{1,0:T(8,128)(2,1)S(1)}, bf16[16,1664]{1,0:T(8,128)(2,1)S(1)}, u32[]{:S(2)}, u32[]{:S(2)}) collective-permute-start(bf16[16,1664]{1,0:T(8,128)(2,1)S(1)} %pad_maximum_fusion.1), channel_id=1, source_target_pairs={{0,8},{8,0},{16,24},{24,16},{1,9},{9,1},{17,25},{25,17},{2,10},{10... | collective-permute-start | bytes 159752 | tf_op jit(solution)/shard_map/ppermute | solution.py:153
  39.5 12.0 %collective-permute-start.3 = (bf16[32,1664]{1,0:T(8,128)(2,1)S(1)}, bf16[32,1664]{1,0:T(8,128)(2,1)}, u32[]{:S(2)}, u32[]{:S(2)}) collective-permute-start(bf16[32,1664]{1,0:T(8,128)(2,1)S(1)} %pad_maximum_fusion), channel_id=1, source_target_pairs={{0,16},{8,24},{16,0},{24,8},{1,17},{9,25},{17,1},{25,9},{2,18},{10... | collective-permute-start | bytes 319496 | tf_op jit(solution)/shard_map/ppermute | solution.py:158
  47.0 10.6 %copy-start = (bf16[512,768]{1,0:T(8,128)(2,1)S(1)}, bf16[512,768]{1,0:T(8,128)(2,1)}, u32[]{:S(2)}) copy-start(bf16[512,768]{1,0:T(8,128)(2,1)} %q_ref.4) | copy-start | bytes 2359300
  47.9 14.4 %all-to-all-start.2 = ((bf16[4,128,768]{2,1,0:T(8,128)(2,1)}), bf16[4,128,768]{2,1,0:T(8,128)(2,1)S(1)}, u32[]{:S(2)}, u32[]{:S(2)}) async-start(bf16[4,128,768]{2,1,0:T(8,128)(2,1)} %broadcast_in_dim.20), calls=%async_computation.2 | async-start | bytes 1572864 | tf_op jit(solution)/shard_map/all_to_all | solution.py:162
  51.5 8.7 %copy-start.4 = (f32[6]{0:T(128)S(1)}, f32[6]{0:T(128)}, u32[]{:S(2)}) copy-start(f32[6]{0:T(128)} %slope_ref.1) | copy-start | bytes 76
  52.4 7.7 %collective-permute-start.4 = (bf16[64,1664]{1,0:T(8,128)(2,1)S(1)}, bf16[64,1664]{1,0:T(8,128)(2,1)S(1)}, u32[]{:S(2)}, u32[]{:S(2)}) collective-permute-start(bf16[64,1664]{1,0:T(8,128)(2,1)S(1)} %constant_dynamic-update-slice_fusion.pa_ref), channel_id=1, source_target_pairs={{0,4},{4,0},{1,5},{5,1},{2,6},{6,2},{3,7},{7,3},{8,12},{12,8},{9,1... | collective-permute-start | bytes 638984 | tf_op jit(solution)/shard_map/ppermute | solution.py:164
  62.4 6.1 %collective-permute-start.5 = (bf16[512,768]{1,0:T(8,128)(2,1)S(1)}, bf16[512,768]{1,0:T(8,128)(2,1)S(1)}, u32[]{:S(2)}, u32[]{:S(2)}) collective-permute-start(bf16[512,768]{1,0:T(8,128)(2,1)S(1)} %bitcast.17), channel_id=1, source_target_pairs={{0,4},{4,0},{1,5},{5,1},{2,6},{6,2},{3,7},{7,3},{8,12},{12,8},{9,1... | collective-permute-start | bytes 2359304 | tf_op jit(solution)/shard_map/ppermute | solution.py:193

commit v9 on v8

--- a/solution.py
+++ b/solution.py
@@ -1,3 +1,4 @@
+import functools
 import math
 
 import jax
@@ -79,12 +80,25 @@
         stat_out_ref[2 * head + 1 : 2 * head + 2, :] = share_n * total_n + share * total
 
 
-def ref_kernel(core_ref, q_ref, own_ref, got_ref, acc_ref, stat_ref, out_ref):
-    first = core_ref[0] == 0
-    for head in range(q_ref.shape[1] // HD):
-        cols = pl.ds(head * HD, HD)
-        keys = jnp.where(first, own_ref[:, cols], got_ref[:, cols])
-        values = jnp.where(first, got_ref[:, cols], own_ref[:, cols]).T
+def split_kernel(side_ref, k_ref, v_ref, out_ref):
+    groups, half = out_ref.shape[1], out_ref.shape[4]
+
+    def move(side):
+        for kind, src in enumerate((k_ref, v_ref)):
+            for group in range(groups):
+                out_ref[:, group, kind] = src[:, :, pl.ds((2 * group + side) * half, half)]
+
+    for side in range(2):
+        pl.when(side_ref[0] == side)(functools.partial(move, side))
+
+
+def ref_heads(q_ref, kv_ref, acc_ref, stat_ref, side, write):
+    count = kv_ref.shape[3] // HD
+    for local in range(count):
+        head = side * count + local
+        cols, lanes = pl.ds(head * HD, HD), pl.ds(local * HD, HD)
+        keys = kv_ref[:, 0, :, lanes].reshape(-1, HD)
+        values = kv_ref[:, 1, :, lanes].reshape(-1, HD).T
         for start in range(0, q_ref.shape[0], STRIP):
             rows = pl.ds(start, STRIP)
             top, total, weights = soft(dot_nt(keys, q_ref[rows, cols]) * UNIT)
@@ -95,7 +109,31 @@
             share_n, share = jnp.exp2(top_n - ceiling), jnp.exp2(top - ceiling)
             scale = 1.0 / (share_n * total_n + share * total)
             merged = (share_n * scale) * acc_ref[cols, rows] + (share * scale) * num
-            out_ref[rows, cols] = merged.astype(jnp.bfloat16).T
+            write(rows, cols, lanes, merged.astype(jnp.bfloat16).T)
+
+
+def own_kernel(core_ref, q_ref, kv_ref, acc_ref, stat_ref, part_ref):
+    def write(rows, cols, lanes, block):
+        part_ref[rows, lanes] = block
+
+    for side in range(2):
+        pl.when(core_ref[0] == side)(
+            functools.partial(ref_heads, q_ref, kv_ref, acc_ref, stat_ref, side, write)
+        )
+
+
+def got_kernel(core_ref, q_ref, kv_ref, acc_ref, stat_ref, part_ref, out_ref):
+    half = part_ref.shape[1]
+
+    def write(rows, cols, lanes, block):
+        out_ref[rows, cols] = block
+
+    def finish(side):
+        out_ref[:, side * half : (side + 1) * half] = part_ref[...]
+        ref_heads(q_ref, kv_ref, acc_ref, stat_ref, 1 - side, write)
+
+    for side in range(2):
+        pl.when(core_ref[0] == side)(functools.partial(finish, side))
 
 
 SMEM = pl.BlockSpec(memory_space=pltpu.SMEM)
@@ -123,15 +161,26 @@
         jax.ShapeDtypeStruct((16, rows), jnp.float32),
     )
 
-    slot_k, slot_v = ref_keys[0], ref_values[0]
-    given = tie(jnp.where(core == 0, slot_v, slot_k))
+    slot_k = ref_keys[0].reshape(n_x, part, -1)
+    slot_v = ref_values[0].reshape(n_x, part, -1)
+    half = width // 2
+    side = core.astype(jnp.int32)[None]
+    split = pl.pallas_call(
+        split_kernel,
+        out_shape=jax.ShapeDtypeStruct((n_x, n_head, 2, part, half), jnp.bfloat16),
+        in_specs=[SMEM, VMEM, VMEM],
+        out_specs=VMEM,
+        compiler_params=near,
+        name="split",
+    )
+    given = split(1 - side, slot_k, slot_v)
     got = lax.ppermute(given, "c", SWAP)
     given, slot_k, slot_v = tie((given, slot_k, slot_v))
-    kept = tie(jnp.where(core == 0, slot_k, slot_v))
+    kept = tie(split(side, slot_k, slot_v))
     mine = jnp.where(owner_c == core, kept, got)
     mine, keys_p, values_p = tie((mine, keys, values))
 
-    spread = lax.all_to_all(mine.reshape(n_x, part, -1), "x", 0, 0, tiled=True)
+    spread = lax.all_to_all(mine.reshape(n_x, -1, half), "x", 0, 0, tiled=True)
     pooled = pl.pallas_call(
         pool_kernel,
         out_shape=jax.ShapeDtypeStruct((POOLS, 2 * width + HD), jnp.bfloat16),
@@ -142,24 +191,24 @@
     )(window_map, pool_segments, keys_p, values_p)
     other = lax.ppermute(pooled, "zh", SWAP)
     piece = lax.dynamic_index_in_dim(spread, owner_x, 0, keepdims=False)
-    piece = piece.reshape(part, n_head, width).transpose(1, 0, 2)
-    piece = jnp.broadcast_to(piece[None], (n_zh, n_head, part, width))
+    piece = piece.reshape(n_head, 2 * part, half)
+    piece = jnp.broadcast_to(piece[None], (n_zh, n_head, 2 * part, half))
     piece, pooled, other = tie((piece, pooled, other))
 
     turned = lax.all_to_all(
-        piece.reshape(n_zh * n_head, part, width), ("zh", "head"), 0, 0, tiled=True
+        piece.reshape(n_zh * n_head, 2 * part, half), ("zh", "head"), 0, 0, tiled=True
     )
     pooled = jnp.concatenate([pooled, other], axis=0)
     other = lax.ppermute(pooled, "x", [(i, i ^ 1) for i in range(n_x)])
     pooled = jnp.concatenate([pooled, other], axis=0)
-    turned = turned.reshape(n_zh, n_head * part, width)
+    turned = turned.reshape(n_zh, n_head * 2 * part, half)
     block = lax.dynamic_index_in_dim(turned, owner_z, 0, keepdims=False)
-    block = jnp.broadcast_to(block[None], (n_x, n_head * part, width))
+    block = jnp.broadcast_to(block[None], (n_x, n_head * 2 * part, half))
     other = lax.ppermute(pooled, "x", [(i, i ^ 2) for i in range(n_x)])
 
     block, queries_w = tie((block, queries))
 
-    own = lax.all_to_all(block, "x", 0, 0, tiled=True).reshape(-1, width)
+    own = lax.all_to_all(block, "x", 0, 0, tiled=True).reshape(-1, 2, part, half)
     pooled = jnp.concatenate([pooled, other], axis=0)
     other = lax.ppermute(pooled, "c", SWAP)
     acc_w, stat_w = pl.pallas_call(
@@ -191,14 +240,27 @@
     own, stat = tie((own, stat))
 
     got = lax.ppermute(own, "c", SWAP)
+    out = pl.pallas_call(
+        own_kernel,
+        out_shape=jax.ShapeDtypeStruct((rows, half), jnp.bfloat16),
+        in_specs=[SMEM] + [VMEM] * 4,
+        out_specs=VMEM,
+        compiler_params=near,
+        cost_estimate=pl.CostEstimate(
+            flops=2 * rows * rows * width,
+            bytes_accessed=5 * rows * width,
+            transcendentals=rows * rows * heads // 2,
+        ),
+        name="own",
+    )(side, queries, own, acc, stat)
     return pl.pallas_call(
-        ref_kernel,
+        got_kernel,
         out_shape=jax.ShapeDtypeStruct((rows, width), jnp.bfloat16),
         in_specs=[SMEM] + [VMEM] * 5,
         out_specs=VMEM,
         compiler_params=near,
-        name="far",
-    )(core.astype(jnp.int32)[None], queries, own, got, acc, stat)
+        name="got",
+    )(side, queries, got, acc, stat, out)
 
 
 def solution(mesh):

time: 72.7 us -> 72.4 us (level)
  local copies, waits for them, and re-layouts: 2.87 us -> 5.02 us
  waiting for transfers between devices: 15.6 us -> 13.8 us
  other arithmetic: 2.65 us -> 1.03 us
    unnamed x17 -> x23, local copies, waits for them, and re-layouts: 0.06 us -> 2.33 us
    select_n x2 -> x0, other arithmetic: 1.66 us -> none  [the longest x1 1.57 us: on_device(): given = tie(jnp.where(core == 0, slot_v, slot_k))]
    ppermute x1, waiting for transfers between devices: 1.89 us -> 0.24 us  [on_device(): got = lax.ppermute(own, 'c', SWAP)]
    pallas_call x1 -> x4, Pallas kernels: 3.77 us -> 4.38 us  [the longest x1 2.59 us: on_device(): pl.pallas_call(got_kernel, out_shape=jax.ShapeDtypeStruct((rows, width),...]
  transfers between devices with their start and end apart: 9 -> 9, of which waited for: 5 -> 5; matrix products, arithmetic and copies ran while one was open for 3% -> 3% of each run, Pallas kernels for 7% -> 9%
where the time goes in v9:
time: 72.4 us; the launch traced here: 71.8 us
  starting transfers between devices  40.9 us (56%)
  waiting for transfers between devices  13.8 us (19%)
  Pallas kernels  9.44 us (13%)
  local copies, waits for them, and re-layouts  5.02 us (7%)
  between operations  1.64 us (2%)
  other arithmetic  1.03 us (1%)
    ppermute x1, starting transfers between devices, on_device(): got = lax.ppermute(given, 'c', SWAP)  8.91 us
    ppermute x1, starting transfers between devices, on_device(): other = lax.ppermute(pooled, 'zh', SWAP)  5.72 us
    all_to_all x1, waiting for transfers between devices, on_device(): spread = lax.all_to_all(mine.reshape(n_x, -1, half), 'x', 0, 0, tiled=True)  5.22 us
    ppermute x1, starting transfers between devices, on_device(): other = lax.ppermute(pooled, 'c', SWAP)  5.18 us
    all_to_all x1, starting transfers between devices, on_device(): lax.all_to_all(piece.reshape(n_zh * n_head, 2 * part, half), ('zh', 'head...  4.89 us
    all_to_all x1, waiting for transfers between devices, on_device(): lax.all_to_all(piece.reshape(n_zh * n_head, 2 * part, half), ('zh', 'head...  4.56 us
    ppermute x1, starting transfers between devices, on_device(): got = lax.ppermute(own, 'c', SWAP)  4.16 us
    all_to_all x1, starting transfers between devices, on_device(): spread = lax.all_to_all(mine.reshape(n_x, -1, half), 'x', 0, 0, tiled=True)  3.49 us
  transfers between devices with their start and end apart: 9, of which 5 were waited for; matrix products, arithmetic and copies ran while one was open for 3% of the time, Pallas kernels for 9%

profile of v9, /device:TPU:1, one launch (start us, length us, event | category | flops | bytes accessed | tf_op | source)
XLA Modules:
  0.0 71.8 jit_solution(7420446836712396)
XLA Ops:
  0.0 1.1 %copy-done.1 = bf16[1,128,3072]{2,1,0:T(8,128)(2,1)S(1)} copy-done((bf16[1,128,3072]{2,1,0:T(8,128)(2,1)S(1)}, bf16[1,128,3072]{2,1,0:T(8,128)(2,1)}, u32[]{:S(2)}) %copy-start.1) | copy-done | bytes 786456
  1.1 1.1 %copy-done.3 = bf16[1,128,3072]{2,1,0:T(8,128)(2,1)S(1)} copy-done((bf16[1,128,3072]{2,1,0:T(8,128)(2,1)S(1)}, bf16[1,128,3072]{2,1,0:T(8,128)(2,1)}, u32[]{:S(2)}) %copy-start.3) | copy-done | bytes 786456
  2.3 0.1 split.2
  2.4 8.9 %collective-permute-start = (bf16[4,4,2,32,384]{4,3,2,1,0:T(8,128)(2,1)S(1)}, bf16[4,4,2,32,384]{4,3,2,1,0:T(8,128)(2,1)S(1)}, u32[]{:S(2)}, u32[]{:S(2)}) collective-permute-start(bf16[4,4,2,32,384]{4,3,2,1,0:T(8,128)(2,1)S(1)} %split.2), channel_id=1, source_target_pairs={{0,4},{4,0},{1,5},{5,1},{2,6},{6,2},{3,7},{7,3},{8,12},{12,8},{9,1... | collective-permute-start | bytes 2359304 | tf_op jit(solution)/shard_map/ppermute | solution.py:177
  12.0 0.1 split.3
  12.0 0.0 copy-start.5
  12.1 0.0 copy-start.6
  12.1 0.0 copy-start.8
  12.1 1.1 %collective-permute-done = bf16[4,4,2,32,384]{4,3,2,1,0:T(8,128)(2,1)S(1)} collective-permute-done((bf16[4,4,2,32,384]{4,3,2,1,0:T(8,128)(2,1)S(1)}, bf16[4,4,2,32,384]{4,3,2,1,0:T(8,128)(2,1)S(1)}, u32[]{:S(2)}, u32[]{:S(2)}) %collective-permute-start) | collective-permute-done | bytes 786464 | tf_op jit(solution)/shard_map/ppermute | solution.py:177
  13.2 1.0 %broadcast_select_fusion = bf16[4,4,2,32,384]{4,3,2,1,0:T(8,128)(2,1)} fusion(bf16[4,4,2,32,384]{4,3,2,1,0:T(8,128)(2,1)S(1)} %split.3, bf16[4,4,2,32,384]{4,3,2,1,0:T(8,128)(2,1)S(1)} %collective-permute-done, pred[]{:T(512)S(6)} %eq.6), kind=kLoop, calls=%fused_computation | loop fusion | flops 393216 | bytes 2359297 | tf_op jit(solution)/shard_map/jit(_where)/select_n | solution.py:180
  14.2 3.5 %all-to-all-start = ((bf16[4,256,384]{2,1,0:T(8,128)(2,1)}), bf16[4,256,384]{2,1,0:T(8,128)(2,1)S(1)}, u32[]{:S(2)}, u32[]{:S(2)}) async-start(bf16[4,256,384]{2,1,0:T(8,128)(2,1)} %bitcast.4), calls=%async_computation | async-start | bytes 1572864 | tf_op jit(solution)/shard_map/all_to_all | solution.py:183
  18.4 0.3 pool.1
  18.7 5.7 %collective-permute-start.1 = (bf16[8,1664]{1,0:T(8,128)(2,1)S(1)}, bf16[8,1664]{1,0:T(8,128)(2,1)S(1)}, u32[]{:S(2)}, u32[]{:S(2)}) collective-permute-start(bf16[8,1664]{1,0:T(8,128)(2,1)S(1)} %pool.1), channel_id=1, source_target_pairs={{0,32},{32,0},{1,33},{33,1},{2,34},{34,2},{3,35},{35,3},{4,36},{36... | collective-permute-start | bytes 79880 | tf_op jit(solution)/shard_map/ppermute | solution.py:192
  24.5 5.2 %all-to-all-done = bf16[4,256,384]{2,1,0:T(8,128)(2,1)S(1)} async-done(((bf16[4,256,384]{2,1,0:T(8,128)(2,1)}), bf16[4,256,384]{2,1,0:T(8,128)(2,1)S(1)}, u32[]{:S(2)}, u32[]{:S(2)}) %all-to-all-start) | async-done | bytes 786464 | tf_op jit(solution)/shard_map/all_to_all | solution.py:183
  29.7 0.0 collective-permute-done.1
  29.7 0.8 %broadcast_in_dim.20 = bf16[2,4,64,384]{3,2,1,0:T(8,128)(2,1)} broadcast(bf16[4,64,384]{2,1,0:T(8,128)(2,1)S(1)} %bitcast.22), dimensions={1,2,3} | broadcast | bytes 589824 | tf_op jit(solution)/shard_map/broadcast_in_dim | solution.py:195
  30.5 4.9 %all-to-all-start.1 = ((bf16[8,64,384]{2,1,0:T(8,128)(2,1)}), bf16[8,64,384]{2,1,0:T(8,128)(2,1)S(1)}, u32[]{:S(2)}, u32[]{:S(2)}) async-start(bf16[8,64,384]{2,1,0:T(8,128)(2,1)} %bitcast.6), calls=%async_computation.1 | async-start | bytes 786432 | tf_op jit(solution)/shard_map/all_to_all | solution.py:198
  35.4 2.2 %collective-permute-start.2 = (bf16[16,1664]{1,0:T(8,128)(2,1)S(1)}, bf16[16,1664]{1,0:T(8,128)(2,1)S(1)}, u32[]{:S(2)}, u32[]{:S(2)}) collective-permute-start(bf16[16,1664]{1,0:T(8,128)(2,1)S(1)} %pad_maximum_fusion.1), channel_id=1, source_target_pairs={{0,8},{8,0},{16,24},{24,16},{1,9},{9,1},{17,25},{25,17},{2,10},{10... | collective-permute-start | bytes 159752 | tf_op jit(solution)/shard_map/ppermute | solution.py:202
  37.6 2.7 %collective-permute-done.2 = bf16[16,1664]{1,0:T(8,128)(2,1)S(1)} collective-permute-done((bf16[16,1664]{1,0:T(8,128)(2,1)S(1)}, bf16[16,1664]{1,0:T(8,128)(2,1)S(1)}, u32[]{:S(2)}, u32[]{:S(2)}) %collective-permute-start.2) | collective-permute-done | bytes 53280 | tf_op jit(solution)/shard_map/ppermute | solution.py:202
  40.3 2.9 %collective-permute-start.3 = (bf16[32,1664]{1,0:T(8,128)(2,1)S(1)}, bf16[32,1664]{1,0:T(8,128)(2,1)}, u32[]{:S(2)}, u32[]{:S(2)}) collective-permute-start(bf16[32,1664]{1,0:T(8,128)(2,1)S(1)} %pad_maximum_fusion), channel_id=1, source_target_pairs={{0,16},{8,24},{16,0},{24,8},{1,17},{9,25},{17,1},{25,9},{2,18},{10... | collective-permute-start | bytes 319496 | tf_op jit(solution)/shard_map/ppermute | solution.py:207
  43.2 4.6 %all-to-all-done.1 = bf16[8,64,384]{2,1,0:T(8,128)(2,1)S(1)} async-done(((bf16[8,64,384]{2,1,0:T(8,128)(2,1)}), bf16[8,64,384]{2,1,0:T(8,128)(2,1)S(1)}, u32[]{:S(2)}, u32[]{:S(2)}) %all-to-all-start.1) | async-done | bytes 393248 | tf_op jit(solution)/shard_map/all_to_all | solution.py:198
  47.8 0.9 %broadcast_in_dim.22 = bf16[4,256,384]{2,1,0:T(8,128)(2,1)} broadcast(bf16[256,384]{1,0:T(8,128)(2,1)S(1)} %dynamic-slice_bitcast_fusion), dimensions={1,2} | broadcast | bytes 983040 | tf_op jit(solution)/shard_map/broadcast_in_dim | solution.py:206
  48.7 3.5 %all-to-all-start.2 = ((bf16[4,256,384]{2,1,0:T(8,128)(2,1)}), bf16[4,256,384]{2,1,0:T(8,128)(2,1)S(1)}, u32[]{:S(2)}, u32[]{:S(2)}) async-start(bf16[4,256,384]{2,1,0:T(8,128)(2,1)} %broadcast_in_dim.22), calls=%async_computation.2 | async-start | bytes 1572864 | tf_op jit(solution)/shard_map/all_to_all | solution.py:211
  52.3 0.0 copy-start.9
  52.3 0.9 %constant_dynamic-update-slice_fusion.pa_ref = bf16[64,1664]{1,0:T(8,128)(2,1)S(1)} fusion(bf16[64,1664]{1,0:T(8,128)(2,1)S(1)} %constant_dynamic-update-slice_fusion.1, bf16[32,1664]{1,0:T(8,128)(2,1)} %collective-permute-done.3), kind=kLoop, calls=%fused_computation.4 | loop fusion | bytes 212992 | tf_op jit(solution)/shard_map/concatenate | solution.py:212
  53.2 5.2 %collective-permute-start.4 = (bf16[64,1664]{1,0:T(8,128)(2,1)S(1)}, bf16[64,1664]{1,0:T(8,128)(2,1)S(1)}, u32[]{:S(2)}, u32[]{:S(2)}) collective-permute-start(bf16[64,1664]{1,0:T(8,128)(2,1)S(1)} %constant_dynamic-update-slice_fusion.pa_ref), channel_id=1, source_target_pairs={{0,4},{4,0},{1,5},{5,1},{2,6},{6,2},{3,7},{7,3},{8,12},{12,8},{9,1... | collective-permute-start | bytes 638984 | tf_op jit(solution)/shard_map/ppermute | solution.py:213
  58.4 2.5 %window.1 = (f32[768,512]{1,0:T(8,128)S(1)}, f32[16,512]{1,0:T(8,128)S(1)}) custom-call(bf16[512,768]{1,0:T(8,128)(2,1)S(1)} %copy-done, bf16[512,768]{1,0:T(8,128)(2,1)S(1)} %copy-done.5, bf16[512,768]{1,0:T(8,128)(2,1)S(1)} %copy-done.7), custom_call_target="tpu_custom_call" | custom-call | flops 805306368 | bytes 3932160 | tf_op jit(solution)/shard_map/window/pallas_call | solution.py:214
  60.9 2.2 %pooled.1 = (f32[768,512]{1,0:T(8,128)S(1)}, f32[16,512]{1,0:T(8,128)S(1)}) custom-call(s32[1]{0:T(128)S(6)} %copy.13.tag_ref, f32[6]{0:T(128)S(1)} %copy-done.9, bf16[512,768]{1,0:T(8,128)(2,1)S(1)} %copy-done, bf16[64,1664]{1,0:T(8,128)(2,1)S(1)} %constant_dynamic-update-slice_fusion.pa_ref, bf16[64,1664]{1,0:T(8,128)(2,1)S(1)} %collective-permute-done.4.pb_ref, ...), custom_call_target="tpu_custom_call" | custom-call | flops 201326592 | bytes 4718592 | tf_op jit(solution)/shard_map/pooled/pallas_call | solution.py:227
  63.2 4.2 %collective-permute-start.5 = (bf16[16,2,32,384]{3,2,1,0:T(8,128)(2,1)S(1)}, bf16[16,2,32,384]{3,2,1,0:T(8,128)(2,1)S(1)}, u32[]{:S(2)}, u32[]{:S(2)}) collective-permute-start(bf16[16,2,32,384]{3,2,1,0:T(8,128)(2,1)S(1)} %bitcast.19), channel_id=1, source_target_pairs={{0,4},{4,0},{1,5},{5,1},{2,6},{6,2},{3,7},{7,3},{8,12},{12,8},{9,1... | collective-permute-start | bytes 2359304 | tf_op jit(solution)/shard_map/ppermute | solution.py:242
  67.4 1.6 %own.1.part_ref = bf16[512,384]{1,0:T(8,128)(2,1)S(1)} custom-call(s32[1]{0:T(128)} %bitcast.side_ref.core_ref, bf16[512,768]{1,0:T(8,128)(2,1)S(1)} %copy-done, bf16[16,2,32,384]{3,2,1,0:T(8,128)(2,1)S(1)} %bitcast.20, f32[768,512]{1,0:T(8,128)S(1)} %get-tuple-element.35.acc_ref, f32[16,512]{1,0:T(8,128)S(1)} %get-tuple-element.36.stat_ref), custom_call_target="tpu_custom_call" | custom-call | flops 402653184 | bytes 1966080 | tf_op jit(solution)/shard_map/own/pallas_call | solution.py:243
  69.0 0.2 collective-permute-done.5.kv_ref
  69.2 2.6 %got.1 = bf16[512,768]{1,0:T(8,128)(2,1)} custom-call(s32[1]{0:T(128)} %bitcast.side_ref.core_ref, bf16[512,768]{1,0:T(8,128)(2,1)S(1)} %copy-done, bf16[16,2,32,384]{3,2,1,0:T(8,128)(2,1)S(1)} %collective-permute-done.5.kv_ref, f32[768,512]{1,0:T(8,128)S(1)} %get-tuple-element.35.acc_ref, f32[16,512]{1,0:T(8,128)S(1)} %get-tuple-element.36.stat_ref, ...), custom_call_target="tpu_custom_call" | custom-call | tf_op jit(solution)/shard_map/got/pallas_call | solution.py:256
  (24 shorter events, 0.1 us)
Async XLA Ops:
  0.0 1.1 %copy-start.1 = (bf16[1,128,3072]{2,1,0:T(8,128)(2,1)S(1)}, bf16[1,128,3072]{2,1,0:T(8,128)(2,1)}, u32[]{:S(2)}) copy-start(bf16[1,128,3072]{2,1,0:T(8,128)(2,1)} %param.15) | copy-start | bytes 2359300
  1.1 1.1 %copy-start.3 = (bf16[1,128,3072]{2,1,0:T(8,128)(2,1)S(1)}, bf16[1,128,3072]{2,1,0:T(8,128)(2,1)}, u32[]{:S(2)}) copy-start(bf16[1,128,3072]{2,1,0:T(8,128)(2,1)} %param.16) | copy-start | bytes 2359300
  2.3 9.7 %copy-start.2 = (bf16[1,128,3072]{2,1,0:T(8,128)(2,1)S(1)}, bf16[1,128,3072]{2,1,0:T(8,128)(2,1)}, u32[]{:S(2)}) copy-start(bf16[1,128,3072]{2,1,0:T(8,128)(2,1)} %param.15) | copy-start | bytes 2359300
  2.3 9.7 %copy-start.4 = (bf16[1,128,3072]{2,1,0:T(8,128)(2,1)S(1)}, bf16[1,128,3072]{2,1,0:T(8,128)(2,1)}, u32[]{:S(2)}) copy-start(bf16[1,128,3072]{2,1,0:T(8,128)(2,1)} %param.16) | copy-start | bytes 2359300
  2.4 10.8 %collective-permute-start = (bf16[4,4,2,32,384]{4,3,2,1,0:T(8,128)(2,1)S(1)}, bf16[4,4,2,32,384]{4,3,2,1,0:T(8,128)(2,1)S(1)}, u32[]{:S(2)}, u32[]{:S(2)}) collective-permute-start(bf16[4,4,2,32,384]{4,3,2,1,0:T(8,128)(2,1)S(1)} %split.2), channel_id=1, source_target_pairs={{0,4},{4,0},{1,5},{5,1},{2,6},{6,2},{3,7},{7,3},{8,12},{12,8},{9,1... | collective-permute-start | bytes 2359304 | tf_op jit(solution)/shard_map/ppermute | solution.py:177
  12.0 6.3 %copy-start.5 = (bf16[512,768]{1,0:T(8,128)(2,1)S(1)}, bf16[512,768]{1,0:T(8,128)(2,1)}, u32[]{:S(2)}) copy-start(bf16[512,768]{1,0:T(8,128)(2,1)} %k_ref.1) | copy-start | bytes 2359300
  12.1 6.3 %copy-start.6 = (bf16[512,768]{1,0:T(8,128)(2,1)S(1)}, bf16[512,768]{1,0:T(8,128)(2,1)}, u32[]{:S(2)}) copy-start(bf16[512,768]{1,0:T(8,128)(2,1)} %v_ref.1) | copy-start | bytes 2359300
  12.1 6.3 %copy-start.8 = (s32[1,512]{1,0:T(1,128)S(1)}, s32[1,512]{1,0:T(1,128)}, u32[]{:S(2)}) copy-start(s32[1,512]{1,0:T(1,128)} %seg_ref.1) | copy-start | bytes 6148
  14.2 15.5 %all-to-all-start = ((bf16[4,256,384]{2,1,0:T(8,128)(2,1)}), bf16[4,256,384]{2,1,0:T(8,128)(2,1)S(1)}, u32[]{:S(2)}, u32[]{:S(2)}) async-start(bf16[4,256,384]{2,1,0:T(8,128)(2,1)} %bitcast.4), calls=%async_computation | async-start | bytes 1572864 | tf_op jit(solution)/shard_map/all_to_all | solution.py:183
  18.7 11.0 %collective-permute-start.1 = (bf16[8,1664]{1,0:T(8,128)(2,1)S(1)}, bf16[8,1664]{1,0:T(8,128)(2,1)S(1)}, u32[]{:S(2)}, u32[]{:S(2)}) collective-permute-start(bf16[8,1664]{1,0:T(8,128)(2,1)S(1)} %pool.1), channel_id=1, source_target_pairs={{0,32},{32,0},{1,33},{33,1},{2,34},{34,2},{3,35},{35,3},{4,36},{36... | collective-permute-start | bytes 79880 | tf_op jit(solution)/shard_map/ppermute | solution.py:192
  30.5 17.3 %all-to-all-start.1 = ((bf16[8,64,384]{2,1,0:T(8,128)(2,1)}), bf16[8,64,384]{2,1,0:T(8,128)(2,1)S(1)}, u32[]{:S(2)}, u32[]{:S(2)}) async-start(bf16[8,64,384]{2,1,0:T(8,128)(2,1)} %bitcast.6), calls=%async_computation.1 | async-start | bytes 786432 | tf_op jit(solution)/shard_map/all_to_all | solution.py:198
  35.4 4.9 %collective-permute-start.2 = (bf16[16,1664]{1,0:T(8,128)(2,1)S(1)}, bf16[16,1664]{1,0:T(8,128)(2,1)S(1)}, u32[]{:S(2)}, u32[]{:S(2)}) collective-permute-start(bf16[16,1664]{1,0:T(8,128)(2,1)S(1)} %pad_maximum_fusion.1), channel_id=1, source_target_pairs={{0,8},{8,0},{16,24},{24,16},{1,9},{9,1},{17,25},{25,17},{2,10},{10... | collective-permute-start | bytes 159752 | tf_op jit(solution)/shard_map/ppermute | solution.py:202
  40.3 12.0 %collective-permute-start.3 = (bf16[32,1664]{1,0:T(8,128)(2,1)S(1)}, bf16[32,1664]{1,0:T(8,128)(2,1)}, u32[]{:S(2)}, u32[]{:S(2)}) collective-permute-start(bf16[32,1664]{1,0:T(8,128)(2,1)S(1)} %pad_maximum_fusion), channel_id=1, source_target_pairs={{0,16},{8,24},{16,0},{24,8},{1,17},{9,25},{17,1},{25,9},{2,18},{10... | collective-permute-start | bytes 319496 | tf_op jit(solution)/shard_map/ppermute | solution.py:207
  47.8 10.6 %copy-start = (bf16[512,768]{1,0:T(8,128)(2,1)S(1)}, bf16[512,768]{1,0:T(8,128)(2,1)}, u32[]{:S(2)}) copy-start(bf16[512,768]{1,0:T(8,128)(2,1)} %q_ref.6) | copy-start | bytes 2359300
  47.8 10.6 %copy-start.7 = (bf16[512,768]{1,0:T(8,128)(2,1)S(1)}, bf16[512,768]{1,0:T(8,128)(2,1)}, u32[]{:S(2)}) copy-start(bf16[512,768]{1,0:T(8,128)(2,1)} %v_ref.1) | copy-start | bytes 2359300
  48.7 14.4 %all-to-all-start.2 = ((bf16[4,256,384]{2,1,0:T(8,128)(2,1)}), bf16[4,256,384]{2,1,0:T(8,128)(2,1)S(1)}, u32[]{:S(2)}, u32[]{:S(2)}) async-start(bf16[4,256,384]{2,1,0:T(8,128)(2,1)} %broadcast_in_dim.22), calls=%async_computation.2 | async-start | bytes 1572864 | tf_op jit(solution)/shard_map/all_to_all | solution.py:211
  52.3 8.7 %copy-start.9 = (f32[6]{0:T(128)S(1)}, f32[6]{0:T(128)}, u32[]{:S(2)}) copy-start(f32[6]{0:T(128)} %slope_ref.1) | copy-start | bytes 76
  53.2 7.7 %collective-permute-start.4 = (bf16[64,1664]{1,0:T(8,128)(2,1)S(1)}, bf16[64,1664]{1,0:T(8,128)(2,1)S(1)}, u32[]{:S(2)}, u32[]{:S(2)}) collective-permute-start(bf16[64,1664]{1,0:T(8,128)(2,1)S(1)} %constant_dynamic-update-slice_fusion.pa_ref), channel_id=1, source_target_pairs={{0,4},{4,0},{1,5},{5,1},{2,6},{6,2},{3,7},{7,3},{8,12},{12,8},{9,1... | collective-permute-start | bytes 638984 | tf_op jit(solution)/shard_map/ppermute | solution.py:213
  63.2 6.1 %collective-permute-start.5 = (bf16[16,2,32,384]{3,2,1,0:T(8,128)(2,1)S(1)}, bf16[16,2,32,384]{3,2,1,0:T(8,128)(2,1)S(1)}, u32[]{:S(2)}, u32[]{:S(2)}) collective-permute-start(bf16[16,2,32,384]{3,2,1,0:T(8,128)(2,1)S(1)} %bitcast.19), channel_id=1, source_target_pairs={{0,4},{4,0},{1,5},{5,1},{2,6},{6,2},{3,7},{7,3},{8,12},{12,8},{9,1... | collective-permute-start | bytes 2359304 | tf_op jit(solution)/shard_map/ppermute | solution.py:242

commit v10 on v9

--- a/solution.py
+++ b/solution.py
@@ -87,6 +87,36 @@
         for kind, src in enumerate((k_ref, v_ref)):
             for group in range(groups):
                 out_ref[:, group, kind] = src[:, :, pl.ds((2 * group + side) * half, half)]
+
+    for side in range(2):
+        pl.when(side_ref[0] == side)(functools.partial(move, side))
+
+
+def give_kernel(side_ref, k_ref, v_ref, out_ref, buf, in_sems, out_sems):
+    groups, half = out_ref.shape[1], out_ref.shape[4]
+
+    def move(side):
+        pairs = [
+            (
+                pltpu.make_async_copy(
+                    src.at[:, :, pl.ds((2 * group + side) * half, half)],
+                    buf.at[:, group, kind],
+                    in_sems.at[kind, group],
+                ),
+                pltpu.make_async_copy(
+                    buf.at[:, group, kind], out_ref.at[:, group, kind], out_sems.at[kind, group]
+                ),
+            )
+            for kind, src in enumerate((k_ref, v_ref))
+            for group in range(groups)
+        ]
+        for fetch, _ in pairs:
+            fetch.start()
+        for fetch, store in pairs:
+            fetch.wait()
+            store.start()
+        for _, store in pairs:
+            store.wait()
 
     for side in range(2):
         pl.when(side_ref[0] == side)(functools.partial(move, side))
@@ -122,15 +152,29 @@
         )
 
 
-def got_kernel(core_ref, q_ref, kv_ref, acc_ref, stat_ref, part_ref, out_ref):
+def got_kernel(core_ref, q_ref, kv_ref, acc_ref, stat_ref, part_ref, out_ref, buf, sems):
     half = part_ref.shape[1]
 
-    def write(rows, cols, lanes, block):
-        out_ref[rows, cols] = block
-
     def finish(side):
-        out_ref[:, side * half : (side + 1) * half] = part_ref[...]
+        done = [
+            pltpu.make_async_copy(
+                part_ref, out_ref.at[:, pl.ds(side * half, half)], sems.at[half // HD]
+            )
+        ]
+        done[0].start()
+
+        def write(rows, cols, lanes, block):
+            buf[rows, lanes] = block
+            if rows.start + rows.size == buf.shape[0]:
+                copy = pltpu.make_async_copy(
+                    buf.at[:, lanes], out_ref.at[:, cols], sems.at[lanes.start // HD]
+                )
+                copy.start()
+                done.append(copy)
+
         ref_heads(q_ref, kv_ref, acc_ref, stat_ref, 1 - side, write)
+        for copy in done:
+            copy.wait()
 
     for side in range(2):
         pl.when(core_ref[0] == side)(functools.partial(finish, side))
@@ -138,6 +182,8 @@
 
 SMEM = pl.BlockSpec(memory_space=pltpu.SMEM)
 VMEM = pl.BlockSpec(memory_space=pltpu.VMEM)
+ANY = pl.BlockSpec(memory_space=pl.ANY)
+GRANT = 63600 * 1024
 
 
 def on_device(
@@ -173,7 +219,19 @@
         compiler_params=near,
         name="split",
     )
-    given = split(1 - side, slot_k, slot_v)
+    given = pl.pallas_call(
+        give_kernel,
+        out_shape=jax.ShapeDtypeStruct((n_x, n_head, 2, part, half), jnp.bfloat16),
+        in_specs=[SMEM, ANY, ANY],
+        out_specs=ANY,
+        scratch_shapes=[
+            pltpu.VMEM((n_x, n_head, 2, part, half), jnp.bfloat16),
+            pltpu.SemaphoreType.DMA((2, n_head)),
+            pltpu.SemaphoreType.DMA((2, n_head)),
+        ],
+        compiler_params=pltpu.CompilerParams(vmem_limit_bytes=GRANT),
+        name="give",
+    )(1 - side, slot_k, slot_v)
     got = lax.ppermute(given, "c", SWAP)
     given, slot_k, slot_v = tie((given, slot_k, slot_v))
     kept = tie(split(side, slot_k, slot_v))
@@ -257,7 +315,11 @@
         got_kernel,
         out_shape=jax.ShapeDtypeStruct((rows, width), jnp.bfloat16),
         in_specs=[SMEM] + [VMEM] * 5,
-        out_specs=VMEM,
+        out_specs=ANY,
+        scratch_shapes=[
+            pltpu.VMEM((rows, half), jnp.bfloat16),
+            pltpu.SemaphoreType.DMA((half // HD + 1,)),
+        ],
         compiler_params=near,
         name="got",
     )(side, queries, got, acc, stat, out)

time: 72.4 us -> 72 us (level)
  local copies, waits for them, and re-layouts: 5.02 us -> 2.75 us
  Pallas kernels: 9.44 us -> 11.2 us
    unnamed x23 -> x17, local copies, waits for them, and re-layouts: 2.33 us -> 0.06 us
    pallas_call x1, Pallas kernels: 0.07 us -> 2.11 us  [on_device(): pl.pallas_call(give_kernel, out_shape=jax.ShapeDtypeStruct((n_x, n_head,...]
where the time goes in v10:
time: 72 us; the launch traced here: 71.4 us
  starting transfers between devices  40.8 us (57%)
  waiting for transfers between devices  14 us (19%)
  Pallas kernels  11.2 us (16%)
  local copies, waits for them, and re-layouts  2.75 us (4%)
  between operations  1.63 us (2%)
  other arithmetic  1.03 us (1%)
    ppermute x1, starting transfers between devices, on_device(): got = lax.ppermute(given, 'c', SWAP)  8.79 us
    ppermute x1, starting transfers between devices, on_device(): other = lax.ppermute(pooled, 'zh', SWAP)  5.72 us
    all_to_all x1, waiting for transfers between devices, on_device(): spread = lax.all_to_all(mine.reshape(n_x, -1, half), 'x', 0, 0, tiled=True)  5.22 us
    ppermute x1, starting transfers between devices, on_device(): other = lax.ppermute(pooled, 'c', SWAP)  5.18 us
    all_to_all x1, starting transfers between devices, on_device(): lax.all_to_all(piece.reshape(n_zh * n_head, 2 * part, half), ('zh', 'head...  4.89 us
    all_to_all x1, waiting for transfers between devices, on_device(): lax.all_to_all(piece.reshape(n_zh * n_head, 2 * part, half), ('zh', 'head...  4.56 us
    ppermute x1, starting transfers between devices, on_device(): got = lax.ppermute(own, 'c', SWAP)  4.18 us
    all_to_all x1, starting transfers between devices, on_device(): spread = lax.all_to_all(mine.reshape(n_x, -1, half), 'x', 0, 0, tiled=True)  3.49 us
  transfers between devices with their start and end apart: 9, of which 5 were waited for; matrix products, arithmetic and copies ran while one was open for 3% of the time, Pallas kernels for 9%

profile of v10, /device:TPU:1, one launch (start us, length us, event | category | flops | bytes accessed | tf_op | source)
XLA Modules:
  0.0 71.4 jit_solution(7651628301045239400)
XLA Ops:
  0.0 2.1 %give.1 = bf16[4,4,2,32,384]{4,3,2,1,0:T(8,128)(2,1)} custom-call(s32[1]{0:T(128)S(6)} %sub.10.side_ref, bf16[4,32,3072]{2,1,0:T(8,128)(2,1)} %bitcast.15, bf16[4,32,3072]{2,1,0:T(8,128)(2,1)} %bitcast.17), custom_call_target="tpu_custom_call" | custom-call | tf_op jit(solution)/shard_map/give/pallas_call | solution.py:222
  2.1 8.8 %collective-permute-start = (bf16[4,4,2,32,384]{4,3,2,1,0:T(8,128)(2,1)}, bf16[4,4,2,32,384]{4,3,2,1,0:T(8,128)(2,1)S(1)}, u32[]{:S(2)}, u32[]{:S(2)}) collective-permute-start(bf16[4,4,2,32,384]{4,3,2,1,0:T(8,128)(2,1)} %give.1), channel_id=1, source_target_pairs={{0,4},{4,0},{1,5},{5,1},{2,6},{6,2},{3,7},{7,3},{8,12},{12,8},{9,1... | collective-permute-start | bytes 2359304 | tf_op jit(solution)/shard_map/ppermute | solution.py:235
  11.6 0.1 split.1
  11.7 0.0 copy-start.3
  11.7 0.0 copy-start.4
  11.7 0.0 copy-start.5
  11.7 1.3 %collective-permute-done = bf16[4,4,2,32,384]{4,3,2,1,0:T(8,128)(2,1)S(1)} collective-permute-done((bf16[4,4,2,32,384]{4,3,2,1,0:T(8,128)(2,1)}, bf16[4,4,2,32,384]{4,3,2,1,0:T(8,128)(2,1)S(1)}, u32[]{:S(2)}, u32[]{:S(2)}) %collective-permute-start) | collective-permute-done | bytes 786464 | tf_op jit(solution)/shard_map/ppermute | solution.py:235
  13.0 1.0 %broadcast_select_fusion = bf16[4,4,2,32,384]{4,3,2,1,0:T(8,128)(2,1)} fusion(bf16[4,4,2,32,384]{4,3,2,1,0:T(8,128)(2,1)S(1)} %split.1, bf16[4,4,2,32,384]{4,3,2,1,0:T(8,128)(2,1)S(1)} %collective-permute-done, pred[]{:T(512)S(6)} %eq.6), kind=kLoop, calls=%fused_computation | loop fusion | flops 393216 | bytes 2359297 | tf_op jit(solution)/shard_map/jit(_where)/select_n | solution.py:238
  14.0 3.5 %all-to-all-start = ((bf16[4,256,384]{2,1,0:T(8,128)(2,1)}), bf16[4,256,384]{2,1,0:T(8,128)(2,1)S(1)}, u32[]{:S(2)}, u32[]{:S(2)}) async-start(bf16[4,256,384]{2,1,0:T(8,128)(2,1)} %bitcast.4), calls=%async_computation | async-start | bytes 1572864 | tf_op jit(solution)/shard_map/all_to_all | solution.py:241
  18.3 0.3 pool.1
  18.6 5.7 %collective-permute-start.1 = (bf16[8,1664]{1,0:T(8,128)(2,1)S(1)}, bf16[8,1664]{1,0:T(8,128)(2,1)S(1)}, u32[]{:S(2)}, u32[]{:S(2)}) collective-permute-start(bf16[8,1664]{1,0:T(8,128)(2,1)S(1)} %pool.1), channel_id=1, source_target_pairs={{0,32},{32,0},{1,33},{33,1},{2,34},{34,2},{3,35},{35,3},{4,36},{36... | collective-permute-start | bytes 79880 | tf_op jit(solution)/shard_map/ppermute | solution.py:250
  24.3 5.2 %all-to-all-done = bf16[4,256,384]{2,1,0:T(8,128)(2,1)S(1)} async-done(((bf16[4,256,384]{2,1,0:T(8,128)(2,1)}), bf16[4,256,384]{2,1,0:T(8,128)(2,1)S(1)}, u32[]{:S(2)}, u32[]{:S(2)}) %all-to-all-start) | async-done | bytes 786464 | tf_op jit(solution)/shard_map/all_to_all | solution.py:241
  29.6 0.0 collective-permute-done.1
  29.6 0.8 %broadcast_in_dim.20 = bf16[2,4,64,384]{3,2,1,0:T(8,128)(2,1)} broadcast(bf16[4,64,384]{2,1,0:T(8,128)(2,1)S(1)} %bitcast.22), dimensions={1,2,3} | broadcast | bytes 589824 | tf_op jit(solution)/shard_map/broadcast_in_dim | solution.py:253
  30.4 4.9 %all-to-all-start.1 = ((bf16[8,64,384]{2,1,0:T(8,128)(2,1)}), bf16[8,64,384]{2,1,0:T(8,128)(2,1)S(1)}, u32[]{:S(2)}, u32[]{:S(2)}) async-start(bf16[8,64,384]{2,1,0:T(8,128)(2,1)} %bitcast.6), calls=%async_computation.1 | async-start | bytes 786432 | tf_op jit(solution)/shard_map/all_to_all | solution.py:256
  35.3 2.2 %collective-permute-start.2 = (bf16[16,1664]{1,0:T(8,128)(2,1)S(1)}, bf16[16,1664]{1,0:T(8,128)(2,1)S(1)}, u32[]{:S(2)}, u32[]{:S(2)}) collective-permute-start(bf16[16,1664]{1,0:T(8,128)(2,1)S(1)} %pad_maximum_fusion.1), channel_id=1, source_target_pairs={{0,8},{8,0},{16,24},{24,16},{1,9},{9,1},{17,25},{25,17},{2,10},{10... | collective-permute-start | bytes 159752 | tf_op jit(solution)/shard_map/ppermute | solution.py:260
  37.5 2.7 %collective-permute-done.2 = bf16[16,1664]{1,0:T(8,128)(2,1)S(1)} collective-permute-done((bf16[16,1664]{1,0:T(8,128)(2,1)S(1)}, bf16[16,1664]{1,0:T(8,128)(2,1)S(1)}, u32[]{:S(2)}, u32[]{:S(2)}) %collective-permute-start.2) | collective-permute-done | bytes 53280 | tf_op jit(solution)/shard_map/ppermute | solution.py:260
  40.2 2.9 %collective-permute-start.3 = (bf16[32,1664]{1,0:T(8,128)(2,1)S(1)}, bf16[32,1664]{1,0:T(8,128)(2,1)}, u32[]{:S(2)}, u32[]{:S(2)}) collective-permute-start(bf16[32,1664]{1,0:T(8,128)(2,1)S(1)} %pad_maximum_fusion), channel_id=1, source_target_pairs={{0,16},{8,24},{16,0},{24,8},{1,17},{9,25},{17,1},{25,9},{2,18},{10... | collective-permute-start | bytes 319496 | tf_op jit(solution)/shard_map/ppermute | solution.py:265
  43.1 4.6 %all-to-all-done.1 = bf16[8,64,384]{2,1,0:T(8,128)(2,1)S(1)} async-done(((bf16[8,64,384]{2,1,0:T(8,128)(2,1)}), bf16[8,64,384]{2,1,0:T(8,128)(2,1)S(1)}, u32[]{:S(2)}, u32[]{:S(2)}) %all-to-all-start.1) | async-done | bytes 393248 | tf_op jit(solution)/shard_map/all_to_all | solution.py:256
  47.7 0.9 %broadcast_in_dim.22 = bf16[4,256,384]{2,1,0:T(8,128)(2,1)} broadcast(bf16[256,384]{1,0:T(8,128)(2,1)S(1)} %dynamic-slice_bitcast_fusion), dimensions={1,2} | broadcast | bytes 983040 | tf_op jit(solution)/shard_map/broadcast_in_dim | solution.py:264
  48.6 3.5 %all-to-all-start.2 = ((bf16[4,256,384]{2,1,0:T(8,128)(2,1)}), bf16[4,256,384]{2,1,0:T(8,128)(2,1)S(1)}, u32[]{:S(2)}, u32[]{:S(2)}) async-start(bf16[4,256,384]{2,1,0:T(8,128)(2,1)} %broadcast_in_dim.22), calls=%async_computation.2 | async-start | bytes 1572864 | tf_op jit(solution)/shard_map/all_to_all | solution.py:269
  52.1 0.0 copy-start.6
  52.1 0.0 collective-permute-done.3
  52.1 0.9 %constant_dynamic-update-slice_fusion.pa_ref = bf16[64,1664]{1,0:T(8,128)(2,1)S(1)} fusion(bf16[64,1664]{1,0:T(8,128)(2,1)S(1)} %constant_dynamic-update-slice_fusion.1, bf16[32,1664]{1,0:T(8,128)(2,1)} %collective-permute-done.3), kind=kLoop, calls=%fused_computation.4 | loop fusion | bytes 212992 | tf_op jit(solution)/shard_map/concatenate | solution.py:270
  53.1 5.2 %collective-permute-start.4 = (bf16[64,1664]{1,0:T(8,128)(2,1)S(1)}, bf16[64,1664]{1,0:T(8,128)(2,1)S(1)}, u32[]{:S(2)}, u32[]{:S(2)}) collective-permute-start(bf16[64,1664]{1,0:T(8,128)(2,1)S(1)} %constant_dynamic-update-slice_fusion.pa_ref), channel_id=1, source_target_pairs={{0,4},{4,0},{1,5},{5,1},{2,6},{6,2},{3,7},{7,3},{8,12},{12,8},{9,1... | collective-permute-start | bytes 638984 | tf_op jit(solution)/shard_map/ppermute | solution.py:271
  58.2 2.5 %window.1 = (f32[768,512]{1,0:T(8,128)S(1)}, f32[16,512]{1,0:T(8,128)S(1)}) custom-call(bf16[512,768]{1,0:T(8,128)(2,1)S(1)} %copy-done, bf16[512,768]{1,0:T(8,128)(2,1)S(1)} %copy-done.3, bf16[512,768]{1,0:T(8,128)(2,1)S(1)} %copy-done.4), custom_call_target="tpu_custom_call" | custom-call | flops 805306368 | bytes 3932160 | tf_op jit(solution)/shard_map/window/pallas_call | solution.py:272
  60.8 0.0 collective-permute-done.4.pb_ref
  60.8 2.2 %pooled.1 = (f32[768,512]{1,0:T(8,128)S(1)}, f32[16,512]{1,0:T(8,128)S(1)}) custom-call(s32[1]{0:T(128)S(6)} %copy.13.tag_ref, f32[6]{0:T(128)S(1)} %copy-done.6, bf16[512,768]{1,0:T(8,128)(2,1)S(1)} %copy-done, bf16[64,1664]{1,0:T(8,128)(2,1)S(1)} %constant_dynamic-update-slice_fusion.pa_ref, bf16[64,1664]{1,0:T(8,128)(2,1)S(1)} %collective-permute-done.4.pb_ref, ...), custom_call_target="tpu_custom_call" | custom-call | flops 201326592 | bytes 4718592 | tf_op jit(solution)/shard_map/pooled/pallas_call | solution.py:285
  63.0 4.2 %collective-permute-start.5 = (bf16[16,2,32,384]{3,2,1,0:T(8,128)(2,1)S(1)}, bf16[16,2,32,384]{3,2,1,0:T(8,128)(2,1)S(1)}, u32[]{:S(2)}, u32[]{:S(2)}) collective-permute-start(bf16[16,2,32,384]{3,2,1,0:T(8,128)(2,1)S(1)} %bitcast.19), channel_id=1, source_target_pairs={{0,4},{4,0},{1,5},{5,1},{2,6},{6,2},{3,7},{7,3},{8,12},{12,8},{9,1... | collective-permute-start | bytes 2359304 | tf_op jit(solution)/shard_map/ppermute | solution.py:300
  67.2 1.6 %own.1.part_ref = bf16[512,384]{1,0:T(8,128)(2,1)S(1)} custom-call(s32[1]{0:T(128)} %bitcast.side_ref.core_ref, bf16[512,768]{1,0:T(8,128)(2,1)S(1)} %copy-done, bf16[16,2,32,384]{3,2,1,0:T(8,128)(2,1)S(1)} %bitcast.20, f32[768,512]{1,0:T(8,128)S(1)} %get-tuple-element.35.acc_ref, f32[16,512]{1,0:T(8,128)S(1)} %get-tuple-element.36.stat_ref), custom_call_target="tpu_custom_call" | custom-call | flops 402653184 | bytes 1966080 | tf_op jit(solution)/shard_map/own/pallas_call | solution.py:301
  68.9 0.2 collective-permute-done.5.kv_ref
  69.1 2.3 %got.1 = bf16[512,768]{1,0:T(8,128)(2,1)} custom-call(s32[1]{0:T(128)} %bitcast.side_ref.core_ref, bf16[512,768]{1,0:T(8,128)(2,1)S(1)} %copy-done, bf16[16,2,32,384]{3,2,1,0:T(8,128)(2,1)S(1)} %collective-permute-done.5.kv_ref, f32[768,512]{1,0:T(8,128)S(1)} %get-tuple-element.35.acc_ref, f32[16,512]{1,0:T(8,128)S(1)} %get-tuple-element.36.stat_ref, ...), custom_call_target="tpu_custom_call" | custom-call | tf_op jit(solution)/shard_map/got/pallas_call | solution.py:314
  (18 shorter events, 0.1 us)
Async XLA Ops:
  0.0 11.6 %copy-start.2 = (bf16[1,128,3072]{2,1,0:T(8,128)(2,1)S(1)}, bf16[1,128,3072]{2,1,0:T(8,128)(2,1)}, u32[]{:S(2)}) copy-start(bf16[1,128,3072]{2,1,0:T(8,128)(2,1)} %param.16) | copy-start | bytes 2359300
  0.0 11.6 %copy-start.1 = (bf16[1,128,3072]{2,1,0:T(8,128)(2,1)S(1)}, bf16[1,128,3072]{2,1,0:T(8,128)(2,1)}, u32[]{:S(2)}) copy-start(bf16[1,128,3072]{2,1,0:T(8,128)(2,1)} %param.15) | copy-start | bytes 2359300
  2.1 10.9 %collective-permute-start = (bf16[4,4,2,32,384]{4,3,2,1,0:T(8,128)(2,1)}, bf16[4,4,2,32,384]{4,3,2,1,0:T(8,128)(2,1)S(1)}, u32[]{:S(2)}, u32[]{:S(2)}) collective-permute-start(bf16[4,4,2,32,384]{4,3,2,1,0:T(8,128)(2,1)} %give.1), channel_id=1, source_target_pairs={{0,4},{4,0},{1,5},{5,1},{2,6},{6,2},{3,7},{7,3},{8,12},{12,8},{9,1... | collective-permute-start | bytes 2359304 | tf_op jit(solution)/shard_map/ppermute | solution.py:235
  11.7 6.6 %copy-start.3 = (bf16[512,768]{1,0:T(8,128)(2,1)S(1)}, bf16[512,768]{1,0:T(8,128)(2,1)}, u32[]{:S(2)}) copy-start(bf16[512,768]{1,0:T(8,128)(2,1)} %k_ref.1) | copy-start | bytes 2359300
  11.7 6.6 %copy-start.4 = (bf16[512,768]{1,0:T(8,128)(2,1)S(1)}, bf16[512,768]{1,0:T(8,128)(2,1)}, u32[]{:S(2)}) copy-start(bf16[512,768]{1,0:T(8,128)(2,1)} %v_ref.1) | copy-start | bytes 2359300
  11.7 6.6 %copy-start.5 = (s32[1,512]{1,0:T(1,128)S(1)}, s32[1,512]{1,0:T(1,128)}, u32[]{:S(2)}) copy-start(s32[1,512]{1,0:T(1,128)} %seg_ref.1) | copy-start | bytes 6148
  14.0 15.5 %all-to-all-start = ((bf16[4,256,384]{2,1,0:T(8,128)(2,1)}), bf16[4,256,384]{2,1,0:T(8,128)(2,1)S(1)}, u32[]{:S(2)}, u32[]{:S(2)}) async-start(bf16[4,256,384]{2,1,0:T(8,128)(2,1)} %bitcast.4), calls=%async_computation | async-start | bytes 1572864 | tf_op jit(solution)/shard_map/all_to_all | solution.py:241
  18.6 11.0 %collective-permute-start.1 = (bf16[8,1664]{1,0:T(8,128)(2,1)S(1)}, bf16[8,1664]{1,0:T(8,128)(2,1)S(1)}, u32[]{:S(2)}, u32[]{:S(2)}) collective-permute-start(bf16[8,1664]{1,0:T(8,128)(2,1)S(1)} %pool.1), channel_id=1, source_target_pairs={{0,32},{32,0},{1,33},{33,1},{2,34},{34,2},{3,35},{35,3},{4,36},{36... | collective-permute-start | bytes 79880 | tf_op jit(solution)/shard_map/ppermute | solution.py:250
  30.4 17.3 %all-to-all-start.1 = ((bf16[8,64,384]{2,1,0:T(8,128)(2,1)}), bf16[8,64,384]{2,1,0:T(8,128)(2,1)S(1)}, u32[]{:S(2)}, u32[]{:S(2)}) async-start(bf16[8,64,384]{2,1,0:T(8,128)(2,1)} %bitcast.6), calls=%async_computation.1 | async-start | bytes 786432 | tf_op jit(solution)/shard_map/all_to_all | solution.py:256
  35.3 4.9 %collective-permute-start.2 = (bf16[16,1664]{1,0:T(8,128)(2,1)S(1)}, bf16[16,1664]{1,0:T(8,128)(2,1)S(1)}, u32[]{:S(2)}, u32[]{:S(2)}) collective-permute-start(bf16[16,1664]{1,0:T(8,128)(2,1)S(1)} %pad_maximum_fusion.1), channel_id=1, source_target_pairs={{0,8},{8,0},{16,24},{24,16},{1,9},{9,1},{17,25},{25,17},{2,10},{10... | collective-permute-start | bytes 159752 | tf_op jit(solution)/shard_map/ppermute | solution.py:260
  40.2 12.0 %collective-permute-start.3 = (bf16[32,1664]{1,0:T(8,128)(2,1)S(1)}, bf16[32,1664]{1,0:T(8,128)(2,1)}, u32[]{:S(2)}, u32[]{:S(2)}) collective-permute-start(bf16[32,1664]{1,0:T(8,128)(2,1)S(1)} %pad_maximum_fusion), channel_id=1, source_target_pairs={{0,16},{8,24},{16,0},{24,8},{1,17},{9,25},{17,1},{25,9},{2,18},{10... | collective-permute-start | bytes 319496 | tf_op jit(solution)/shard_map/ppermute | solution.py:265
  47.6 10.6 %copy-start = (bf16[512,768]{1,0:T(8,128)(2,1)S(1)}, bf16[512,768]{1,0:T(8,128)(2,1)}, u32[]{:S(2)}) copy-start(bf16[512,768]{1,0:T(8,128)(2,1)} %q_ref.6) | copy-start | bytes 2359300
  48.6 14.4 %all-to-all-start.2 = ((bf16[4,256,384]{2,1,0:T(8,128)(2,1)}), bf16[4,256,384]{2,1,0:T(8,128)(2,1)S(1)}, u32[]{:S(2)}, u32[]{:S(2)}) async-start(bf16[4,256,384]{2,1,0:T(8,128)(2,1)} %broadcast_in_dim.22), calls=%async_computation.2 | async-start | bytes 1572864 | tf_op jit(solution)/shard_map/all_to_all | solution.py:269
  52.1 8.7 %copy-start.6 = (f32[6]{0:T(128)S(1)}, f32[6]{0:T(128)}, u32[]{:S(2)}) copy-start(f32[6]{0:T(128)} %slope_ref.1) | copy-start | bytes 76
  53.1 7.7 %collective-permute-start.4 = (bf16[64,1664]{1,0:T(8,128)(2,1)S(1)}, bf16[64,1664]{1,0:T(8,128)(2,1)S(1)}, u32[]{:S(2)}, u32[]{:S(2)}) collective-permute-start(bf16[64,1664]{1,0:T(8,128)(2,1)S(1)} %constant_dynamic-update-slice_fusion.pa_ref), channel_id=1, source_target_pairs={{0,4},{4,0},{1,5},{5,1},{2,6},{6,2},{3,7},{7,3},{8,12},{12,8},{9,1... | collective-permute-start | bytes 638984 | tf_op jit(solution)/shard_map/ppermute | solution.py:271
  63.0 6.1 %collective-permute-start.5 = (bf16[16,2,32,384]{3,2,1,0:T(8,128)(2,1)S(1)}, bf16[16,2,32,384]{3,2,1,0:T(8,128)(2,1)S(1)}, u32[]{:S(2)}, u32[]{:S(2)}) collective-permute-start(bf16[16,2,32,384]{3,2,1,0:T(8,128)(2,1)S(1)} %bitcast.19), channel_id=1, source_target_pairs={{0,4},{4,0},{1,5},{5,1},{2,6},{6,2},{3,7},{7,3},{8,12},{12,8},{9,1... | collective-permute-start | bytes 2359304 | tf_op jit(solution)/shard_map/ppermute | solution.py:300

commit v11 on v10

--- a/solution.py
+++ b/solution.py
@@ -183,7 +183,7 @@
 SMEM = pl.BlockSpec(memory_space=pltpu.SMEM)
 VMEM = pl.BlockSpec(memory_space=pltpu.VMEM)
 ANY = pl.BlockSpec(memory_space=pl.ANY)
-GRANT = 63600 * 1024
+GRANT = 64900 * 1024
 
 
 def on_device(

time: 72 us -> 74 us (1.028)
  local copies, waits for them, and re-layouts: 2.75 us -> 5 us
    unnamed x17, local copies, waits for them, and re-layouts: 0.06 us -> 2.32 us
    ppermute x1, waiting for transfers between devices: 1.29 us -> 0.01 us  [on_device(): got = lax.ppermute(given, 'c', SWAP)]
    all_to_all x1, waiting for transfers between devices: 4.56 us -> 5.66 us  [on_device(): lax.all_to_all(piece.reshape(n_zh * n_head, 2 * part, half), ('zh', 'head...]
  transfers between devices with their start and end apart: 9 -> 9, of which waited for: 5 -> 4; matrix products, arithmetic and copies ran while one was open for 3% -> 3% of each run, Pallas kernels for 9% -> 9%
where the time goes in v11:
time: 74 us; the launch traced here: 73.4 us
  starting transfers between devices  40.4 us (55%)
  waiting for transfers between devices  14.2 us (19%)
  Pallas kernels  11.1 us (15%)
  local copies, waits for them, and re-layouts  5 us (7%)
  between operations  1.63 us (2%)
  other arithmetic  0.99 us (1%)
    ppermute x1, starting transfers between devices, on_device(): got = lax.ppermute(given, 'c', SWAP)  8.79 us
    ppermute x1, starting transfers between devices, on_device(): other = lax.ppermute(pooled, 'zh', SWAP)  5.72 us
    all_to_all x1, waiting for transfers between devices, on_device(): lax.all_to_all(piece.reshape(n_zh * n_head, 2 * part, half), ('zh', 'head...  5.66 us
    all_to_all x1, waiting for transfers between devices, on_device(): spread = lax.all_to_all(mine.reshape(n_x, -1, half), 'x', 0, 0, tiled=True)  5.62 us
    all_to_all x1, starting transfers between devices, on_device(): lax.all_to_all(piece.reshape(n_zh * n_head, 2 * part, half), ('zh', 'head...  4.89 us
    ppermute x1, starting transfers between devices, on_device(): got = lax.ppermute(own, 'c', SWAP)  4.89 us
    ppermute x1, starting transfers between devices, on_device(): other = lax.ppermute(pooled, 'c', SWAP)  4.46 us
    all_to_all x1, starting transfers between devices, on_device(): lax.all_to_all(block, 'x', 0, 0, tiled=True).reshape(-1, 2, part, half)  3.49 us
  transfers between devices with their start and end apart: 9, of which 4 were waited for; matrix products, arithmetic and copies ran while one was open for 3% of the time, Pallas kernels for 9%

profile of v11, /device:TPU:1, one launch (start us, length us, event | category | flops | bytes accessed | tf_op | source)
XLA Modules:
  0.0 73.4 jit_solution(3852313097856619102)
XLA Ops:
  0.0 2.0 %give.1 = bf16[4,4,2,32,384]{4,3,2,1,0:T(8,128)(2,1)} custom-call(s32[1]{0:T(128)S(6)} %sub.10.side_ref, bf16[4,32,3072]{2,1,0:T(8,128)(2,1)} %bitcast.15, bf16[4,32,3072]{2,1,0:T(8,128)(2,1)} %bitcast.17), custom_call_target="tpu_custom_call" | custom-call | tf_op jit(solution)/shard_map/give/pallas_call | solution.py:222
  2.0 8.8 %collective-permute-start = (bf16[4,4,2,32,384]{4,3,2,1,0:T(8,128)(2,1)}, bf16[4,4,2,32,384]{4,3,2,1,0:T(8,128)(2,1)S(1)}, u32[]{:S(2)}, u32[]{:S(2)}) collective-permute-start(bf16[4,4,2,32,384]{4,3,2,1,0:T(8,128)(2,1)} %give.1), channel_id=1, source_target_pairs={{0,4},{4,0},{1,5},{5,1},{2,6},{6,2},{3,7},{7,3},{8,12},{12,8},{9,1... | collective-permute-start | bytes 2359304 | tf_op jit(solution)/shard_map/ppermute | solution.py:235
  11.5 0.0 copy-start.1
  11.5 1.1 %copy-done.1 = bf16[1,128,3072]{2,1,0:T(8,128)(2,1)S(1)} copy-done((bf16[1,128,3072]{2,1,0:T(8,128)(2,1)S(1)}, bf16[1,128,3072]{2,1,0:T(8,128)(2,1)}, u32[]{:S(2)}) %copy-start.1) | copy-done | bytes 786456
  12.6 1.1 %copy-done.2 = bf16[1,128,3072]{2,1,0:T(8,128)(2,1)S(1)} copy-done((bf16[1,128,3072]{2,1,0:T(8,128)(2,1)S(1)}, bf16[1,128,3072]{2,1,0:T(8,128)(2,1)}, u32[]{:S(2)}) %copy-start.2) | copy-done | bytes 786456
  13.7 0.1 split.1
  13.8 0.0 copy-start.3
  13.8 0.0 copy-start.4
  13.8 0.0 copy-start.5
  13.9 1.0 %broadcast_select_fusion = bf16[4,4,2,32,384]{4,3,2,1,0:T(8,128)(2,1)} fusion(bf16[4,4,2,32,384]{4,3,2,1,0:T(8,128)(2,1)S(1)} %split.1, bf16[4,4,2,32,384]{4,3,2,1,0:T(8,128)(2,1)S(1)} %collective-permute-done, pred[]{:T(512)S(6)} %eq.6), kind=kLoop, calls=%fused_computation | loop fusion | flops 393216 | bytes 2359297 | tf_op jit(solution)/shard_map/jit(_where)/select_n | solution.py:238
  14.8 3.5 %all-to-all-start = ((bf16[4,256,384]{2,1,0:T(8,128)(2,1)}), bf16[4,256,384]{2,1,0:T(8,128)(2,1)S(1)}, u32[]{:S(2)}, u32[]{:S(2)}) async-start(bf16[4,256,384]{2,1,0:T(8,128)(2,1)} %bitcast.4), calls=%async_computation | async-start | bytes 1572864 | tf_op jit(solution)/shard_map/all_to_all | solution.py:241
  19.1 0.3 pool.1
  19.4 5.7 %collective-permute-start.1 = (bf16[8,1664]{1,0:T(8,128)(2,1)S(1)}, bf16[8,1664]{1,0:T(8,128)(2,1)S(1)}, u32[]{:S(2)}, u32[]{:S(2)}) collective-permute-start(bf16[8,1664]{1,0:T(8,128)(2,1)S(1)} %pool.1), channel_id=1, source_target_pairs={{0,32},{32,0},{1,33},{33,1},{2,34},{34,2},{3,35},{35,3},{4,36},{36... | collective-permute-start | bytes 79880 | tf_op jit(solution)/shard_map/ppermute | solution.py:250
  25.1 5.6 %all-to-all-done = bf16[4,256,384]{2,1,0:T(8,128)(2,1)S(1)} async-done(((bf16[4,256,384]{2,1,0:T(8,128)(2,1)}), bf16[4,256,384]{2,1,0:T(8,128)(2,1)S(1)}, u32[]{:S(2)}, u32[]{:S(2)}) %all-to-all-start) | async-done | bytes 786464 | tf_op jit(solution)/shard_map/all_to_all | solution.py:241
  30.8 0.8 %broadcast_in_dim.20 = bf16[2,4,64,384]{3,2,1,0:T(8,128)(2,1)} broadcast(bf16[4,64,384]{2,1,0:T(8,128)(2,1)S(1)} %bitcast.22), dimensions={1,2,3} | broadcast | bytes 589824 | tf_op jit(solution)/shard_map/broadcast_in_dim | solution.py:253
  31.6 4.9 %all-to-all-start.1 = ((bf16[8,64,384]{2,1,0:T(8,128)(2,1)}), bf16[8,64,384]{2,1,0:T(8,128)(2,1)S(1)}, u32[]{:S(2)}, u32[]{:S(2)}) async-start(bf16[8,64,384]{2,1,0:T(8,128)(2,1)} %bitcast.6), calls=%async_computation.1 | async-start | bytes 786432 | tf_op jit(solution)/shard_map/all_to_all | solution.py:256
  36.5 2.2 %collective-permute-start.2 = (bf16[16,1664]{1,0:T(8,128)(2,1)S(1)}, bf16[16,1664]{1,0:T(8,128)(2,1)S(1)}, u32[]{:S(2)}, u32[]{:S(2)}) collective-permute-start(bf16[16,1664]{1,0:T(8,128)(2,1)S(1)} %pad_maximum_fusion.1), channel_id=1, source_target_pairs={{0,8},{8,0},{16,24},{24,16},{1,9},{9,1},{17,25},{25,17},{2,10},{10... | collective-permute-start | bytes 159752 | tf_op jit(solution)/shard_map/ppermute | solution.py:260
  38.7 2.7 %collective-permute-done.2 = bf16[16,1664]{1,0:T(8,128)(2,1)S(1)} collective-permute-done((bf16[16,1664]{1,0:T(8,128)(2,1)S(1)}, bf16[16,1664]{1,0:T(8,128)(2,1)S(1)}, u32[]{:S(2)}, u32[]{:S(2)}) %collective-permute-start.2) | collective-permute-done | bytes 53280 | tf_op jit(solution)/shard_map/ppermute | solution.py:260
  41.4 2.5 %collective-permute-start.3 = (bf16[32,1664]{1,0:T(8,128)(2,1)S(1)}, bf16[32,1664]{1,0:T(8,128)(2,1)}, u32[]{:S(2)}, u32[]{:S(2)}) collective-permute-start(bf16[32,1664]{1,0:T(8,128)(2,1)S(1)} %pad_maximum_fusion), channel_id=1, source_target_pairs={{0,16},{8,24},{16,0},{24,8},{1,17},{9,25},{17,1},{25,9},{2,18},{10... | collective-permute-start | bytes 319496 | tf_op jit(solution)/shard_map/ppermute | solution.py:265
  43.9 5.7 %all-to-all-done.1 = bf16[8,64,384]{2,1,0:T(8,128)(2,1)S(1)} async-done(((bf16[8,64,384]{2,1,0:T(8,128)(2,1)}), bf16[8,64,384]{2,1,0:T(8,128)(2,1)S(1)}, u32[]{:S(2)}, u32[]{:S(2)}) %all-to-all-start.1) | async-done | bytes 393248 | tf_op jit(solution)/shard_map/all_to_all | solution.py:256
  49.6 0.9 %broadcast_in_dim.22 = bf16[4,256,384]{2,1,0:T(8,128)(2,1)} broadcast(bf16[256,384]{1,0:T(8,128)(2,1)S(1)} %dynamic-slice_bitcast_fusion), dimensions={1,2} | broadcast | bytes 983040 | tf_op jit(solution)/shard_map/broadcast_in_dim | solution.py:264
  50.5 3.5 %all-to-all-start.2 = ((bf16[4,256,384]{2,1,0:T(8,128)(2,1)}), bf16[4,256,384]{2,1,0:T(8,128)(2,1)S(1)}, u32[]{:S(2)}, u32[]{:S(2)}) async-start(bf16[4,256,384]{2,1,0:T(8,128)(2,1)} %broadcast_in_dim.22), calls=%async_computation.2 | async-start | bytes 1572864 | tf_op jit(solution)/shard_map/all_to_all | solution.py:269
  54.0 0.0 copy-start.6
  54.0 0.0 collective-permute-done.3
  54.1 0.9 %constant_dynamic-update-slice_fusion.pa_ref = bf16[64,1664]{1,0:T(8,128)(2,1)S(1)} fusion(bf16[64,1664]{1,0:T(8,128)(2,1)S(1)} %constant_dynamic-update-slice_fusion.1, bf16[32,1664]{1,0:T(8,128)(2,1)} %collective-permute-done.3), kind=kLoop, calls=%fused_computation.4 | loop fusion | bytes 212992 | tf_op jit(solution)/shard_map/concatenate | solution.py:270
  55.0 4.5 %collective-permute-start.4 = (bf16[64,1664]{1,0:T(8,128)(2,1)S(1)}, bf16[64,1664]{1,0:T(8,128)(2,1)S(1)}, u32[]{:S(2)}, u32[]{:S(2)}) collective-permute-start(bf16[64,1664]{1,0:T(8,128)(2,1)S(1)} %constant_dynamic-update-slice_fusion.pa_ref), channel_id=1, source_target_pairs={{0,4},{4,0},{1,5},{5,1},{2,6},{6,2},{3,7},{7,3},{8,12},{12,8},{9,1... | collective-permute-start | bytes 638984 | tf_op jit(solution)/shard_map/ppermute | solution.py:271
  59.4 2.5 %window.1 = (f32[768,512]{1,0:T(8,128)S(1)}, f32[16,512]{1,0:T(8,128)S(1)}) custom-call(bf16[512,768]{1,0:T(8,128)(2,1)S(1)} %copy-done, bf16[512,768]{1,0:T(8,128)(2,1)S(1)} %copy-done.3, bf16[512,768]{1,0:T(8,128)(2,1)S(1)} %copy-done.4), custom_call_target="tpu_custom_call" | custom-call | flops 805306368 | bytes 3932160 | tf_op jit(solution)/shard_map/window/pallas_call | solution.py:272
  62.0 2.2 %pooled.1 = (f32[768,512]{1,0:T(8,128)S(1)}, f32[16,512]{1,0:T(8,128)S(1)}) custom-call(s32[1]{0:T(128)S(6)} %copy.13.tag_ref, f32[6]{0:T(128)S(1)} %copy-done.6, bf16[512,768]{1,0:T(8,128)(2,1)S(1)} %copy-done, bf16[64,1664]{1,0:T(8,128)(2,1)S(1)} %constant_dynamic-update-slice_fusion.pa_ref, bf16[64,1664]{1,0:T(8,128)(2,1)S(1)} %collective-permute-done.4.pb_ref, ...), custom_call_target="tpu_custom_call" | custom-call | flops 201326592 | bytes 4718592 | tf_op jit(solution)/shard_map/pooled/pallas_call | solution.py:285
  64.2 4.9 %collective-permute-start.5 = (bf16[16,2,32,384]{3,2,1,0:T(8,128)(2,1)S(1)}, bf16[16,2,32,384]{3,2,1,0:T(8,128)(2,1)S(1)}, u32[]{:S(2)}, u32[]{:S(2)}) collective-permute-start(bf16[16,2,32,384]{3,2,1,0:T(8,128)(2,1)S(1)} %bitcast.19), channel_id=1, source_target_pairs={{0,4},{4,0},{1,5},{5,1},{2,6},{6,2},{3,7},{7,3},{8,12},{12,8},{9,1... | collective-permute-start | bytes 2359304 | tf_op jit(solution)/shard_map/ppermute | solution.py:300
  69.1 1.6 %own.1.part_ref = bf16[512,384]{1,0:T(8,128)(2,1)S(1)} custom-call(s32[1]{0:T(128)} %bitcast.side_ref.core_ref, bf16[512,768]{1,0:T(8,128)(2,1)S(1)} %copy-done, bf16[16,2,32,384]{3,2,1,0:T(8,128)(2,1)S(1)} %bitcast.20, f32[768,512]{1,0:T(8,128)S(1)} %get-tuple-element.35.acc_ref, f32[16,512]{1,0:T(8,128)S(1)} %get-tuple-element.36.stat_ref), custom_call_target="tpu_custom_call" | custom-call | flops 402653184 | bytes 1966080 | tf_op jit(solution)/shard_map/own/pallas_call | solution.py:301
  70.8 0.2 collective-permute-done.5.kv_ref
  71.0 2.4 %got.1 = bf16[512,768]{1,0:T(8,128)(2,1)} custom-call(s32[1]{0:T(128)} %bitcast.side_ref.core_ref, bf16[512,768]{1,0:T(8,128)(2,1)S(1)} %copy-done, bf16[16,2,32,384]{3,2,1,0:T(8,128)(2,1)S(1)} %collective-permute-done.5.kv_ref, f32[768,512]{1,0:T(8,128)S(1)} %get-tuple-element.35.acc_ref, f32[16,512]{1,0:T(8,128)S(1)} %get-tuple-element.36.stat_ref, ...), custom_call_target="tpu_custom_call" | custom-call | tf_op jit(solution)/shard_map/got/pallas_call | solution.py:314
  (18 shorter events, 0.1 us)
Async XLA Ops:
  2.0 11.8 %collective-permute-start = (bf16[4,4,2,32,384]{4,3,2,1,0:T(8,128)(2,1)}, bf16[4,4,2,32,384]{4,3,2,1,0:T(8,128)(2,1)S(1)}, u32[]{:S(2)}, u32[]{:S(2)}) collective-permute-start(bf16[4,4,2,32,384]{4,3,2,1,0:T(8,128)(2,1)} %give.1), channel_id=1, source_target_pairs={{0,4},{4,0},{1,5},{5,1},{2,6},{6,2},{3,7},{7,3},{8,12},{12,8},{9,1... | collective-permute-start | bytes 2359304 | tf_op jit(solution)/shard_map/ppermute | solution.py:235
  11.5 1.1 %copy-start.1 = (bf16[1,128,3072]{2,1,0:T(8,128)(2,1)S(1)}, bf16[1,128,3072]{2,1,0:T(8,128)(2,1)}, u32[]{:S(2)}) copy-start(bf16[1,128,3072]{2,1,0:T(8,128)(2,1)} %param.15) | copy-start | bytes 2359300
  12.6 1.1 %copy-start.2 = (bf16[1,128,3072]{2,1,0:T(8,128)(2,1)S(1)}, bf16[1,128,3072]{2,1,0:T(8,128)(2,1)}, u32[]{:S(2)}) copy-start(bf16[1,128,3072]{2,1,0:T(8,128)(2,1)} %param.16) | copy-start | bytes 2359300
  13.8 5.2 %copy-start.3 = (bf16[512,768]{1,0:T(8,128)(2,1)S(1)}, bf16[512,768]{1,0:T(8,128)(2,1)}, u32[]{:S(2)}) copy-start(bf16[512,768]{1,0:T(8,128)(2,1)} %k_ref.1) | copy-start | bytes 2359300
  13.8 5.2 %copy-start.4 = (bf16[512,768]{1,0:T(8,128)(2,1)S(1)}, bf16[512,768]{1,0:T(8,128)(2,1)}, u32[]{:S(2)}) copy-start(bf16[512,768]{1,0:T(8,128)(2,1)} %v_ref.1) | copy-start | bytes 2359300
  13.8 5.2 %copy-start.5 = (s32[1,512]{1,0:T(1,128)S(1)}, s32[1,512]{1,0:T(1,128)}, u32[]{:S(2)}) copy-start(s32[1,512]{1,0:T(1,128)} %seg_ref.1) | copy-start | bytes 6148
  14.8 15.9 %all-to-all-start = ((bf16[4,256,384]{2,1,0:T(8,128)(2,1)}), bf16[4,256,384]{2,1,0:T(8,128)(2,1)S(1)}, u32[]{:S(2)}, u32[]{:S(2)}) async-start(bf16[4,256,384]{2,1,0:T(8,128)(2,1)} %bitcast.4), calls=%async_computation | async-start | bytes 1572864 | tf_op jit(solution)/shard_map/all_to_all | solution.py:241
  19.4 11.4 %collective-permute-start.1 = (bf16[8,1664]{1,0:T(8,128)(2,1)S(1)}, bf16[8,1664]{1,0:T(8,128)(2,1)S(1)}, u32[]{:S(2)}, u32[]{:S(2)}) collective-permute-start(bf16[8,1664]{1,0:T(8,128)(2,1)S(1)} %pool.1), channel_id=1, source_target_pairs={{0,32},{32,0},{1,33},{33,1},{2,34},{34,2},{3,35},{35,3},{4,36},{36... | collective-permute-start | bytes 79880 | tf_op jit(solution)/shard_map/ppermute | solution.py:250
  31.6 18.0 %all-to-all-start.1 = ((bf16[8,64,384]{2,1,0:T(8,128)(2,1)}), bf16[8,64,384]{2,1,0:T(8,128)(2,1)S(1)}, u32[]{:S(2)}, u32[]{:S(2)}) async-start(bf16[8,64,384]{2,1,0:T(8,128)(2,1)} %bitcast.6), calls=%async_computation.1 | async-start | bytes 786432 | tf_op jit(solution)/shard_map/all_to_all | solution.py:256
  36.5 4.9 %collective-permute-start.2 = (bf16[16,1664]{1,0:T(8,128)(2,1)S(1)}, bf16[16,1664]{1,0:T(8,128)(2,1)S(1)}, u32[]{:S(2)}, u32[]{:S(2)}) collective-permute-start(bf16[16,1664]{1,0:T(8,128)(2,1)S(1)} %pad_maximum_fusion.1), channel_id=1, source_target_pairs={{0,8},{8,0},{16,24},{24,16},{1,9},{9,1},{17,25},{25,17},{2,10},{10... | collective-permute-start | bytes 159752 | tf_op jit(solution)/shard_map/ppermute | solution.py:260
  41.4 12.7 %collective-permute-start.3 = (bf16[32,1664]{1,0:T(8,128)(2,1)S(1)}, bf16[32,1664]{1,0:T(8,128)(2,1)}, u32[]{:S(2)}, u32[]{:S(2)}) collective-permute-start(bf16[32,1664]{1,0:T(8,128)(2,1)S(1)} %pad_maximum_fusion), channel_id=1, source_target_pairs={{0,16},{8,24},{16,0},{24,8},{1,17},{9,25},{17,1},{25,9},{2,18},{10... | collective-permute-start | bytes 319496 | tf_op jit(solution)/shard_map/ppermute | solution.py:265
  49.5 9.9 %copy-start = (bf16[512,768]{1,0:T(8,128)(2,1)S(1)}, bf16[512,768]{1,0:T(8,128)(2,1)}, u32[]{:S(2)}) copy-start(bf16[512,768]{1,0:T(8,128)(2,1)} %q_ref.6) | copy-start | bytes 2359300
  50.5 13.7 %all-to-all-start.2 = ((bf16[4,256,384]{2,1,0:T(8,128)(2,1)}), bf16[4,256,384]{2,1,0:T(8,128)(2,1)S(1)}, u32[]{:S(2)}, u32[]{:S(2)}) async-start(bf16[4,256,384]{2,1,0:T(8,128)(2,1)} %broadcast_in_dim.22), calls=%async_computation.2 | async-start | bytes 1572864 | tf_op jit(solution)/shard_map/all_to_all | solution.py:269
  54.0 7.9 %copy-start.6 = (f32[6]{0:T(128)S(1)}, f32[6]{0:T(128)}, u32[]{:S(2)}) copy-start(f32[6]{0:T(128)} %slope_ref.1) | copy-start | bytes 76
  55.0 7.0 %collective-permute-start.4 = (bf16[64,1664]{1,0:T(8,128)(2,1)S(1)}, bf16[64,1664]{1,0:T(8,128)(2,1)S(1)}, u32[]{:S(2)}, u32[]{:S(2)}) collective-permute-start(bf16[64,1664]{1,0:T(8,128)(2,1)S(1)} %constant_dynamic-update-slice_fusion.pa_ref), channel_id=1, source_target_pairs={{0,4},{4,0},{1,5},{5,1},{2,6},{6,2},{3,7},{7,3},{8,12},{12,8},{9,1... | collective-permute-start | bytes 638984 | tf_op jit(solution)/shard_map/ppermute | solution.py:271
  64.2 6.8 %collective-permute-start.5 = (bf16[16,2,32,384]{3,2,1,0:T(8,128)(2,1)S(1)}, bf16[16,2,32,384]{3,2,1,0:T(8,128)(2,1)S(1)}, u32[]{:S(2)}, u32[]{:S(2)}) collective-permute-start(bf16[16,2,32,384]{3,2,1,0:T(8,128)(2,1)S(1)} %bitcast.19), channel_id=1, source_target_pairs={{0,4},{4,0},{1,5},{5,1},{2,6},{6,2},{3,7},{7,3},{8,12},{12,8},{9,1... | collective-permute-start | bytes 2359304 | tf_op jit(solution)/shard_map/ppermute | solution.py:300

commit v12 on v10

--- a/solution.py
+++ b/solution.py
@@ -257,12 +257,12 @@
         piece.reshape(n_zh * n_head, 2 * part, half), ("zh", "head"), 0, 0, tiled=True
     )
     pooled = jnp.concatenate([pooled, other], axis=0)
-    other = lax.ppermute(pooled, "x", [(i, i ^ 1) for i in range(n_x)])
+    other = lax.ppermute(pooled, "x", [(i, i ^ 2) for i in range(n_x)])
     pooled = jnp.concatenate([pooled, other], axis=0)
     turned = turned.reshape(n_zh, n_head * 2 * part, half)
     block = lax.dynamic_index_in_dim(turned, owner_z, 0, keepdims=False)
     block = jnp.broadcast_to(block[None], (n_x, n_head * 2 * part, half))
-    other = lax.ppermute(pooled, "x", [(i, i ^ 2) for i in range(n_x)])
+    other = lax.ppermute(pooled, "x", [(i, i ^ 1) for i in range(n_x)])
 
     block, queries_w = tie((block, queries))
 

time: 72 us -> 72 us (level)
    ppermute x1, waiting for transfers between devices: 0.01 us -> 3.45 us  [on_device(): other = lax.ppermute(pooled, 'x', [(i, i ^ 2) for i in range(n_x)])]
    ppermute x1, waiting for transfers between devices: 2.65 us -> 0.01 us  [on_device(): other = lax.ppermute(pooled, 'x', [(i, i ^ 1) for i in range(n_x)])]
    all_to_all x1, waiting for transfers between devices: 4.56 us -> 3.77 us  [on_device(): lax.all_to_all(piece.reshape(n_zh * n_head, 2 * part, half), ('zh', 'head...]
where the time goes in v12:
time: 72 us; the launch traced here: 71.4 us
  starting transfers between devices  40.8 us (57%)
  waiting for transfers between devices  14 us (19%)
  Pallas kernels  11.2 us (16%)
  local copies, waits for them, and re-layouts  2.75 us (4%)
  between operations  1.63 us (2%)
  other arithmetic  1.03 us (1%)
    ppermute x1, starting transfers between devices, on_device(): got = lax.ppermute(given, 'c', SWAP)  8.79 us
    ppermute x1, starting transfers between devices, on_device(): other = lax.ppermute(pooled, 'zh', SWAP)  5.72 us
    all_to_all x1, waiting for transfers between devices, on_device(): spread = lax.all_to_all(mine.reshape(n_x, -1, half), 'x', 0, 0, tiled=True)  5.22 us
    ppermute x1, starting transfers between devices, on_device(): other = lax.ppermute(pooled, 'c', SWAP)  5.18 us
    all_to_all x1, starting transfers between devices, on_device(): lax.all_to_all(piece.reshape(n_zh * n_head, 2 * part, half), ('zh', 'head...  4.89 us
    ppermute x1, starting transfers between devices, on_device(): got = lax.ppermute(own, 'c', SWAP)  4.18 us
    all_to_all x1, waiting for transfers between devices, on_device(): lax.all_to_all(piece.reshape(n_zh * n_head, 2 * part, half), ('zh', 'head...  3.77 us
    all_to_all x1, starting transfers between devices, on_device(): spread = lax.all_to_all(mine.reshape(n_x, -1, half), 'x', 0, 0, tiled=True)  3.49 us
  transfers between devices with their start and end apart: 9, of which 5 were waited for; matrix products, arithmetic and copies ran while one was open for 3% of the time, Pallas kernels for 9%

profile of v12, /device:TPU:1, one launch (start us, length us, event | category | flops | bytes accessed | tf_op | source)
XLA Modules:
  0.0 71.4 jit_solution(6053849928811747315)
XLA Ops:
  0.0 2.1 %give.1 = bf16[4,4,2,32,384]{4,3,2,1,0:T(8,128)(2,1)} custom-call(s32[1]{0:T(128)S(6)} %sub.10.side_ref, bf16[4,32,3072]{2,1,0:T(8,128)(2,1)} %bitcast.15, bf16[4,32,3072]{2,1,0:T(8,128)(2,1)} %bitcast.17), custom_call_target="tpu_custom_call" | custom-call | tf_op jit(solution)/shard_map/give/pallas_call | solution.py:222
  2.1 8.8 %collective-permute-start = (bf16[4,4,2,32,384]{4,3,2,1,0:T(8,128)(2,1)}, bf16[4,4,2,32,384]{4,3,2,1,0:T(8,128)(2,1)S(1)}, u32[]{:S(2)}, u32[]{:S(2)}) collective-permute-start(bf16[4,4,2,32,384]{4,3,2,1,0:T(8,128)(2,1)} %give.1), channel_id=1, source_target_pairs={{0,4},{4,0},{1,5},{5,1},{2,6},{6,2},{3,7},{7,3},{8,12},{12,8},{9,1... | collective-permute-start | bytes 2359304 | tf_op jit(solution)/shard_map/ppermute | solution.py:235
  11.6 0.1 split.1
  11.7 0.0 copy-start.3
  11.7 0.0 copy-start.4
  11.7 0.0 copy-start.5
  11.7 1.3 %collective-permute-done = bf16[4,4,2,32,384]{4,3,2,1,0:T(8,128)(2,1)S(1)} collective-permute-done((bf16[4,4,2,32,384]{4,3,2,1,0:T(8,128)(2,1)}, bf16[4,4,2,32,384]{4,3,2,1,0:T(8,128)(2,1)S(1)}, u32[]{:S(2)}, u32[]{:S(2)}) %collective-permute-start) | collective-permute-done | bytes 786464 | tf_op jit(solution)/shard_map/ppermute | solution.py:235
  13.0 1.0 %broadcast_select_fusion = bf16[4,4,2,32,384]{4,3,2,1,0:T(8,128)(2,1)} fusion(bf16[4,4,2,32,384]{4,3,2,1,0:T(8,128)(2,1)S(1)} %split.1, bf16[4,4,2,32,384]{4,3,2,1,0:T(8,128)(2,1)S(1)} %collective-permute-done, pred[]{:T(512)S(6)} %eq.6), kind=kLoop, calls=%fused_computation | loop fusion | flops 393216 | bytes 2359297 | tf_op jit(solution)/shard_map/jit(_where)/select_n | solution.py:238
  14.0 3.5 %all-to-all-start = ((bf16[4,256,384]{2,1,0:T(8,128)(2,1)}), bf16[4,256,384]{2,1,0:T(8,128)(2,1)S(1)}, u32[]{:S(2)}, u32[]{:S(2)}) async-start(bf16[4,256,384]{2,1,0:T(8,128)(2,1)} %bitcast.4), calls=%async_computation | async-start | bytes 1572864 | tf_op jit(solution)/shard_map/all_to_all | solution.py:241
  18.3 0.3 pool.1
  18.6 5.7 %collective-permute-start.1 = (bf16[8,1664]{1,0:T(8,128)(2,1)S(1)}, bf16[8,1664]{1,0:T(8,128)(2,1)S(1)}, u32[]{:S(2)}, u32[]{:S(2)}) collective-permute-start(bf16[8,1664]{1,0:T(8,128)(2,1)S(1)} %pool.1), channel_id=1, source_target_pairs={{0,32},{32,0},{1,33},{33,1},{2,34},{34,2},{3,35},{35,3},{4,36},{36... | collective-permute-start | bytes 79880 | tf_op jit(solution)/shard_map/ppermute | solution.py:250
  24.3 5.2 %all-to-all-done = bf16[4,256,384]{2,1,0:T(8,128)(2,1)S(1)} async-done(((bf16[4,256,384]{2,1,0:T(8,128)(2,1)}), bf16[4,256,384]{2,1,0:T(8,128)(2,1)S(1)}, u32[]{:S(2)}, u32[]{:S(2)}) %all-to-all-start) | async-done | bytes 786464 | tf_op jit(solution)/shard_map/all_to_all | solution.py:241
  29.6 0.0 collective-permute-done.1
  29.6 0.8 %broadcast_in_dim.20 = bf16[2,4,64,384]{3,2,1,0:T(8,128)(2,1)} broadcast(bf16[4,64,384]{2,1,0:T(8,128)(2,1)S(1)} %bitcast.22), dimensions={1,2,3} | broadcast | bytes 589824 | tf_op jit(solution)/shard_map/broadcast_in_dim | solution.py:253
  30.4 4.9 %all-to-all-start.1 = ((bf16[8,64,384]{2,1,0:T(8,128)(2,1)}), bf16[8,64,384]{2,1,0:T(8,128)(2,1)S(1)}, u32[]{:S(2)}, u32[]{:S(2)}) async-start(bf16[8,64,384]{2,1,0:T(8,128)(2,1)} %bitcast.6), calls=%async_computation.1 | async-start | bytes 786432 | tf_op jit(solution)/shard_map/all_to_all | solution.py:256
  35.3 2.9 %collective-permute-start.2 = (bf16[16,1664]{1,0:T(8,128)(2,1)S(1)}, bf16[16,1664]{1,0:T(8,128)(2,1)S(1)}, u32[]{:S(2)}, u32[]{:S(2)}) collective-permute-start(bf16[16,1664]{1,0:T(8,128)(2,1)S(1)} %pad_maximum_fusion.1), channel_id=1, source_target_pairs={{0,16},{8,24},{16,0},{24,8},{1,17},{9,25},{17,1},{25,9},{2,18},{10... | collective-permute-start | bytes 159752 | tf_op jit(solution)/shard_map/ppermute | solution.py:260
  38.2 3.4 %collective-permute-done.2 = bf16[16,1664]{1,0:T(8,128)(2,1)S(1)} collective-permute-done((bf16[16,1664]{1,0:T(8,128)(2,1)S(1)}, bf16[16,1664]{1,0:T(8,128)(2,1)S(1)}, u32[]{:S(2)}, u32[]{:S(2)}) %collective-permute-start.2) | collective-permute-done | bytes 53280 | tf_op jit(solution)/shard_map/ppermute | solution.py:260
  41.7 2.2 %collective-permute-start.3 = (bf16[32,1664]{1,0:T(8,128)(2,1)S(1)}, bf16[32,1664]{1,0:T(8,128)(2,1)}, u32[]{:S(2)}, u32[]{:S(2)}) collective-permute-start(bf16[32,1664]{1,0:T(8,128)(2,1)S(1)} %pad_maximum_fusion), channel_id=1, source_target_pairs={{0,8},{8,0},{16,24},{24,16},{1,9},{9,1},{17,25},{25,17},{2,10},{10... | collective-permute-start | bytes 319496 | tf_op jit(solution)/shard_map/ppermute | solution.py:265
  43.9 3.8 %all-to-all-done.1 = bf16[8,64,384]{2,1,0:T(8,128)(2,1)S(1)} async-done(((bf16[8,64,384]{2,1,0:T(8,128)(2,1)}), bf16[8,64,384]{2,1,0:T(8,128)(2,1)S(1)}, u32[]{:S(2)}, u32[]{:S(2)}) %all-to-all-start.1) | async-done | bytes 393248 | tf_op jit(solution)/shard_map/all_to_all | solution.py:256
  47.7 0.9 %broadcast_in_dim.22 = bf16[4,256,384]{2,1,0:T(8,128)(2,1)} broadcast(bf16[256,384]{1,0:T(8,128)(2,1)S(1)} %dynamic-slice_bitcast_fusion), dimensions={1,2} | broadcast | bytes 983040 | tf_op jit(solution)/shard_map/broadcast_in_dim | solution.py:264
  48.6 3.5 %all-to-all-start.2 = ((bf16[4,256,384]{2,1,0:T(8,128)(2,1)}), bf16[4,256,384]{2,1,0:T(8,128)(2,1)S(1)}, u32[]{:S(2)}, u32[]{:S(2)}) async-start(bf16[4,256,384]{2,1,0:T(8,128)(2,1)} %broadcast_in_dim.22), calls=%async_computation.2 | async-start | bytes 1572864 | tf_op jit(solution)/shard_map/all_to_all | solution.py:269
  52.1 0.0 copy-start.6
  52.1 0.0 collective-permute-done.3
  52.1 0.9 %constant_dynamic-update-slice_fusion.pa_ref = bf16[64,1664]{1,0:T(8,128)(2,1)S(1)} fusion(bf16[64,1664]{1,0:T(8,128)(2,1)S(1)} %constant_dynamic-update-slice_fusion.1, bf16[32,1664]{1,0:T(8,128)(2,1)} %collective-permute-done.3), kind=kLoop, calls=%fused_computation.4 | loop fusion | bytes 212992 | tf_op jit(solution)/shard_map/concatenate | solution.py:270
  53.1 5.2 %collective-permute-start.4 = (bf16[64,1664]{1,0:T(8,128)(2,1)S(1)}, bf16[64,1664]{1,0:T(8,128)(2,1)S(1)}, u32[]{:S(2)}, u32[]{:S(2)}) collective-permute-start(bf16[64,1664]{1,0:T(8,128)(2,1)S(1)} %constant_dynamic-update-slice_fusion.pa_ref), channel_id=1, source_target_pairs={{0,4},{4,0},{1,5},{5,1},{2,6},{6,2},{3,7},{7,3},{8,12},{12,8},{9,1... | collective-permute-start | bytes 638984 | tf_op jit(solution)/shard_map/ppermute | solution.py:271
  58.2 2.5 %window.1 = (f32[768,512]{1,0:T(8,128)S(1)}, f32[16,512]{1,0:T(8,128)S(1)}) custom-call(bf16[512,768]{1,0:T(8,128)(2,1)S(1)} %copy-done, bf16[512,768]{1,0:T(8,128)(2,1)S(1)} %copy-done.3, bf16[512,768]{1,0:T(8,128)(2,1)S(1)} %copy-done.4), custom_call_target="tpu_custom_call" | custom-call | flops 805306368 | bytes 3932160 | tf_op jit(solution)/shard_map/window/pallas_call | solution.py:272
  60.8 0.0 collective-permute-done.4.pb_ref
  60.8 2.2 %pooled.1 = (f32[768,512]{1,0:T(8,128)S(1)}, f32[16,512]{1,0:T(8,128)S(1)}) custom-call(s32[1]{0:T(128)S(6)} %copy.13.tag_ref, f32[6]{0:T(128)S(1)} %copy-done.6, bf16[512,768]{1,0:T(8,128)(2,1)S(1)} %copy-done, bf16[64,1664]{1,0:T(8,128)(2,1)S(1)} %constant_dynamic-update-slice_fusion.pa_ref, bf16[64,1664]{1,0:T(8,128)(2,1)S(1)} %collective-permute-done.4.pb_ref, ...), custom_call_target="tpu_custom_call" | custom-call | flops 201326592 | bytes 4718592 | tf_op jit(solution)/shard_map/pooled/pallas_call | solution.py:285
  63.0 4.2 %collective-permute-start.5 = (bf16[16,2,32,384]{3,2,1,0:T(8,128)(2,1)S(1)}, bf16[16,2,32,384]{3,2,1,0:T(8,128)(2,1)S(1)}, u32[]{:S(2)}, u32[]{:S(2)}) collective-permute-start(bf16[16,2,32,384]{3,2,1,0:T(8,128)(2,1)S(1)} %bitcast.19), channel_id=1, source_target_pairs={{0,4},{4,0},{1,5},{5,1},{2,6},{6,2},{3,7},{7,3},{8,12},{12,8},{9,1... | collective-permute-start | bytes 2359304 | tf_op jit(solution)/shard_map/ppermute | solution.py:300
  67.2 1.6 %own.1.part_ref = bf16[512,384]{1,0:T(8,128)(2,1)S(1)} custom-call(s32[1]{0:T(128)} %bitcast.side_ref.core_ref, bf16[512,768]{1,0:T(8,128)(2,1)S(1)} %copy-done, bf16[16,2,32,384]{3,2,1,0:T(8,128)(2,1)S(1)} %bitcast.20, f32[768,512]{1,0:T(8,128)S(1)} %get-tuple-element.35.acc_ref, f32[16,512]{1,0:T(8,128)S(1)} %get-tuple-element.36.stat_ref), custom_call_target="tpu_custom_call" | custom-call | flops 402653184 | bytes 1966080 | tf_op jit(solution)/shard_map/own/pallas_call | solution.py:301
  68.9 0.2 collective-permute-done.5.kv_ref
  69.1 2.3 %got.1 = bf16[512,768]{1,0:T(8,128)(2,1)} custom-call(s32[1]{0:T(128)} %bitcast.side_ref.core_ref, bf16[512,768]{1,0:T(8,128)(2,1)S(1)} %copy-done, bf16[16,2,32,384]{3,2,1,0:T(8,128)(2,1)S(1)} %collective-permute-done.5.kv_ref, f32[768,512]{1,0:T(8,128)S(1)} %get-tuple-element.35.acc_ref, f32[16,512]{1,0:T(8,128)S(1)} %get-tuple-element.36.stat_ref, ...), custom_call_target="tpu_custom_call" | custom-call | tf_op jit(solution)/shard_map/got/pallas_call | solution.py:314
  (18 shorter events, 0.1 us)
Async XLA Ops:
  0.0 11.6 %copy-start.2 = (bf16[1,128,3072]{2,1,0:T(8,128)(2,1)S(1)}, bf16[1,128,3072]{2,1,0:T(8,128)(2,1)}, u32[]{:S(2)}) copy-start(bf16[1,128,3072]{2,1,0:T(8,128)(2,1)} %param.16) | copy-start | bytes 2359300
  0.0 11.6 %copy-start.1 = (bf16[1,128,3072]{2,1,0:T(8,128)(2,1)S(1)}, bf16[1,128,3072]{2,1,0:T(8,128)(2,1)}, u32[]{:S(2)}) copy-start(bf16[1,128,3072]{2,1,0:T(8,128)(2,1)} %param.15) | copy-start | bytes 2359300
  2.1 10.9 %collective-permute-start = (bf16[4,4,2,32,384]{4,3,2,1,0:T(8,128)(2,1)}, bf16[4,4,2,32,384]{4,3,2,1,0:T(8,128)(2,1)S(1)}, u32[]{:S(2)}, u32[]{:S(2)}) collective-permute-start(bf16[4,4,2,32,384]{4,3,2,1,0:T(8,128)(2,1)} %give.1), channel_id=1, source_target_pairs={{0,4},{4,0},{1,5},{5,1},{2,6},{6,2},{3,7},{7,3},{8,12},{12,8},{9,1... | collective-permute-start | bytes 2359304 | tf_op jit(solution)/shard_map/ppermute | solution.py:235
  11.7 6.6 %copy-start.3 = (bf16[512,768]{1,0:T(8,128)(2,1)S(1)}, bf16[512,768]{1,0:T(8,128)(2,1)}, u32[]{:S(2)}) copy-start(bf16[512,768]{1,0:T(8,128)(2,1)} %k_ref.1) | copy-start | bytes 2359300
  11.7 6.6 %copy-start.4 = (bf16[512,768]{1,0:T(8,128)(2,1)S(1)}, bf16[512,768]{1,0:T(8,128)(2,1)}, u32[]{:S(2)}) copy-start(bf16[512,768]{1,0:T(8,128)(2,1)} %v_ref.1) | copy-start | bytes 2359300
  11.7 6.6 %copy-start.5 = (s32[1,512]{1,0:T(1,128)S(1)}, s32[1,512]{1,0:T(1,128)}, u32[]{:S(2)}) copy-start(s32[1,512]{1,0:T(1,128)} %seg_ref.1) | copy-start | bytes 6148
  14.0 15.5 %all-to-all-start = ((bf16[4,256,384]{2,1,0:T(8,128)(2,1)}), bf16[4,256,384]{2,1,0:T(8,128)(2,1)S(1)}, u32[]{:S(2)}, u32[]{:S(2)}) async-start(bf16[4,256,384]{2,1,0:T(8,128)(2,1)} %bitcast.4), calls=%async_computation | async-start | bytes 1572864 | tf_op jit(solution)/shard_map/all_to_all | solution.py:241
  18.6 11.0 %collective-permute-start.1 = (bf16[8,1664]{1,0:T(8,128)(2,1)S(1)}, bf16[8,1664]{1,0:T(8,128)(2,1)S(1)}, u32[]{:S(2)}, u32[]{:S(2)}) collective-permute-start(bf16[8,1664]{1,0:T(8,128)(2,1)S(1)} %pool.1), channel_id=1, source_target_pairs={{0,32},{32,0},{1,33},{33,1},{2,34},{34,2},{3,35},{35,3},{4,36},{36... | collective-permute-start | bytes 79880 | tf_op jit(solution)/shard_map/ppermute | solution.py:250
  30.4 17.3 %all-to-all-start.1 = ((bf16[8,64,384]{2,1,0:T(8,128)(2,1)}), bf16[8,64,384]{2,1,0:T(8,128)(2,1)S(1)}, u32[]{:S(2)}, u32[]{:S(2)}) async-start(bf16[8,64,384]{2,1,0:T(8,128)(2,1)} %bitcast.6), calls=%async_computation.1 | async-start | bytes 786432 | tf_op jit(solution)/shard_map/all_to_all | solution.py:256
  35.3 6.4 %collective-permute-start.2 = (bf16[16,1664]{1,0:T(8,128)(2,1)S(1)}, bf16[16,1664]{1,0:T(8,128)(2,1)S(1)}, u32[]{:S(2)}, u32[]{:S(2)}) collective-permute-start(bf16[16,1664]{1,0:T(8,128)(2,1)S(1)} %pad_maximum_fusion.1), channel_id=1, source_target_pairs={{0,16},{8,24},{16,0},{24,8},{1,17},{9,25},{17,1},{25,9},{2,18},{10... | collective-permute-start | bytes 159752 | tf_op jit(solution)/shard_map/ppermute | solution.py:260
  41.7 10.5 %collective-permute-start.3 = (bf16[32,1664]{1,0:T(8,128)(2,1)S(1)}, bf16[32,1664]{1,0:T(8,128)(2,1)}, u32[]{:S(2)}, u32[]{:S(2)}) collective-permute-start(bf16[32,1664]{1,0:T(8,128)(2,1)S(1)} %pad_maximum_fusion), channel_id=1, source_target_pairs={{0,8},{8,0},{16,24},{24,16},{1,9},{9,1},{17,25},{25,17},{2,10},{10... | collective-permute-start | bytes 319496 | tf_op jit(solution)/shard_map/ppermute | solution.py:265
  47.6 10.6 %copy-start = (bf16[512,768]{1,0:T(8,128)(2,1)S(1)}, bf16[512,768]{1,0:T(8,128)(2,1)}, u32[]{:S(2)}) copy-start(bf16[512,768]{1,0:T(8,128)(2,1)} %q_ref.6) | copy-start | bytes 2359300
  48.6 14.4 %all-to-all-start.2 = ((bf16[4,256,384]{2,1,0:T(8,128)(2,1)}), bf16[4,256,384]{2,1,0:T(8,128)(2,1)S(1)}, u32[]{:S(2)}, u32[]{:S(2)}) async-start(bf16[4,256,384]{2,1,0:T(8,128)(2,1)} %broadcast_in_dim.22), calls=%async_computation.2 | async-start | bytes 1572864 | tf_op jit(solution)/shard_map/all_to_all | solution.py:269
  52.1 8.7 %copy-start.6 = (f32[6]{0:T(128)S(1)}, f32[6]{0:T(128)}, u32[]{:S(2)}) copy-start(f32[6]{0:T(128)} %slope_ref.1) | copy-start | bytes 76
  53.1 7.7 %collective-permute-start.4 = (bf16[64,1664]{1,0:T(8,128)(2,1)S(1)}, bf16[64,1664]{1,0:T(8,128)(2,1)S(1)}, u32[]{:S(2)}, u32[]{:S(2)}) collective-permute-start(bf16[64,1664]{1,0:T(8,128)(2,1)S(1)} %constant_dynamic-update-slice_fusion.pa_ref), channel_id=1, source_target_pairs={{0,4},{4,0},{1,5},{5,1},{2,6},{6,2},{3,7},{7,3},{8,12},{12,8},{9,1... | collective-permute-start | bytes 638984 | tf_op jit(solution)/shard_map/ppermute | solution.py:271
  63.0 6.1 %collective-permute-start.5 = (bf16[16,2,32,384]{3,2,1,0:T(8,128)(2,1)S(1)}, bf16[16,2,32,384]{3,2,1,0:T(8,128)(2,1)S(1)}, u32[]{:S(2)}, u32[]{:S(2)}) collective-permute-start(bf16[16,2,32,384]{3,2,1,0:T(8,128)(2,1)S(1)} %bitcast.19), channel_id=1, source_target_pairs={{0,4},{4,0},{1,5},{5,1},{2,6},{6,2},{3,7},{7,3},{8,12},{12,8},{9,1... | collective-permute-start | bytes 2359304 | tf_op jit(solution)/shard_map/ppermute | solution.py:300

commit v13 on v9

--- a/solution.py
+++ b/solution.py
@@ -122,15 +122,29 @@
         )
 
 
-def got_kernel(core_ref, q_ref, kv_ref, acc_ref, stat_ref, part_ref, out_ref):
+def got_kernel(core_ref, q_ref, kv_ref, acc_ref, stat_ref, part_ref, out_ref, buf, sems):
     half = part_ref.shape[1]
 
-    def write(rows, cols, lanes, block):
-        out_ref[rows, cols] = block
-
     def finish(side):
-        out_ref[:, side * half : (side + 1) * half] = part_ref[...]
+        done = [
+            pltpu.make_async_copy(
+                part_ref, out_ref.at[:, pl.ds(side * half, half)], sems.at[half // HD]
+            )
+        ]
+        done[0].start()
+
+        def write(rows, cols, lanes, block):
+            buf[rows, lanes] = block
+            if rows.start + rows.size == buf.shape[0]:
+                copy = pltpu.make_async_copy(
+                    buf.at[:, lanes], out_ref.at[:, cols], sems.at[lanes.start // HD]
+                )
+                copy.start()
+                done.append(copy)
+
         ref_heads(q_ref, kv_ref, acc_ref, stat_ref, 1 - side, write)
+        for copy in done:
+            copy.wait()
 
     for side in range(2):
         pl.when(core_ref[0] == side)(functools.partial(finish, side))
@@ -138,6 +152,7 @@
 
 SMEM = pl.BlockSpec(memory_space=pltpu.SMEM)
 VMEM = pl.BlockSpec(memory_space=pltpu.VMEM)
+ANY = pl.BlockSpec(memory_space=pl.ANY)
 
 
 def on_device(
@@ -257,7 +272,11 @@
         got_kernel,
         out_shape=jax.ShapeDtypeStruct((rows, width), jnp.bfloat16),
         in_specs=[SMEM] + [VMEM] * 5,
-        out_specs=VMEM,
+        out_specs=ANY,
+        scratch_shapes=[
+            pltpu.VMEM((rows, half), jnp.bfloat16),
+            pltpu.SemaphoreType.DMA((half // HD + 1,)),
+        ],
         compiler_params=near,
         name="got",
     )(side, queries, got, acc, stat, out)

time: 72.4 us -> 72.2 us (level)
  no operation moved by 1% of the time
where the time goes in v13:
time: 72.2 us; the launch traced here: 71.6 us
  starting transfers between devices  40.9 us (57%)
  waiting for transfers between devices  13.8 us (19%)
  Pallas kernels  9.22 us (13%)
  local copies, waits for them, and re-layouts  5.02 us (7%)
  between operations  1.64 us (2%)
  other arithmetic  1.03 us (1%)
    ppermute x1, starting transfers between devices, on_device(): got = lax.ppermute(given, 'c', SWAP)  8.91 us
    ppermute x1, starting transfers between devices, on_device(): other = lax.ppermute(pooled, 'zh', SWAP)  5.72 us
    all_to_all x1, waiting for transfers between devices, on_device(): spread = lax.all_to_all(mine.reshape(n_x, -1, half), 'x', 0, 0, tiled=True)  5.22 us
    ppermute x1, starting transfers between devices, on_device(): other = lax.ppermute(pooled, 'c', SWAP)  5.18 us
    all_to_all x1, starting transfers between devices, on_device(): lax.all_to_all(piece.reshape(n_zh * n_head, 2 * part, half), ('zh', 'head...  4.89 us
    all_to_all x1, waiting for transfers between devices, on_device(): lax.all_to_all(piece.reshape(n_zh * n_head, 2 * part, half), ('zh', 'head...  4.56 us
    ppermute x1, starting transfers between devices, on_device(): got = lax.ppermute(own, 'c', SWAP)  4.16 us
    all_to_all x1, starting transfers between devices, on_device(): spread = lax.all_to_all(mine.reshape(n_x, -1, half), 'x', 0, 0, tiled=True)  3.49 us
  transfers between devices with their start and end apart: 9, of which 5 were waited for; matrix products, arithmetic and copies ran while one was open for 3% of the time, Pallas kernels for 9%

profile of v13, /device:TPU:1, one launch (start us, length us, event | category | flops | bytes accessed | tf_op | source)
XLA Modules:
  0.0 71.6 jit_solution(1017898388611597807)
XLA Ops:
  0.0 1.1 %copy-done.1 = bf16[1,128,3072]{2,1,0:T(8,128)(2,1)S(1)} copy-done((bf16[1,128,3072]{2,1,0:T(8,128)(2,1)S(1)}, bf16[1,128,3072]{2,1,0:T(8,128)(2,1)}, u32[]{:S(2)}) %copy-start.1) | copy-done | bytes 786456
  1.1 1.1 %copy-done.3 = bf16[1,128,3072]{2,1,0:T(8,128)(2,1)S(1)} copy-done((bf16[1,128,3072]{2,1,0:T(8,128)(2,1)S(1)}, bf16[1,128,3072]{2,1,0:T(8,128)(2,1)}, u32[]{:S(2)}) %copy-start.3) | copy-done | bytes 786456
  2.3 0.1 split.2
  2.4 8.9 %collective-permute-start = (bf16[4,4,2,32,384]{4,3,2,1,0:T(8,128)(2,1)S(1)}, bf16[4,4,2,32,384]{4,3,2,1,0:T(8,128)(2,1)S(1)}, u32[]{:S(2)}, u32[]{:S(2)}) collective-permute-start(bf16[4,4,2,32,384]{4,3,2,1,0:T(8,128)(2,1)S(1)} %split.2), channel_id=1, source_target_pairs={{0,4},{4,0},{1,5},{5,1},{2,6},{6,2},{3,7},{7,3},{8,12},{12,8},{9,1... | collective-permute-start | bytes 2359304 | tf_op jit(solution)/shard_map/ppermute | solution.py:192
  12.0 0.1 split.3
  12.0 0.0 copy-start.5
  12.1 0.0 copy-start.6
  12.1 0.0 copy-start.8
  12.1 1.1 %collective-permute-done = bf16[4,4,2,32,384]{4,3,2,1,0:T(8,128)(2,1)S(1)} collective-permute-done((bf16[4,4,2,32,384]{4,3,2,1,0:T(8,128)(2,1)S(1)}, bf16[4,4,2,32,384]{4,3,2,1,0:T(8,128)(2,1)S(1)}, u32[]{:S(2)}, u32[]{:S(2)}) %collective-permute-start) | collective-permute-done | bytes 786464 | tf_op jit(solution)/shard_map/ppermute | solution.py:192
  13.2 1.0 %broadcast_select_fusion = bf16[4,4,2,32,384]{4,3,2,1,0:T(8,128)(2,1)} fusion(bf16[4,4,2,32,384]{4,3,2,1,0:T(8,128)(2,1)S(1)} %split.3, bf16[4,4,2,32,384]{4,3,2,1,0:T(8,128)(2,1)S(1)} %collective-permute-done, pred[]{:T(512)S(6)} %eq.6), kind=kLoop, calls=%fused_computation | loop fusion | flops 393216 | bytes 2359297 | tf_op jit(solution)/shard_map/jit(_where)/select_n | solution.py:195
  14.2 3.5 %all-to-all-start = ((bf16[4,256,384]{2,1,0:T(8,128)(2,1)}), bf16[4,256,384]{2,1,0:T(8,128)(2,1)S(1)}, u32[]{:S(2)}, u32[]{:S(2)}) async-start(bf16[4,256,384]{2,1,0:T(8,128)(2,1)} %bitcast.4), calls=%async_computation | async-start | bytes 1572864 | tf_op jit(solution)/shard_map/all_to_all | solution.py:198
  18.4 0.3 pool.1
  18.7 5.7 %collective-permute-start.1 = (bf16[8,1664]{1,0:T(8,128)(2,1)S(1)}, bf16[8,1664]{1,0:T(8,128)(2,1)S(1)}, u32[]{:S(2)}, u32[]{:S(2)}) collective-permute-start(bf16[8,1664]{1,0:T(8,128)(2,1)S(1)} %pool.1), channel_id=1, source_target_pairs={{0,32},{32,0},{1,33},{33,1},{2,34},{34,2},{3,35},{35,3},{4,36},{36... | collective-permute-start | bytes 79880 | tf_op jit(solution)/shard_map/ppermute | solution.py:207
  24.5 5.2 %all-to-all-done = bf16[4,256,384]{2,1,0:T(8,128)(2,1)S(1)} async-done(((bf16[4,256,384]{2,1,0:T(8,128)(2,1)}), bf16[4,256,384]{2,1,0:T(8,128)(2,1)S(1)}, u32[]{:S(2)}, u32[]{:S(2)}) %all-to-all-start) | async-done | bytes 786464 | tf_op jit(solution)/shard_map/all_to_all | solution.py:198
  29.7 0.8 %broadcast_in_dim.20 = bf16[2,4,64,384]{3,2,1,0:T(8,128)(2,1)} broadcast(bf16[4,64,384]{2,1,0:T(8,128)(2,1)S(1)} %bitcast.22), dimensions={1,2,3} | broadcast | bytes 589824 | tf_op jit(solution)/shard_map/broadcast_in_dim | solution.py:210
  30.5 4.9 %all-to-all-start.1 = ((bf16[8,64,384]{2,1,0:T(8,128)(2,1)}), bf16[8,64,384]{2,1,0:T(8,128)(2,1)S(1)}, u32[]{:S(2)}, u32[]{:S(2)}) async-start(bf16[8,64,384]{2,1,0:T(8,128)(2,1)} %bitcast.6), calls=%async_computation.1 | async-start | bytes 786432 | tf_op jit(solution)/shard_map/all_to_all | solution.py:213
  35.4 2.2 %collective-permute-start.2 = (bf16[16,1664]{1,0:T(8,128)(2,1)S(1)}, bf16[16,1664]{1,0:T(8,128)(2,1)S(1)}, u32[]{:S(2)}, u32[]{:S(2)}) collective-permute-start(bf16[16,1664]{1,0:T(8,128)(2,1)S(1)} %pad_maximum_fusion.1), channel_id=1, source_target_pairs={{0,8},{8,0},{16,24},{24,16},{1,9},{9,1},{17,25},{25,17},{2,10},{10... | collective-permute-start | bytes 159752 | tf_op jit(solution)/shard_map/ppermute | solution.py:217
  37.6 2.7 %collective-permute-done.2 = bf16[16,1664]{1,0:T(8,128)(2,1)S(1)} collective-permute-done((bf16[16,1664]{1,0:T(8,128)(2,1)S(1)}, bf16[16,1664]{1,0:T(8,128)(2,1)S(1)}, u32[]{:S(2)}, u32[]{:S(2)}) %collective-permute-start.2) | collective-permute-done | bytes 53280 | tf_op jit(solution)/shard_map/ppermute | solution.py:217
  40.3 2.9 %collective-permute-start.3 = (bf16[32,1664]{1,0:T(8,128)(2,1)S(1)}, bf16[32,1664]{1,0:T(8,128)(2,1)}, u32[]{:S(2)}, u32[]{:S(2)}) collective-permute-start(bf16[32,1664]{1,0:T(8,128)(2,1)S(1)} %pad_maximum_fusion), channel_id=1, source_target_pairs={{0,16},{8,24},{16,0},{24,8},{1,17},{9,25},{17,1},{25,9},{2,18},{10... | collective-permute-start | bytes 319496 | tf_op jit(solution)/shard_map/ppermute | solution.py:222
  43.2 4.6 %all-to-all-done.1 = bf16[8,64,384]{2,1,0:T(8,128)(2,1)S(1)} async-done(((bf16[8,64,384]{2,1,0:T(8,128)(2,1)}), bf16[8,64,384]{2,1,0:T(8,128)(2,1)S(1)}, u32[]{:S(2)}, u32[]{:S(2)}) %all-to-all-start.1) | async-done | bytes 393248 | tf_op jit(solution)/shard_map/all_to_all | solution.py:213
  47.8 0.9 %broadcast_in_dim.22 = bf16[4,256,384]{2,1,0:T(8,128)(2,1)} broadcast(bf16[256,384]{1,0:T(8,128)(2,1)S(1)} %dynamic-slice_bitcast_fusion), dimensions={1,2} | broadcast | bytes 983040 | tf_op jit(solution)/shard_map/broadcast_in_dim | solution.py:221
  48.7 3.5 %all-to-all-start.2 = ((bf16[4,256,384]{2,1,0:T(8,128)(2,1)}), bf16[4,256,384]{2,1,0:T(8,128)(2,1)S(1)}, u32[]{:S(2)}, u32[]{:S(2)}) async-start(bf16[4,256,384]{2,1,0:T(8,128)(2,1)} %broadcast_in_dim.22), calls=%async_computation.2 | async-start | bytes 1572864 | tf_op jit(solution)/shard_map/all_to_all | solution.py:226
  52.3 0.0 copy-start.9
  52.3 0.9 %constant_dynamic-update-slice_fusion.pa_ref = bf16[64,1664]{1,0:T(8,128)(2,1)S(1)} fusion(bf16[64,1664]{1,0:T(8,128)(2,1)S(1)} %constant_dynamic-update-slice_fusion.1, bf16[32,1664]{1,0:T(8,128)(2,1)} %collective-permute-done.3), kind=kLoop, calls=%fused_computation.4 | loop fusion | bytes 212992 | tf_op jit(solution)/shard_map/concatenate | solution.py:227
  53.2 5.2 %collective-permute-start.4 = (bf16[64,1664]{1,0:T(8,128)(2,1)S(1)}, bf16[64,1664]{1,0:T(8,128)(2,1)S(1)}, u32[]{:S(2)}, u32[]{:S(2)}) collective-permute-start(bf16[64,1664]{1,0:T(8,128)(2,1)S(1)} %constant_dynamic-update-slice_fusion.pa_ref), channel_id=1, source_target_pairs={{0,4},{4,0},{1,5},{5,1},{2,6},{6,2},{3,7},{7,3},{8,12},{12,8},{9,1... | collective-permute-start | bytes 638984 | tf_op jit(solution)/shard_map/ppermute | solution.py:228
  58.4 2.5 %window.1 = (f32[768,512]{1,0:T(8,128)S(1)}, f32[16,512]{1,0:T(8,128)S(1)}) custom-call(bf16[512,768]{1,0:T(8,128)(2,1)S(1)} %copy-done, bf16[512,768]{1,0:T(8,128)(2,1)S(1)} %copy-done.5, bf16[512,768]{1,0:T(8,128)(2,1)S(1)} %copy-done.7), custom_call_target="tpu_custom_call" | custom-call | flops 805306368 | bytes 3932160 | tf_op jit(solution)/shard_map/window/pallas_call | solution.py:229
  60.9 0.0 collective-permute-done.4.pb_ref
  60.9 2.2 %pooled.1 = (f32[768,512]{1,0:T(8,128)S(1)}, f32[16,512]{1,0:T(8,128)S(1)}) custom-call(s32[1]{0:T(128)S(6)} %copy.13.tag_ref, f32[6]{0:T(128)S(1)} %copy-done.9, bf16[512,768]{1,0:T(8,128)(2,1)S(1)} %copy-done, bf16[64,1664]{1,0:T(8,128)(2,1)S(1)} %constant_dynamic-update-slice_fusion.pa_ref, bf16[64,1664]{1,0:T(8,128)(2,1)S(1)} %collective-permute-done.4.pb_ref, ...), custom_call_target="tpu_custom_call" | custom-call | flops 201326592 | bytes 4718592 | tf_op jit(solution)/shard_map/pooled/pallas_call | solution.py:242
  63.2 4.2 %collective-permute-start.5 = (bf16[16,2,32,384]{3,2,1,0:T(8,128)(2,1)S(1)}, bf16[16,2,32,384]{3,2,1,0:T(8,128)(2,1)S(1)}, u32[]{:S(2)}, u32[]{:S(2)}) collective-permute-start(bf16[16,2,32,384]{3,2,1,0:T(8,128)(2,1)S(1)} %bitcast.19), channel_id=1, source_target_pairs={{0,4},{4,0},{1,5},{5,1},{2,6},{6,2},{3,7},{7,3},{8,12},{12,8},{9,1... | collective-permute-start | bytes 2359304 | tf_op jit(solution)/shard_map/ppermute | solution.py:257
  67.4 1.6 %own.1.part_ref = bf16[512,384]{1,0:T(8,128)(2,1)S(1)} custom-call(s32[1]{0:T(128)} %bitcast.side_ref.core_ref, bf16[512,768]{1,0:T(8,128)(2,1)S(1)} %copy-done, bf16[16,2,32,384]{3,2,1,0:T(8,128)(2,1)S(1)} %bitcast.20, f32[768,512]{1,0:T(8,128)S(1)} %get-tuple-element.35.acc_ref, f32[16,512]{1,0:T(8,128)S(1)} %get-tuple-element.36.stat_ref), custom_call_target="tpu_custom_call" | custom-call | flops 402653184 | bytes 1966080 | tf_op jit(solution)/shard_map/own/pallas_call | solution.py:258
  69.0 0.2 collective-permute-done.5.kv_ref
  69.2 2.4 %got.1 = bf16[512,768]{1,0:T(8,128)(2,1)} custom-call(s32[1]{0:T(128)} %bitcast.side_ref.core_ref, bf16[512,768]{1,0:T(8,128)(2,1)S(1)} %copy-done, bf16[16,2,32,384]{3,2,1,0:T(8,128)(2,1)S(1)} %collective-permute-done.5.kv_ref, f32[768,512]{1,0:T(8,128)S(1)} %get-tuple-element.35.acc_ref, f32[16,512]{1,0:T(8,128)S(1)} %get-tuple-element.36.stat_ref, ...), custom_call_target="tpu_custom_call" | custom-call | tf_op jit(solution)/shard_map/got/pallas_call | solution.py:271
  (24 shorter events, 0.1 us)
Async XLA Ops:
  0.0 1.1 %copy-start.1 = (bf16[1,128,3072]{2,1,0:T(8,128)(2,1)S(1)}, bf16[1,128,3072]{2,1,0:T(8,128)(2,1)}, u32[]{:S(2)}) copy-start(bf16[1,128,3072]{2,1,0:T(8,128)(2,1)} %param.15) | copy-start | bytes 2359300
  1.1 1.1 %copy-start.3 = (bf16[1,128,3072]{2,1,0:T(8,128)(2,1)S(1)}, bf16[1,128,3072]{2,1,0:T(8,128)(2,1)}, u32[]{:S(2)}) copy-start(bf16[1,128,3072]{2,1,0:T(8,128)(2,1)} %param.16) | copy-start | bytes 2359300
  2.3 9.7 %copy-start.2 = (bf16[1,128,3072]{2,1,0:T(8,128)(2,1)S(1)}, bf16[1,128,3072]{2,1,0:T(8,128)(2,1)}, u32[]{:S(2)}) copy-start(bf16[1,128,3072]{2,1,0:T(8,128)(2,1)} %param.15) | copy-start | bytes 2359300
  2.3 9.7 %copy-start.4 = (bf16[1,128,3072]{2,1,0:T(8,128)(2,1)S(1)}, bf16[1,128,3072]{2,1,0:T(8,128)(2,1)}, u32[]{:S(2)}) copy-start(bf16[1,128,3072]{2,1,0:T(8,128)(2,1)} %param.16) | copy-start | bytes 2359300
  2.4 10.8 %collective-permute-start = (bf16[4,4,2,32,384]{4,3,2,1,0:T(8,128)(2,1)S(1)}, bf16[4,4,2,32,384]{4,3,2,1,0:T(8,128)(2,1)S(1)}, u32[]{:S(2)}, u32[]{:S(2)}) collective-permute-start(bf16[4,4,2,32,384]{4,3,2,1,0:T(8,128)(2,1)S(1)} %split.2), channel_id=1, source_target_pairs={{0,4},{4,0},{1,5},{5,1},{2,6},{6,2},{3,7},{7,3},{8,12},{12,8},{9,1... | collective-permute-start | bytes 2359304 | tf_op jit(solution)/shard_map/ppermute | solution.py:192
  12.0 6.3 %copy-start.5 = (bf16[512,768]{1,0:T(8,128)(2,1)S(1)}, bf16[512,768]{1,0:T(8,128)(2,1)}, u32[]{:S(2)}) copy-start(bf16[512,768]{1,0:T(8,128)(2,1)} %k_ref.1) | copy-start | bytes 2359300
  12.1 6.3 %copy-start.6 = (bf16[512,768]{1,0:T(8,128)(2,1)S(1)}, bf16[512,768]{1,0:T(8,128)(2,1)}, u32[]{:S(2)}) copy-start(bf16[512,768]{1,0:T(8,128)(2,1)} %v_ref.1) | copy-start | bytes 2359300
  12.1 6.3 %copy-start.8 = (s32[1,512]{1,0:T(1,128)S(1)}, s32[1,512]{1,0:T(1,128)}, u32[]{:S(2)}) copy-start(s32[1,512]{1,0:T(1,128)} %seg_ref.1) | copy-start | bytes 6148
  14.2 15.5 %all-to-all-start = ((bf16[4,256,384]{2,1,0:T(8,128)(2,1)}), bf16[4,256,384]{2,1,0:T(8,128)(2,1)S(1)}, u32[]{:S(2)}, u32[]{:S(2)}) async-start(bf16[4,256,384]{2,1,0:T(8,128)(2,1)} %bitcast.4), calls=%async_computation | async-start | bytes 1572864 | tf_op jit(solution)/shard_map/all_to_all | solution.py:198
  18.7 11.0 %collective-permute-start.1 = (bf16[8,1664]{1,0:T(8,128)(2,1)S(1)}, bf16[8,1664]{1,0:T(8,128)(2,1)S(1)}, u32[]{:S(2)}, u32[]{:S(2)}) collective-permute-start(bf16[8,1664]{1,0:T(8,128)(2,1)S(1)} %pool.1), channel_id=1, source_target_pairs={{0,32},{32,0},{1,33},{33,1},{2,34},{34,2},{3,35},{35,3},{4,36},{36... | collective-permute-start | bytes 79880 | tf_op jit(solution)/shard_map/ppermute | solution.py:207
  30.5 17.3 %all-to-all-start.1 = ((bf16[8,64,384]{2,1,0:T(8,128)(2,1)}), bf16[8,64,384]{2,1,0:T(8,128)(2,1)S(1)}, u32[]{:S(2)}, u32[]{:S(2)}) async-start(bf16[8,64,384]{2,1,0:T(8,128)(2,1)} %bitcast.6), calls=%async_computation.1 | async-start | bytes 786432 | tf_op jit(solution)/shard_map/all_to_all | solution.py:213
  35.4 4.9 %collective-permute-start.2 = (bf16[16,1664]{1,0:T(8,128)(2,1)S(1)}, bf16[16,1664]{1,0:T(8,128)(2,1)S(1)}, u32[]{:S(2)}, u32[]{:S(2)}) collective-permute-start(bf16[16,1664]{1,0:T(8,128)(2,1)S(1)} %pad_maximum_fusion.1), channel_id=1, source_target_pairs={{0,8},{8,0},{16,24},{24,16},{1,9},{9,1},{17,25},{25,17},{2,10},{10... | collective-permute-start | bytes 159752 | tf_op jit(solution)/shard_map/ppermute | solution.py:217
  40.3 12.0 %collective-permute-start.3 = (bf16[32,1664]{1,0:T(8,128)(2,1)S(1)}, bf16[32,1664]{1,0:T(8,128)(2,1)}, u32[]{:S(2)}, u32[]{:S(2)}) collective-permute-start(bf16[32,1664]{1,0:T(8,128)(2,1)S(1)} %pad_maximum_fusion), channel_id=1, source_target_pairs={{0,16},{8,24},{16,0},{24,8},{1,17},{9,25},{17,1},{25,9},{2,18},{10... | collective-permute-start | bytes 319496 | tf_op jit(solution)/shard_map/ppermute | solution.py:222
  47.8 10.6 %copy-start = (bf16[512,768]{1,0:T(8,128)(2,1)S(1)}, bf16[512,768]{1,0:T(8,128)(2,1)}, u32[]{:S(2)}) copy-start(bf16[512,768]{1,0:T(8,128)(2,1)} %q_ref.6) | copy-start | bytes 2359300
  47.8 10.6 %copy-start.7 = (bf16[512,768]{1,0:T(8,128)(2,1)S(1)}, bf16[512,768]{1,0:T(8,128)(2,1)}, u32[]{:S(2)}) copy-start(bf16[512,768]{1,0:T(8,128)(2,1)} %v_ref.1) | copy-start | bytes 2359300
  48.7 14.4 %all-to-all-start.2 = ((bf16[4,256,384]{2,1,0:T(8,128)(2,1)}), bf16[4,256,384]{2,1,0:T(8,128)(2,1)S(1)}, u32[]{:S(2)}, u32[]{:S(2)}) async-start(bf16[4,256,384]{2,1,0:T(8,128)(2,1)} %broadcast_in_dim.22), calls=%async_computation.2 | async-start | bytes 1572864 | tf_op jit(solution)/shard_map/all_to_all | solution.py:226
  52.3 8.7 %copy-start.9 = (f32[6]{0:T(128)S(1)}, f32[6]{0:T(128)}, u32[]{:S(2)}) copy-start(f32[6]{0:T(128)} %slope_ref.1) | copy-start | bytes 76
  53.2 7.7 %collective-permute-start.4 = (bf16[64,1664]{1,0:T(8,128)(2,1)S(1)}, bf16[64,1664]{1,0:T(8,128)(2,1)S(1)}, u32[]{:S(2)}, u32[]{:S(2)}) collective-permute-start(bf16[64,1664]{1,0:T(8,128)(2,1)S(1)} %constant_dynamic-update-slice_fusion.pa_ref), channel_id=1, source_target_pairs={{0,4},{4,0},{1,5},{5,1},{2,6},{6,2},{3,7},{7,3},{8,12},{12,8},{9,1... | collective-permute-start | bytes 638984 | tf_op jit(solution)/shard_map/ppermute | solution.py:228
  63.2 6.1 %collective-permute-start.5 = (bf16[16,2,32,384]{3,2,1,0:T(8,128)(2,1)S(1)}, bf16[16,2,32,384]{3,2,1,0:T(8,128)(2,1)S(1)}, u32[]{:S(2)}, u32[]{:S(2)}) collective-permute-start(bf16[16,2,32,384]{3,2,1,0:T(8,128)(2,1)S(1)} %bitcast.19), channel_id=1, source_target_pairs={{0,4},{4,0},{1,5},{5,1},{2,6},{6,2},{3,7},{7,3},{8,12},{12,8},{9,1... | collective-permute-start | bytes 2359304 | tf_op jit(solution)/shard_map/ppermute | solution.py:257
